TPU v7x, 128 devices: a whole 4x4x4 slice. The times are simulated.
128 devices in a mesh: front: 1, row: 64 (over z, y, x), col: 2 (over core).
Axes of the slice: x: 4, y: 4, z: 4, core: 2. Of those that a mesh axis runs over, the one named last changes fastest.
Arguments:
- contributions: float32 [64, 128, 4096], P(('front', 'row'), None, 'col'), may hold values from -0.088388348 to 0.088388348
- valid_rows: int32 [64], P(('front', 'row')), may hold values from 1 to 128, 5120 in all
Outputs:
- r_rows: float32 [512, 4096], P('front', 'col')
All inputs are finite; a program needn't handle non-finite values. No bound on the sum of `valid_rows` on one device may be relied on, other than what follows from the above.
Results may differ from a plain program's by a relative error of at most 0.0003.
Values sent between devices are 32-bit elements; how exact they have to be, the bound alone decides.
No kernel may reach another device: no remote copies, remote signals or barrier semaphores. Data moves between devices by JAX's collectives and lax.ppermute only.
A program may use at most 64 MiB of HBM per device.

v0:
```python
import jax
import jax.numpy as jnp
from jax import lax
from jax.experimental import pallas as pl
from jax.experimental.pallas import tpu as pltpu
from jax.sharding import PartitionSpec as P

LEAD = 512
HI = lax.Precision.HIGHEST

S8=(8,128)
def lb(x,c): return jnp.broadcast_to(x[:,c:c+1],S8)
def sb(x,j): return jnp.broadcast_to(x[j:j+1,:],S8)

def chol_inv_128(V, sub, lane):
    V=list(V)
    E=[jnp.where(lane==sub+8*k,1.0,0.0) for k in range(16)]
    out=[]
    for k in range(16):
        X=V[k]
        LB=[lb(X,8*k+j) for j in range(8)]
        S=[[sb(LB[j],i) if i>=j else None for j in range(8)] for i in range(8)]
        R=[sb(X,j) for j in range(8)]
        F=[sb(E[k],j) for j in range(8)]
        l=[[None]*8 for _ in range(8)]
        inv=[None]*8
        for j in range(8):
            inv[j]=1.0/S[j][j]
            for i in range(j+1,8):
                l[i][j]=S[i][j]*inv[j]
                for m in range(j+1,i+1):
                    S[i][m]=S[i][m]-l[i][j]*S[m][j]
            for i in range(j+1,8):
                R[i]=R[i]-l[i][j]*R[j]
                F[i]=F[i]-l[i][j]*F[j]
        o=F[0]*lax.rsqrt(S[0][0])
        for j in range(1,8):
            o=jnp.where(sub==j,F[j]*lax.rsqrt(S[j][j]),o)
        out.append(o)
        if k<15:
            W=[R[j]*inv[j] for j in range(8)]
            H=[F[j]*inv[j] for j in range(8)]
            for i in range(7,0,-1):
                for j in range(i):
                    W[j]=W[j]-l[i][j]*W[i]
                    H[j]=H[j]-l[i][j]*H[i]
            for m in range(k+1,16):
                Y=V[m]; v=Y; e=E[m]
                for j in range(7,-1,-1):
                    c=lb(Y,8*k+j)
                    v=v-c*W[j]
                    e=e-c*H[j]
                V[m]=v; E[m]=e
    return out

def kernel(g_ref, o_ref, a, u, stack):
    a[...]=g_ref[...]
    o_ref[...]=jnp.zeros_like(o_ref)
    sub=lax.broadcasted_iota(jnp.int32,S8,0); lane=lax.broadcasted_iota(jnp.int32,S8,1)
    d=stack
    d[...]=g_ref[0:128,0:128]
    T=(((0,),(0,)),((),()))
    @pl.loop(0,4)
    def _(p):
        o=chol_inv_128([d[8*k:8*k+8,:] for k in range(16)],sub,lane)
        for k in range(16): d[8*k:8*k+8,:]=o[k]
        for q in range(4):
            @pl.when(p==q)
            def _():
                lo,hi=128*q,128*(q+1)
                linv=d[...]
                if q<3:
                    up=jnp.dot(linv,a[lo:hi,hi:],precision=HI,preferred_element_type=jnp.float32)
                    d[...]=a[hi:hi+128,hi:hi+128]-lax.dot_general(up[:,:128],up[:,:128],T,precision=HI,preferred_element_type=jnp.float32)
                    if q<2:
                        a[hi:,hi:]=a[hi:,hi:]-lax.dot_general(up,up,T,precision=HI,preferred_element_type=jnp.float32)
                o_ref[lo:hi,lo:hi]=linv
                if q>0:
                    o_ref[lo:hi,:lo]=jnp.dot(linv,o_ref[lo:hi,:lo],precision=HI,preferred_element_type=jnp.float32)
                if q<3:
                    o_ref[hi:,:hi]=o_ref[hi:,:hi]-lax.dot_general(up,o_ref[lo:hi,:hi],T,precision=HI,preferred_element_type=jnp.float32)

def inverse_factor(g):
    n=g.shape[0]
    return pl.pallas_call(kernel,out_shape=jax.ShapeDtypeStruct((n,n),jnp.float32),
        in_specs=[pl.BlockSpec(memory_space=pltpu.VMEM)],out_specs=pl.BlockSpec(memory_space=pltpu.VMEM),
        scratch_shapes=[pltpu.VMEM((n,n),jnp.float32),pltpu.VMEM((8,128),jnp.float32),pltpu.VMEM((128,128),jnp.float32)],
        compiler_params=pltpu.CompilerParams(vmem_limit_bytes=32*2**20),
        cost_estimate=pl.CostEstimate(flops=300_000_000*6,bytes_accessed=2**21,transcendentals=0))(g)


def body(contributions, valid_rows):
    blocks, height, width = contributions.shape
    live = jnp.arange(height, dtype=jnp.int32)[None, :] < valid_rows[:, None]
    frontal = jnp.where(live[:, :, None], contributions, 0.0).reshape(blocks * height, width)
    own = frontal[:, :LEAD]
    core = lax.axis_index("col")
    other = lax.ppermute(own, "col", [(0, 1), (1, 0)])
    lead = jnp.where(core == 0, own, other)
    gram = jnp.einsum("rp,rc->pc", lead, frontal, precision=HI)
    pieces = lax.all_to_all(gram.reshape(64, LEAD // 64, width), "row", 0, 0)
    mine = jnp.sum(pieces, axis=0)
    mine11 = mine[:, :LEAD]
    other11 = lax.ppermute(mine11, "col", [(0, 1), (1, 0)])
    mine11 = jnp.where(core == 0, mine11, other11)
    g11 = lax.all_to_all(jnp.broadcast_to(mine11[None], (64, LEAD // 64, LEAD)), "row", 0, 0)
    g11 = g11.reshape(LEAD, LEAD)
    mine, _ = lax.optimization_barrier((mine, g11[:8, :128]))
    gram_all = lax.all_gather(mine, "row", axis=0, tiled=True)
    inverse = inverse_factor(g11)
    projected = jnp.dot(inverse, gram_all, precision=HI)
    column_ids = core * width + jnp.arange(width, dtype=jnp.int32)
    kept = column_ids[None, :] >= jnp.arange(LEAD, dtype=jnp.int32)[:, None]
    return jnp.where(kept, projected, 0.0)


def solution(mesh):
    return jax.shard_map(
        body,
        mesh=mesh,
        in_specs=(P(("front", "row"), None, "col"), P(("front", "row"))),
        out_specs=P("front", "col"),
        check_vma=False,
    )
```

profile of v0, /device:TPU:0, one launch (start us, length us, event | category | flops | bytes accessed | tf_op | source)
XLA Modules:
  0.0 170.3 jit_solution(2596199851260000217)
XLA Ops:
  6.5 0.0 all-gather.2.cloned.1.call-start
  7.2 1.6 copy.4
  8.8 0.1 select_bitcast_fusion
  8.9 0.1 collective-permute-start
  9.0 1.5 collective-permute-done
  10.5 3.5 %fusion.1 = f32[64,8,2048]{2,1,0:T(8,128)S(1)} fusion(f32[1,128,2048]{1,2,0:T(8,128)S(1)} %copy.4, pred[128]{0:T(512)(128)(4,1)S(1)} %iota_compare_fusion.1, f32[128,512]{0,1:T(8,128)S(1)} %collective-permute-done, pred[]{:T(512)S(6)} %eq.4, f32[128,2048]{0,1:T(8,128)S(1)} %select_bitcast_fusion), kind=kOutput, calls=%fused_computation.2 | convolution fusion | flops 1610940416 | bytes 5767681 | tf_op jit(solution)/shard_map/rp,rc->pc/dot_general | solution.py:100
  14.0 64.3 %all_to_all.10 = f32[64,8,2048]{2,1,0:T(8,128)} all-to-all(f32[64,8,2048]{2,1,0:T(8,128)S(1)} %fusion.1), channel_id=1, replica_groups=mesh['front'=1,'row'=64,'col'=2] {'row'}, dimensions={0} | all-to-all | bytes 8388608 | tf_op jit(solution)/shard_map/all_to_all | solution.py:101
  78.3 3.0 %reduce_sum.9 = f32[8,2048]{1,0:T(8,128)} reduce(f32[64,8,2048]{2,1,0:T(8,128)} %all_to_all.10, f32[]{:T(128)} %constant.3.clone.1), dimensions={0}, to_apply=%region_0.1 | reduce | flops 1032192 | bytes 4259844 | tf_op jit(solution)/shard_map/reduce_sum | solution.py:102
  81.3 0.0 all-gather.2.cloned.1.call-update
  81.3 0.7 slice.10
  82.1 0.0 collective-permute-start.1
  82.1 1.2 collective-permute-done.1
  83.2 0.7 broadcast_select_fusion
  84.0 1.1 broadcast_in_dim.29
  85.1 5.9 %all-to-all-start.1 = ((f32[64,8,512]{2,1,0:T(8,128)}), f32[64,8,512]{2,1,0:T(8,128)S(1)}, u32[]{:S(2)}, u32[]{:S(2)}) async-start(f32[64,8,512]{2,1,0:T(8,128)} %broadcast_in_dim.29), calls=%async_computation.1 | async-start | bytes 2097152 | tf_op jit(solution)/shard_map/all_to_all | solution.py:106
  91.0 19.5 %all-to-all-done.1 = f32[64,8,512]{2,1,0:T(8,128)S(1)} async-done(((f32[64,8,512]{2,1,0:T(8,128)}), f32[64,8,512]{2,1,0:T(8,128)S(1)}, u32[]{:S(2)}, u32[]{:S(2)}) %all-to-all-start.1) | async-done | bytes 1048608 | tf_op jit(solution)/shard_map/all_to_all | solution.py:106
  110.5 20.7 %shard_map.28 = f32[512,512]{1,0:T(8,128)S(1)} custom-call(f32[512,512]{1,0:T(8,128)S(1)} %bitcast.16), custom_call_target="tpu_custom_call" | custom-call | flops 1800000000 | bytes 2097152 | tf_op jit(solution)/shard_map/pallas_call | solution.py:85
  131.2 22.3 %all-gather.2.cloned.1.call-done = f32[512,2048]{1,0:T(8,128)} async-done(((f32[8,2048]{1,0:T(8,128)}), f32[512,2048]{1,0:T(8,128)}) %all-gather.2.cloned.1.call-update) | async-done | bytes 4194320 | tf_op jit(solution)/shard_map/all_gather | solution.py:109
  153.4 10.1 %fusion = f32[512,2048]{1,0:T(8,128)} fusion(f32[512,512]{1,0:T(8,128)S(1)} %shard_map.28, f32[512,2048]{1,0:T(8,128)} %all-gather.2.cloned.1.call-done, s32[2048]{0:T(1024)S(1)} %iota_add_fusion), kind=kOutput, calls=%fused_computation.1 | convolution fusion | flops 6444548096 | bytes 9445376 | tf_op jit(solution)/shard_map/dot_general | solution.py:111
  (3 shorter events, 0.0 us)
Async XLA Ops:
  6.5 146.9 %all-gather.2.cloned.1.call-start = ((), (), s32[]{:S(2)}) async-start(), calls=%async_computation.2 | async-start | bytes 4259840 | tf_op jit(solution)/shard_map/all_gather | solution.py:109
  8.9 1.6 collective-permute-start
  82.1 1.2 collective-permute-start.1
  85.1 25.4 %all-to-all-start.1 = ((f32[64,8,512]{2,1,0:T(8,128)}), f32[64,8,512]{2,1,0:T(8,128)S(1)}, u32[]{:S(2)}, u32[]{:S(2)}) async-start(f32[64,8,512]{2,1,0:T(8,128)} %broadcast_in_dim.29), calls=%async_computation.1 | async-start | bytes 2097152 | tf_op jit(solution)/shard_map/all_to_all | solution.py:106
Sparse Core Ops, SparseCore 0:
  81.5 71.9 all-gather.1
where the time goes:
time: 171 us; the launch traced here: 170 us
  blocking collectives  64.3 us (38%)
  waiting for transfers between devices  44.5 us (26%)
  Pallas kernels  20.7 us (12%)
  between operations  14.1 us (8%)
  matrix products  13.6 us (8%)
  starting transfers between devices  5.97 us (3%)
  other arithmetic  3.83 us (2%)
  local copies, waits for them, and re-layouts  3.39 us (2%)
    all_to_all x1, blocking collectives, body(): pieces = lax.all_to_all(gram.reshape(64, LEAD // 64, width), 'row', 0, 0)  64.3 us
    all_gather x1, waiting for transfers between devices, body(): gram_all = lax.all_gather(mine, 'row', axis=0, tiled=True)  22.3 us
    pallas_call x1, Pallas kernels, inverse_factor(): pl.pallas_call(kernel, out_shape=jax.ShapeDtypeStruct((n, n), jnp.float32...  20.7 us
    all_to_all x1, waiting for transfers between devices, body(): lax.all_to_all(jnp.broadcast_to(mine11[None], (64, LEAD // 64, LEAD)), 'r...  19.5 us
    dot_general x1, matrix products, body(): projected = jnp.dot(inverse, gram_all, precision=HI)  10.1 us
    all_to_all x1, starting transfers between devices, body(): lax.all_to_all(jnp.broadcast_to(mine11[None], (64, LEAD // 64, LEAD)), 'r...  5.88 us
    dot_general x1, matrix products, body(): gram = jnp.einsum('rp,rc->pc', lead, frontal, precision=HI)  3.55 us
  transfers between devices with their start and end apart: 4, of which 4 were waited for; matrix products, arithmetic and copies ran while one was open for 1% of the time, Pallas kernels for 12%

commit v1 on v0

--- a/solution.py
+++ b/solution.py
@@ -7,6 +7,7 @@
 
 LEAD = 512
 HI = lax.Precision.HIGHEST
+
 
 S8=(8,128)
 def lb(x,c): return jnp.broadcast_to(x[:,c:c+1],S8)
@@ -89,29 +90,124 @@
         cost_estimate=pl.CostEstimate(flops=300_000_000*6,bytes_accessed=2**21,transcendentals=0))(g)
 
 
+def flip(link):
+    axis, kind = link
+    pairs = []
+    for chip in range(64):
+        at = [chip % 4, chip // 4 % 4, chip // 16]
+        for core in range(2):
+            to = list(at)
+            to[axis] ^= (1, 3)[kind ^ core]
+            pairs.append((chip * 2 + core, (to[0] + 4 * to[1] + 16 * to[2]) * 2 + core))
+    return pairs
+
+
+XP, XM, YP, YM, ZP, ZM = [(axis, kind) for axis in range(3) for kind in range(2)]
+
+
 def body(contributions, valid_rows):
     blocks, height, width = contributions.shape
+    half = width // 2
+    core = lax.axis_index("col")
+    row = lax.axis_index("row")
+    place = (row % 4, row // 4 % 4, row // 16)
+
+    def bit(link):
+        axis, kind = link
+        high, low = place[axis] // 2, place[axis] % 2
+        return jnp.where((core ^ kind) == 1, high, high ^ low) == 1
+
+    def swap(x, link):
+        return lax.ppermute(x, ("row", "col"), flip(link))
+
+    def across(x):
+        return lax.ppermute(x, "col", [(0, 1), (1, 0)])
+
+    def halves(x, link):
+        low, high = jnp.split(x, 2, axis=0)
+        mine = bit(link)
+        return jnp.where(mine, high, low), jnp.where(mine, low, high)
+
+    def joined(own, got, link, axis):
+        mine = bit(link)
+        return jnp.concatenate([jnp.where(mine, got, own), jnp.where(mine, own, got)], axis=axis)
+
+    def side(x, n):
+        return jnp.concatenate(jnp.split(x, n, axis=0), axis=1)
+
+    def stacked(x, n):
+        return jnp.concatenate(jnp.split(x, n, axis=1), axis=0)
+
     live = jnp.arange(height, dtype=jnp.int32)[None, :] < valid_rows[:, None]
     frontal = jnp.where(live[:, :, None], contributions, 0.0).reshape(blocks * height, width)
     own = frontal[:, :LEAD]
-    core = lax.axis_index("col")
-    other = lax.ppermute(own, "col", [(0, 1), (1, 0)])
+    other = across(own)
     lead = jnp.where(core == 0, own, other)
-    gram = jnp.einsum("rp,rc->pc", lead, frontal, precision=HI)
-    pieces = lax.all_to_all(gram.reshape(64, LEAD // 64, width), "row", 0, 0)
-    mine = jnp.sum(pieces, axis=0)
-    mine11 = mine[:, :LEAD]
-    other11 = lax.ppermute(mine11, "col", [(0, 1), (1, 0)])
-    mine11 = jnp.where(core == 0, mine11, other11)
-    g11 = lax.all_to_all(jnp.broadcast_to(mine11[None], (64, LEAD // 64, LEAD)), "row", 0, 0)
-    g11 = g11.reshape(LEAD, LEAD)
-    mine, _ = lax.optimization_barrier((mine, g11[:8, :128]))
-    gram_all = lax.all_gather(mine, "row", axis=0, tiled=True)
+    upper = bit(XP)
+    kept = jnp.where(upper, frontal[:, half:], frontal[:, :half])
+    given = jnp.where(upper, frontal[:, :half], frontal[:, half:])
+    got = swap(jnp.concatenate([lead, given], axis=1), XP)
+    lead = jnp.concatenate([lead, got[:, :LEAD]], axis=0)
+    columns = jnp.concatenate([kept, got[:, LEAD:]], axis=0)
+    quarter = 2 * core + upper.astype(jnp.int32)
+    square = lax.dynamic_slice(lead, (0, quarter * 128), (lead.shape[0], 128))
+    gram = jnp.einsum("rp,rc->pc", lead, jnp.concatenate([columns, square], axis=1), precision=HI)
+
+    a, b, c, h = gram[:, :384], gram[:, 384:768], gram[:, 768:1024], gram[:, 1024:]
+    a, a_out = halves(a, XM)
+    b, b_out = halves(b, YP)
+    ch, ch_out = halves(gram[:, 768:], ZP)
+    ch = ch + swap(ch_out, ZP)
+    a = a + swap(a_out, XM)
+    b = b + swap(b_out, YP)
+    c, h = ch[:, :256], ch[:, 256:]
+
+    c, c_out = halves(c, XM)
+    a, a_out = halves(a, YP)
+    b, b_out = halves(b, ZP)
+    ch = swap(jnp.concatenate([c_out, side(h, 2)], axis=1), XM)
+    a = a + swap(a_out, YP)
+    b = b + swap(b_out, ZP)
+    c, h = c + ch[:, :256], h + stacked(ch[:, 256:], 2)
+
+    c, c_out = halves(c, YP)
+    a, a_out = halves(a, ZP)
+    b, b_out = halves(b, XM)
+    ch = swap(jnp.concatenate([c_out, side(h, 4)], axis=1), YP)
+    a = a + swap(a_out, ZP)
+    b = b + swap(b_out, XM)
+    c, h = c + ch[:, :256], h + stacked(ch[:, 256:], 4)
+
+    rest = jnp.concatenate([a, b, c], axis=1)
+    for link in (YM, ZM):
+        rest, out = halves(rest, link)
+        n = out.shape[0]
+        got = swap(jnp.concatenate([out, side(h, 8)], axis=0), link)
+        rest, h = rest + got[:n], h + stacked(got[n:], 8)
+
+    h = joined(h, swap(h, ZP), ZP, 0)
+    h = joined(h, swap(h, XP), XP, 1)
+    got = across(h)
+    g11 = jnp.concatenate([jnp.where(core == 0, h, got), jnp.where(core == 0, got, h)], axis=1)
     inverse = inverse_factor(g11)
-    projected = jnp.dot(inverse, gram_all, precision=HI)
+
+    rest = joined(rest, swap(rest, ZM), ZM, 0)
+    rest = joined(rest, swap(rest, YM), YM, 0)
+    got = swap(rest, XM)
+    view = lambda x: x.reshape(1, 1, 1, 1, *x.shape)
+    cut = lambda x: (view(x[:, :384]), view(x[:, 384:768]), view(x[:, 768:]))
+    order = ((XM, YP, ZP), (YP, ZP, XM), (ZP, XM, YP))
+    axis_of = lambda part, link: 0 if link == XP else 1 + order[part].index(link)
+    parts = [joined(u, v, XM, axis_of(i, XM)) for i, (u, v) in enumerate(zip(cut(rest), cut(got)))]
+    for step in ((YP, ZP, XP), (ZP, XP, YP), (XP, YP, ZP)):
+        gots = [swap(parts[i], step[i]) for i in range(3)]
+        parts = [joined(parts[i], gots[i], step[i], axis_of(i, step[i])) for i in range(3)]
+    parts = [x.reshape(2, LEAD, x.shape[-1]) for x in parts]
+    whole = jnp.concatenate([x[s] for s in range(2) for x in parts], axis=1)
+    projected = jnp.dot(inverse, whole, precision=HI)
     column_ids = core * width + jnp.arange(width, dtype=jnp.int32)
-    kept = column_ids[None, :] >= jnp.arange(LEAD, dtype=jnp.int32)[:, None]
-    return jnp.where(kept, projected, 0.0)
+    keep = column_ids[None, :] >= jnp.arange(LEAD, dtype=jnp.int32)[:, None]
+    return jnp.where(keep, projected, 0.0)
 
 
 def solution(mesh):

time: 171 us -> 141 us (0.82)
  blocking collectives: 64.3 us -> 0 us
  waiting for transfers between devices: 44.5 us -> 70.2 us
  starting transfers between devices: 5.97 us -> 31.4 us
  between operations: 14.1 us -> 1.57 us
  matrix products: 13.6 us -> 10.9 us
  local copies, waits for them, and re-layouts: 3.39 us -> 0.77 us
    ppermute x2 -> x28, waiting for transfers between devices: 2.7 us -> 70.2 us  [the longest x26 68.9 us: swap(): return lax.ppermute(x, ('row', 'col'), flip(link))]
    all_to_all x1 -> x0, blocking collectives: 64.3 us -> none  [body(): pieces = lax.all_to_all(gram.reshape(64, LEAD // 64, width), 'row', 0, 0)]
    ppermute x2 -> x28, starting transfers between devices: 0.09 us -> 31.4 us  [the longest x26 31.2 us: swap(): return lax.ppermute(x, ('row', 'col'), flip(link))]
    all_gather x1 -> x0, waiting for transfers between devices: 22.3 us -> none  [body(): gram_all = lax.all_gather(mine, 'row', axis=0, tiled=True)]
    all_to_all x1 -> x0, waiting for transfers between devices: 19.5 us -> none  [body(): lax.all_to_all(jnp.broadcast_to(mine11[None], (64, LEAD // 64, LEAD)), 'r...]
    all_to_all x1 -> x0, starting transfers between devices: 5.88 us -> none  [body(): lax.all_to_all(jnp.broadcast_to(mine11[None], (64, LEAD // 64, LEAD)), 'r...]
    reduce_sum x1 -> x0, other arithmetic: 3.03 us -> none  [body(): mine = jnp.sum(pieces, axis=0)]
    dot_general x2, matrix products: 13.6 us -> 10.9 us  [the longest x1 8.58 us: body(): projected = jnp.dot(inverse, whole, precision=HI)]
  transfers between devices with their start and end apart: 4 -> 28, of which waited for: 4 -> 23; matrix products, arithmetic and copies ran while one was open for 1% -> 1% of each run, Pallas kernels for 12% -> 15%
where the time goes in v1:
time: 141 us
  waiting for transfers between devices  70.2 us (50%)
  starting transfers between devices  31.4 us (22%)
  Pallas kernels  20.7 us (15%)
  matrix products  10.9 us (8%)
  other arithmetic  5.14 us (4%)
  between operations  1.57 us (1%)
    ppermute x26, waiting for transfers between devices, swap(): return lax.ppermute(x, ('row', 'col'), flip(link))  68.9 us
    ppermute x26, starting transfers between devices, swap(): return lax.ppermute(x, ('row', 'col'), flip(link))  31.2 us
    pallas_call x1, Pallas kernels, inverse_factor(): pl.pallas_call(kernel, out_shape=jax.ShapeDtypeStruct((n, n), jnp.float32...  20.7 us
    dot_general x1, matrix products, body(): projected = jnp.dot(inverse, whole, precision=HI)  8.58 us
  transfers between devices with their start and end apart: 28, of which 23 were waited for; matrix products, arithmetic and copies ran while one was open for 1% of the time, Pallas kernels for 15%

profile of v1, /device:TPU:0, one launch (start us, length us, event | category | flops | bytes accessed | tf_op | source)
XLA Modules:
  0.0 140.6 jit_solution(12249609611855492952)
XLA Ops:
  0.7 1.4 select_bitcast_fusion
  2.1 0.1 collective-permute-start
  2.2 0.1 slice_select_fusion
  2.3 1.3 collective-permute-done
  3.8 1.7 %collective-permute-start.1 = (f32[128,1536]{1,0:T(8,128)S(1)}, f32[128,1536]{1,0:T(8,128)S(1)}, u32[]{:S(2)}, u32[]{:S(2)}) collective-permute-start(f32[128,1536]{1,0:T(8,128)S(1)} %pad_maximum_fusion.2), channel_id=1, source_target_pairs={{0,2},{1,7},{2,0},{3,5},{4,6},{5,3},{6,4},{7,1},{8,10},{9,15},{10,... | collective-permute-start | bytes 2359304 | tf_op jit(solution)/shard_map/ppermute | solution.py:121
  5.4 10.4 %collective-permute-done.1 = f32[128,1536]{1,0:T(8,128)S(1)} collective-permute-done((f32[128,1536]{1,0:T(8,128)S(1)}, f32[128,1536]{1,0:T(8,128)S(1)}, u32[]{:S(2)}, u32[]{:S(2)}) %collective-permute-start.1) | collective-permute-done | bytes 786464 | tf_op jit(solution)/shard_map/ppermute | solution.py:121
  15.9 2.3 %fusion.1 = f32[512,1152]{1,0:T(8,128)S(1)} fusion(f32[256,128]{1,0:T(8,128)S(1)} %fusion.9, f32[128,1024]{1,0:T(8,128)S(1)} %slice.134, f32[128,1024]{1,0:T(8,128)S(1)} %get-tuple-element.23, f32[128,512]{1,0:T(8,128)S(1)} %slice.133, f32[128,512]{1,0:T(8,128)S(1)} %broadcast_select_fusion.14), kind=kOutput, calls=%fused_computation.4 | convolution fusion | flops 1812660224 | bytes 4063232 | tf_op jit(solution)/shard_map/rp,rc->pc/dot_general | solution.py:154
  18.3 0.1 slice_select_fusion.3
  18.4 2.1 %collective-permute-start.2 = (f32[256,384]{1,0:T(8,128)S(1)}, f32[256,384]{1,0:T(8,128)}, u32[]{:S(2)}, u32[]{:S(2)}) collective-permute-start(f32[256,384]{1,0:T(8,128)S(1)} %get-tuple-element.10), channel_id=1, source_target_pairs={{0,32},{1,97},{2,34},{3,99},{4,36},{5,101},{6,38},{7,103},{8,40},{... | collective-permute-start | bytes 1179656 | tf_op jit(solution)/shard_map/ppermute | solution.py:121
  20.5 2.8 %collective-permute-start.5 = (f32[256,384]{1,0:T(8,128)S(1)}, f32[256,384]{1,0:T(8,128)}, u32[]{:S(2)}, u32[]{:S(2)}) collective-permute-start(f32[256,384]{1,0:T(8,128)S(1)} %get-tuple-element.8), channel_id=1, source_target_pairs={{0,6},{1,3},{2,4},{3,1},{4,2},{5,7},{6,0},{7,5},{8,14},{9,11},{10,... | collective-permute-start | bytes 1179656 | tf_op jit(solution)/shard_map/ppermute | solution.py:121
  23.2 1.6 %collective-permute-start.8 = (f32[256,384]{1,0:T(8,128)S(1)}, f32[256,384]{1,0:T(8,128)}, u32[]{:S(2)}, u32[]{:S(2)}) collective-permute-start(f32[256,384]{1,0:T(8,128)S(1)} %get-tuple-element.9), channel_id=1, source_target_pairs={{0,8},{1,25},{2,10},{3,27},{4,12},{5,29},{6,14},{7,31},{8,0},{9,17... | collective-permute-start | bytes 1179656 | tf_op jit(solution)/shard_map/ppermute | solution.py:121
  24.8 1.5 %collective-permute-done.2 = f32[256,384]{1,0:T(8,128)} collective-permute-done((f32[256,384]{1,0:T(8,128)S(1)}, f32[256,384]{1,0:T(8,128)}, u32[]{:S(2)}, u32[]{:S(2)}) %collective-permute-start.2) | collective-permute-done | bytes 393248 | tf_op jit(solution)/shard_map/ppermute | solution.py:121
  26.4 3.2 %collective-permute-done.5 = f32[256,384]{1,0:T(8,128)} collective-permute-done((f32[256,384]{1,0:T(8,128)S(1)}, f32[256,384]{1,0:T(8,128)}, u32[]{:S(2)}, u32[]{:S(2)}) %collective-permute-start.5) | collective-permute-done | bytes 393248 | tf_op jit(solution)/shard_map/ppermute | solution.py:121
  29.6 1.5 %collective-permute-done.8 = f32[256,384]{1,0:T(8,128)} collective-permute-done((f32[256,384]{1,0:T(8,128)S(1)}, f32[256,384]{1,0:T(8,128)}, u32[]{:S(2)}, u32[]{:S(2)}) %collective-permute-start.8) | collective-permute-done | bytes 393248 | tf_op jit(solution)/shard_map/ppermute | solution.py:121
  31.1 1.4 select_add_fusion.1
  32.5 1.7 %collective-permute-start.6 = (f32[128,384]{1,0:T(8,128)S(1)}, f32[128,384]{1,0:T(8,128)S(1)}, u32[]{:S(2)}, u32[]{:S(2)}) collective-permute-start(f32[128,384]{1,0:T(8,128)S(1)} %slice_select_fusion.6), channel_id=1, source_target_pairs={{0,8},{1,25},{2,10},{3,27},{4,12},{5,29},{6,14},{7,31},{8,0},{9,17... | collective-permute-start | bytes 589832 | tf_op jit(solution)/shard_map/ppermute | solution.py:121
  34.3 0.2 collective-permute-start.9
  34.5 1.3 collective-permute-start.3
  35.8 2.5 %collective-permute-done.6 = f32[128,384]{1,0:T(8,128)S(1)} collective-permute-done((f32[128,384]{1,0:T(8,128)S(1)}, f32[128,384]{1,0:T(8,128)S(1)}, u32[]{:S(2)}, u32[]{:S(2)}) %collective-permute-start.6) | collective-permute-done | bytes 196640 | tf_op jit(solution)/shard_map/ppermute | solution.py:121
  38.4 0.2 collective-permute-start.7
  38.5 1.5 %collective-permute-done.9 = f32[128,384]{1,0:T(8,128)S(1)} collective-permute-done((f32[128,384]{1,0:T(8,128)S(1)}, f32[128,384]{1,0:T(8,128)S(1)}, u32[]{:S(2)}, u32[]{:S(2)}) %collective-permute-start.9) | collective-permute-done | bytes 196640 | tf_op jit(solution)/shard_map/ppermute | solution.py:121
  40.1 1.3 collective-permute-start.10
  41.4 0.8 collective-permute-done.3
  42.3 0.5 collective-permute-start.4
  42.8 0.2 collective-permute-done.7
  43.1 2.9 %collective-permute-done.10 = f32[64,384]{1,0:T(8,128)S(1)} collective-permute-done((f32[64,384]{1,0:T(8,128)S(1)}, f32[64,384]{1,0:T(8,128)S(1)}, u32[]{:S(2)}, u32[]{:S(2)}) %collective-permute-start.10) | collective-permute-done | bytes 98336 | tf_op jit(solution)/shard_map/ppermute | solution.py:121
  46.0 2.0 %collective-permute-done.4 = f32[64,768]{1,0:T(8,128)S(1)} collective-permute-done((f32[64,768]{1,0:T(8,128)S(1)}, f32[64,768]{1,0:T(8,128)S(1)}, u32[]{:S(2)}, u32[]{:S(2)}) %collective-permute-start.4) | collective-permute-done | bytes 196640 | tf_op jit(solution)/shard_map/ppermute | solution.py:121
  48.3 2.3 %collective-permute-start.11 = (f32[64,1024]{1,0:T(8,128)S(1)}, f32[64,1024]{1,0:T(8,128)S(1)}, u32[]{:S(2)}, u32[]{:S(2)}) collective-permute-start(f32[64,1024]{1,0:T(8,128)S(1)} %pad_maximum_fusion.15), channel_id=1, source_target_pairs={{0,24},{1,9},{2,26},{3,11},{4,28},{5,13},{6,30},{7,15},{8,16},{9,1... | collective-permute-start | bytes 786440 | tf_op jit(solution)/shard_map/ppermute | solution.py:121
  50.5 5.4 %collective-permute-done.11 = f32[64,1024]{1,0:T(8,128)S(1)} collective-permute-done((f32[64,1024]{1,0:T(8,128)S(1)}, f32[64,1024]{1,0:T(8,128)S(1)}, u32[]{:S(2)}, u32[]{:S(2)}) %collective-permute-start.11) | collective-permute-done | bytes 262176 | tf_op jit(solution)/shard_map/ppermute | solution.py:121
  56.2 4.1 %collective-permute-start.12 = (f32[48,1024]{1,0:T(8,128)S(1)}, f32[48,1024]{1,0:T(8,128)S(1)}, u32[]{:S(2)}, u32[]{:S(2)}) collective-permute-start(f32[48,1024]{1,0:T(8,128)S(1)} %pad_maximum_fusion.18), channel_id=1, source_target_pairs={{0,96},{1,33},{2,98},{3,35},{4,100},{5,37},{6,102},{7,39},{8,104},... | collective-permute-start | bytes 589832 | tf_op jit(solution)/shard_map/ppermute | solution.py:121
  60.3 4.6 %collective-permute-done.12 = f32[48,1024]{1,0:T(8,128)S(1)} collective-permute-done((f32[48,1024]{1,0:T(8,128)S(1)}, f32[48,1024]{1,0:T(8,128)S(1)}, u32[]{:S(2)}, u32[]{:S(2)}) %collective-permute-start.12) | collective-permute-done | bytes 196640 | tf_op jit(solution)/shard_map/ppermute | solution.py:121
  65.0 3.1 %collective-permute-start.16 = (f32[16,1024]{1,0:T(8,128)S(1)}, f32[16,1024]{1,0:T(8,128)S(1)}, u32[]{:S(2)}, u32[]{:S(2)}) collective-permute-start(f32[16,1024]{1,0:T(8,128)S(1)} %slice_add_fusion.3), channel_id=1, source_target_pairs={{0,96},{1,33},{2,98},{3,35},{4,100},{5,37},{6,102},{7,39},{8,104},... | collective-permute-start | bytes 196616 | tf_op jit(solution)/shard_map/ppermute | solution.py:121
  68.2 0.1 collective-permute-start.13
  68.3 2.3 %collective-permute-done.16 = f32[16,1024]{1,0:T(8,128)S(1)} collective-permute-done((f32[16,1024]{1,0:T(8,128)S(1)}, f32[16,1024]{1,0:T(8,128)S(1)}, u32[]{:S(2)}, u32[]{:S(2)}) %collective-permute-start.16) | collective-permute-done | bytes 65568 | tf_op jit(solution)/shard_map/ppermute | solution.py:121
  70.6 2.4 %collective-permute-start.17 = (f32[32,1024]{1,0:T(8,128)S(1)}, f32[32,1024]{1,0:T(8,128)S(1)}, u32[]{:S(2)}, u32[]{:S(2)}) collective-permute-start(f32[32,1024]{1,0:T(8,128)S(1)} %pad_maximum_fusion.21), channel_id=1, source_target_pairs={{0,24},{1,9},{2,26},{3,11},{4,28},{5,13},{6,30},{7,15},{8,16},{9,1... | collective-permute-start | bytes 393224 | tf_op jit(solution)/shard_map/ppermute | solution.py:121
  72.9 0.3 collective-permute-done.13
  73.3 0.1 collective-permute-start.14
  73.4 3.5 %collective-permute-done.17 = f32[32,1024]{1,0:T(8,128)S(1)} collective-permute-done((f32[32,1024]{1,0:T(8,128)S(1)}, f32[32,1024]{1,0:T(8,128)S(1)}, u32[]{:S(2)}, u32[]{:S(2)}) %collective-permute-start.17) | collective-permute-done | bytes 131104 | tf_op jit(solution)/shard_map/ppermute | solution.py:121
  76.9 1.7 %collective-permute-start.18 = (f32[64,1024]{1,0:T(8,128)S(1)}, f32[64,1024]{1,0:T(8,128)S(1)}, u32[]{:S(2)}, u32[]{:S(2)}) collective-permute-start(f32[64,1024]{1,0:T(8,128)S(1)} %pad_maximum_fusion.10), channel_id=1, source_target_pairs={{0,6},{1,3},{2,4},{3,1},{4,2},{5,7},{6,0},{7,5},{8,14},{9,11},{10,... | collective-permute-start | bytes 786440 | tf_op jit(solution)/shard_map/ppermute | solution.py:121
  78.6 1.1 collective-permute-done.14
  79.9 4.8 %collective-permute-done.18 = f32[64,1024]{1,0:T(8,128)S(1)} collective-permute-done((f32[64,1024]{1,0:T(8,128)S(1)}, f32[64,1024]{1,0:T(8,128)S(1)}, u32[]{:S(2)}, u32[]{:S(2)}) %collective-permute-start.18) | collective-permute-done | bytes 262176 | tf_op jit(solution)/shard_map/ppermute | solution.py:121
  84.9 0.1 collective-permute-start.22
  85.1 4.7 %collective-permute-done.25 = f32[1,1,2,1,64,256]{5,4,3,2,1,0:T(8,128)S(1)} collective-permute-done((f32[1,1,2,1,64,256]{5,4,3,2,1,0:T(8,128)S(1)}, f32[1,1,2,1,64,256]{5,4,3,2,1,0:T(8,128)S(1)}, u32[]{:S(2)}, u32[]{:S(2)}) %collective-permute-start.25) | collective-permute-done | bytes 131104 | tf_op jit(solution)/shard_map/ppermute | solution.py:121
  89.9 0.7 collective-permute-done.22
  90.7 2.1 %collective-permute-start.23 = (f32[1,1,2,2,64,384]{5,4,3,2,1,0:T(8,128)S(1)}, f32[1,1,2,2,64,384]{5,4,3,2,1,0:T(8,128)S(1)}, u32[]{:S(2)}, u32[]{:S(2)}) collective-permute-start(f32[1,1,2,2,64,384]{5,4,3,2,1,0:T(8,128)S(1)} %pad_maximum_fusion.12), channel_id=1, source_target_pairs={{0,2},{1,7},{2,0},{3,5},{4,6},{5,3},{6,4},{7,1},{8,10},{9,15},{10,... | collective-permute-start | bytes 1179656 | tf_op jit(solution)/shard_map/ppermute | solution.py:121
  92.9 0.1 collective-permute-start.20
  93.0 3.3 %collective-permute-done.26 = f32[2,1,2,1,64,256]{5,4,3,2,1,0:T(8,128)S(1)} collective-permute-done((f32[2,1,2,1,64,256]{5,4,3,2,1,0:T(8,128)S(1)}, f32[2,1,2,1,64,256]{5,4,3,2,1,0:T(8,128)S(1)}, u32[]{:S(2)}, u32[]{:S(2)}) %collective-permute-start.26) | collective-permute-done | bytes 262176 | tf_op jit(solution)/shard_map/ppermute | solution.py:121
  96.4 0.3 collective-permute-start.27
  96.7 0.1 pad_maximum_fusion.g_ref
  96.9 20.7 %shard_map.28 = f32[512,512]{1,0:T(8,128)S(1)} custom-call(f32[512,512]{1,0:T(8,128)S(1)} %pad_maximum_fusion.g_ref), custom_call_target="tpu_custom_call" | custom-call | flops 1800000000 | bytes 2097152 | tf_op jit(solution)/shard_map/pallas_call | solution.py:86
  117.7 1.3 collective-permute-start.21
  119.2 0.1 collective-permute-start.24
  119.3 0.1 broadcast_select_fusion.4
  119.4 0.1 pad_maximum_fusion.7
  119.5 10.3 %collective-permute-done.21 = f32[1,2,2,2,64,384]{5,4,3,2,1,0:T(8,128)S(1)} collective-permute-done((f32[1,2,2,2,64,384]{5,4,3,2,1,0:T(8,128)S(1)}, f32[1,2,2,2,64,384]{5,4,3,2,1,0:T(8,128)S(1)}, u32[]{:S(2)}, u32[]{:S(2)}) %collective-permute-start.21) | collective-permute-done | bytes 786464 | tf_op jit(solution)/shard_map/ppermute | solution.py:121
  129.8 0.2 broadcast_select_fusion.2
  129.9 0.1 constant_dynamic-update-slice_fusion.42
  130.1 1.2 collective-permute-done.24
  131.3 0.1 broadcast_select_fusion
  131.4 0.1 pad_maximum_fusion.1
  131.6 0.1 constant_dynamic-update-slice_fusion.41
  131.7 0.1 constant_dynamic-update-slice_fusion.39
  131.8 0.1 constant_dynamic-update-slice_fusion.38
  132.0 8.6 %fusion = f32[512,2048]{1,0:T(8,128)} fusion(f32[512,512]{1,0:T(8,128)S(1)} %shard_map.28, f32[512,2048]{1,0:T(8,128)S(1)} %constant_dynamic-update-slice_fusion.37, s32[2048]{0:T(1024)S(1)} %iota_add_fusion), kind=kOutput, calls=%fused_computation.1 | convolution fusion | flops 6444548096 | bytes 9445376 | tf_op jit(solution)/shard_map/dot_general | solution.py:207
  (108 shorter events, 2.1 us)
Async XLA Ops:
  2.1 1.6 %collective-permute-start = (f32[128,512]{1,0:T(8,128)S(1)}, f32[128,512]{1,0:T(8,128)S(1)}, u32[]{:S(2)}, u32[]{:S(2)}) collective-permute-start(f32[128,512]{1,0:T(8,128)S(1)} %slice.130), channel_id=1, source_target_pairs={{0,1},{1,0},{2,3},{3,2},{4,5},{5,4},{6,7},{7,6},{8,9},{9,8},{10,11... | collective-permute-start | bytes 786440 | tf_op jit(solution)/shard_map/ppermute | solution.py:124
  3.8 12.1 %collective-permute-start.1 = (f32[128,1536]{1,0:T(8,128)S(1)}, f32[128,1536]{1,0:T(8,128)S(1)}, u32[]{:S(2)}, u32[]{:S(2)}) collective-permute-start(f32[128,1536]{1,0:T(8,128)S(1)} %pad_maximum_fusion.2), channel_id=1, source_target_pairs={{0,2},{1,7},{2,0},{3,5},{4,6},{5,3},{6,4},{7,1},{8,10},{9,15},{10,... | collective-permute-start | bytes 2359304 | tf_op jit(solution)/shard_map/ppermute | solution.py:121
  18.4 8.0 %collective-permute-start.2 = (f32[256,384]{1,0:T(8,128)S(1)}, f32[256,384]{1,0:T(8,128)}, u32[]{:S(2)}, u32[]{:S(2)}) collective-permute-start(f32[256,384]{1,0:T(8,128)S(1)} %get-tuple-element.10), channel_id=1, source_target_pairs={{0,32},{1,97},{2,34},{3,99},{4,36},{5,101},{6,38},{7,103},{8,40},{... | collective-permute-start | bytes 1179656 | tf_op jit(solution)/shard_map/ppermute | solution.py:121
  20.5 9.1 %collective-permute-start.5 = (f32[256,384]{1,0:T(8,128)S(1)}, f32[256,384]{1,0:T(8,128)}, u32[]{:S(2)}, u32[]{:S(2)}) collective-permute-start(f32[256,384]{1,0:T(8,128)S(1)} %get-tuple-element.8), channel_id=1, source_target_pairs={{0,6},{1,3},{2,4},{3,1},{4,2},{5,7},{6,0},{7,5},{8,14},{9,11},{10,... | collective-permute-start | bytes 1179656 | tf_op jit(solution)/shard_map/ppermute | solution.py:121
  23.2 7.9 %collective-permute-start.8 = (f32[256,384]{1,0:T(8,128)S(1)}, f32[256,384]{1,0:T(8,128)}, u32[]{:S(2)}, u32[]{:S(2)}) collective-permute-start(f32[256,384]{1,0:T(8,128)S(1)} %get-tuple-element.9), channel_id=1, source_target_pairs={{0,8},{1,25},{2,10},{3,27},{4,12},{5,29},{6,14},{7,31},{8,0},{9,17... | collective-permute-start | bytes 1179656 | tf_op jit(solution)/shard_map/ppermute | solution.py:121
  32.5 5.7 %collective-permute-start.6 = (f32[128,384]{1,0:T(8,128)S(1)}, f32[128,384]{1,0:T(8,128)S(1)}, u32[]{:S(2)}, u32[]{:S(2)}) collective-permute-start(f32[128,384]{1,0:T(8,128)S(1)} %slice_select_fusion.6), channel_id=1, source_target_pairs={{0,8},{1,25},{2,10},{3,27},{4,12},{5,29},{6,14},{7,31},{8,0},{9,17... | collective-permute-start | bytes 589832 | tf_op jit(solution)/shard_map/ppermute | solution.py:121
  34.3 5.8 %collective-permute-start.9 = (f32[128,384]{1,0:T(8,128)S(1)}, f32[128,384]{1,0:T(8,128)S(1)}, u32[]{:S(2)}, u32[]{:S(2)}) collective-permute-start(f32[128,384]{1,0:T(8,128)S(1)} %slice_select_fusion.5), channel_id=1, source_target_pairs={{0,32},{1,97},{2,34},{3,99},{4,36},{5,101},{6,38},{7,103},{8,40},{... | collective-permute-start | bytes 589832 | tf_op jit(solution)/shard_map/ppermute | solution.py:121
  34.5 7.7 %collective-permute-start.3 = (f32[128,512]{1,0:T(8,128)S(1)}, f32[128,512]{1,0:T(8,128)S(1)}, u32[]{:S(2)}, u32[]{:S(2)}) collective-permute-start(f32[128,512]{1,0:T(8,128)S(1)} %pad_maximum_fusion.13), channel_id=1, source_target_pairs={{0,6},{1,3},{2,4},{3,1},{4,2},{5,7},{6,0},{7,5},{8,14},{9,11},{10,... | collective-permute-start | bytes 786440 | tf_op jit(solution)/shard_map/ppermute | solution.py:121
  38.4 4.7 %collective-permute-start.7 = (f32[64,384]{1,0:T(8,128)S(1)}, f32[64,384]{1,0:T(8,128)S(1)}, u32[]{:S(2)}, u32[]{:S(2)}) collective-permute-start(f32[64,384]{1,0:T(8,128)S(1)} %slice_select_fusion.10), channel_id=1, source_target_pairs={{0,32},{1,97},{2,34},{3,99},{4,36},{5,101},{6,38},{7,103},{8,40},{... | collective-permute-start | bytes 294920 | tf_op jit(solution)/shard_map/ppermute | solution.py:121
  40.1 5.9 %collective-permute-start.10 = (f32[64,384]{1,0:T(8,128)S(1)}, f32[64,384]{1,0:T(8,128)S(1)}, u32[]{:S(2)}, u32[]{:S(2)}) collective-permute-start(f32[64,384]{1,0:T(8,128)S(1)} %slice_select_fusion.9), channel_id=1, source_target_pairs={{0,6},{1,3},{2,4},{3,1},{4,2},{5,7},{6,0},{7,5},{8,14},{9,11},{10,... | collective-permute-start | bytes 294920 | tf_op jit(solution)/shard_map/ppermute | solution.py:121
  42.3 5.7 %collective-permute-start.4 = (f32[64,768]{1,0:T(8,128)S(1)}, f32[64,768]{1,0:T(8,128)S(1)}, u32[]{:S(2)}, u32[]{:S(2)}) collective-permute-start(f32[64,768]{1,0:T(8,128)S(1)} %constant_dynamic-update-slice_fusion), channel_id=1, source_target_pairs={{0,8},{1,25},{2,10},{3,27},{4,12},{5,29},{6,14},{7,31},{8,0},{9,17... | collective-permute-start | bytes 589832 | tf_op jit(solution)/shard_map/ppermute | solution.py:121
  48.3 7.7 %collective-permute-start.11 = (f32[64,1024]{1,0:T(8,128)S(1)}, f32[64,1024]{1,0:T(8,128)S(1)}, u32[]{:S(2)}, u32[]{:S(2)}) collective-permute-start(f32[64,1024]{1,0:T(8,128)S(1)} %pad_maximum_fusion.15), channel_id=1, source_target_pairs={{0,24},{1,9},{2,26},{3,11},{4,28},{5,13},{6,30},{7,15},{8,16},{9,1... | collective-permute-start | bytes 786440 | tf_op jit(solution)/shard_map/ppermute | solution.py:121
  56.2 8.8 %collective-permute-start.12 = (f32[48,1024]{1,0:T(8,128)S(1)}, f32[48,1024]{1,0:T(8,128)S(1)}, u32[]{:S(2)}, u32[]{:S(2)}) collective-permute-start(f32[48,1024]{1,0:T(8,128)S(1)} %pad_maximum_fusion.18), channel_id=1, source_target_pairs={{0,96},{1,33},{2,98},{3,35},{4,100},{5,37},{6,102},{7,39},{8,104},... | collective-permute-start | bytes 589832 | tf_op jit(solution)/shard_map/ppermute | solution.py:121
  65.0 5.6 %collective-permute-start.16 = (f32[16,1024]{1,0:T(8,128)S(1)}, f32[16,1024]{1,0:T(8,128)S(1)}, u32[]{:S(2)}, u32[]{:S(2)}) collective-permute-start(f32[16,1024]{1,0:T(8,128)S(1)} %slice_add_fusion.3), channel_id=1, source_target_pairs={{0,96},{1,33},{2,98},{3,35},{4,100},{5,37},{6,102},{7,39},{8,104},... | collective-permute-start | bytes 196616 | tf_op jit(solution)/shard_map/ppermute | solution.py:121
  68.2 5.0 %collective-permute-start.13 = (f32[256,128]{1,0:T(8,128)S(1)}, f32[256,128]{1,0:T(8,128)S(1)}, u32[]{:S(2)}, u32[]{:S(2)}) collective-permute-start(f32[256,128]{1,0:T(8,128)S(1)} %add.129), channel_id=1, source_target_pairs={{0,32},{1,97},{2,34},{3,99},{4,36},{5,101},{6,38},{7,103},{8,40},{... | collective-permute-start | bytes 393224 | tf_op jit(solution)/shard_map/ppermute | solution.py:121
  70.6 6.3 %collective-permute-start.17 = (f32[32,1024]{1,0:T(8,128)S(1)}, f32[32,1024]{1,0:T(8,128)S(1)}, u32[]{:S(2)}, u32[]{:S(2)}) collective-permute-start(f32[32,1024]{1,0:T(8,128)S(1)} %pad_maximum_fusion.21), channel_id=1, source_target_pairs={{0,24},{1,9},{2,26},{3,11},{4,28},{5,13},{6,30},{7,15},{8,16},{9,1... | collective-permute-start | bytes 393224 | tf_op jit(solution)/shard_map/ppermute | solution.py:121
  73.3 6.5 %collective-permute-start.14 = (f32[512,128]{1,0:T(8,128)S(1)}, f32[512,128]{1,0:T(8,128)S(1)}, u32[]{:S(2)}, u32[]{:S(2)}) collective-permute-start(f32[512,128]{1,0:T(8,128)S(1)} %pad_maximum_fusion.16), channel_id=1, source_target_pairs={{0,2},{1,7},{2,0},{3,5},{4,6},{5,3},{6,4},{7,1},{8,10},{9,15},{10,... | collective-permute-start | bytes 786440 | tf_op jit(solution)/shard_map/ppermute | solution.py:121
  76.9 7.8 %collective-permute-start.18 = (f32[64,1024]{1,0:T(8,128)S(1)}, f32[64,1024]{1,0:T(8,128)S(1)}, u32[]{:S(2)}, u32[]{:S(2)}) collective-permute-start(f32[64,1024]{1,0:T(8,128)S(1)} %pad_maximum_fusion.10), channel_id=1, source_target_pairs={{0,6},{1,3},{2,4},{3,1},{4,2},{5,7},{6,0},{7,5},{8,14},{9,11},{10,... | collective-permute-start | bytes 786440 | tf_op jit(solution)/shard_map/ppermute | solution.py:121
  79.8 16.8 %collective-permute-start.15 = (f32[512,256]{1,0:T(8,128)S(1)}, f32[512,256]{1,0:T(8,128)S(1)}, u32[]{:S(2)}, u32[]{:S(2)}) collective-permute-start(f32[512,256]{1,0:T(8,128)S(1)} %pad_maximum_fusion.8), channel_id=1, source_target_pairs={{0,1},{1,0},{2,3},{3,2},{4,5},{5,4},{6,7},{7,6},{8,9},{9,8},{10,11... | collective-permute-start | bytes 1572872 | tf_op jit(solution)/shard_map/ppermute | solution.py:124
  84.7 5.0 %collective-permute-start.25 = (f32[1,1,2,1,64,256]{5,4,3,2,1,0:T(8,128)S(1)}, f32[1,1,2,1,64,256]{5,4,3,2,1,0:T(8,128)S(1)}, u32[]{:S(2)}, u32[]{:S(2)}) collective-permute-start(f32[1,1,2,1,64,256]{5,4,3,2,1,0:T(8,128)S(1)} %pad_maximum_fusion.22), channel_id=1, source_target_pairs={{0,2},{1,7},{2,0},{3,5},{4,6},{5,3},{6,4},{7,1},{8,10},{9,15},{10,... | collective-permute-start | bytes 393224 | tf_op jit(solution)/shard_map/ppermute | solution.py:121
  84.9 5.8 %collective-permute-start.22 = (f32[1,1,1,2,64,384]{5,4,3,2,1,0:T(8,128)S(1)}, f32[1,1,1,2,64,384]{5,4,3,2,1,0:T(8,128)S(1)}, u32[]{:S(2)}, u32[]{:S(2)}) collective-permute-start(f32[1,1,1,2,64,384]{5,4,3,2,1,0:T(8,128)S(1)} %pad_maximum_fusion.20), channel_id=1, source_target_pairs={{0,32},{1,97},{2,34},{3,99},{4,36},{5,101},{6,38},{7,103},{8,40},{... | collective-permute-start | bytes 589832 | tf_op jit(solution)/shard_map/ppermute | solution.py:121
  85.0 7.8 %collective-permute-start.19 = (f32[1,2,1,1,64,384]{5,4,3,2,1,0:T(8,128)S(1)}, f32[1,2,1,1,64,384]{5,4,3,2,1,0:T(8,128)S(1)}, u32[]{:S(2)}, u32[]{:S(2)}) collective-permute-start(f32[1,2,1,1,64,384]{5,4,3,2,1,0:T(8,128)S(1)} %pad_maximum_fusion.19), channel_id=1, source_target_pairs={{0,8},{1,25},{2,10},{3,27},{4,12},{5,29},{6,14},{7,31},{8,0},{9,17... | collective-permute-start | bytes 589832 | tf_op jit(solution)/shard_map/ppermute | solution.py:121
  89.8 6.5 %collective-permute-start.26 = (f32[2,1,2,1,64,256]{5,4,3,2,1,0:T(8,128)S(1)}, f32[2,1,2,1,64,256]{5,4,3,2,1,0:T(8,128)S(1)}, u32[]{:S(2)}, u32[]{:S(2)}) collective-permute-start(f32[2,1,2,1,64,256]{5,4,3,2,1,0:T(8,128)S(1)} %pad_maximum_fusion.17), channel_id=1, source_target_pairs={{0,8},{1,25},{2,10},{3,27},{4,12},{5,29},{6,14},{7,31},{8,0},{9,17... | collective-permute-start | bytes 786440 | tf_op jit(solution)/shard_map/ppermute | solution.py:121
  90.7 28.4 %collective-permute-start.23 = (f32[1,1,2,2,64,384]{5,4,3,2,1,0:T(8,128)S(1)}, f32[1,1,2,2,64,384]{5,4,3,2,1,0:T(8,128)S(1)}, u32[]{:S(2)}, u32[]{:S(2)}) collective-permute-start(f32[1,1,2,2,64,384]{5,4,3,2,1,0:T(8,128)S(1)} %pad_maximum_fusion.12), channel_id=1, source_target_pairs={{0,2},{1,7},{2,0},{3,5},{4,6},{5,3},{6,4},{7,1},{8,10},{9,15},{10,... | collective-permute-start | bytes 1179656 | tf_op jit(solution)/shard_map/ppermute | solution.py:121
  92.9 24.7 %collective-permute-start.20 = (f32[1,2,2,1,64,384]{5,4,3,2,1,0:T(8,128)S(1)}, f32[1,2,2,1,64,384]{5,4,3,2,1,0:T(8,128)S(1)}, u32[]{:S(2)}, u32[]{:S(2)}) collective-permute-start(f32[1,2,2,1,64,384]{5,4,3,2,1,0:T(8,128)S(1)} %pad_maximum_fusion.11), channel_id=1, source_target_pairs={{0,32},{1,97},{2,34},{3,99},{4,36},{5,101},{6,38},{7,103},{8,40},{... | collective-permute-start | bytes 1179656 | tf_op jit(solution)/shard_map/ppermute | solution.py:121
  96.4 23.0 %collective-permute-start.27 = (f32[2,1,2,2,64,256]{5,4,3,2,1,0:T(8,128)S(1)}, f32[2,1,2,2,64,256]{5,4,3,2,1,0:T(8,128)S(1)}, u32[]{:S(2)}, u32[]{:S(2)}) collective-permute-start(f32[2,1,2,2,64,256]{5,4,3,2,1,0:T(8,128)S(1)} %pad_maximum_fusion.9), channel_id=1, source_target_pairs={{0,32},{1,97},{2,34},{3,99},{4,36},{5,101},{6,38},{7,103},{8,40},{... | collective-permute-start | bytes 1572872 | tf_op jit(solution)/shard_map/ppermute | solution.py:121
  117.7 12.1 %collective-permute-start.21 = (f32[1,2,2,2,64,384]{5,4,3,2,1,0:T(8,128)S(1)}, f32[1,2,2,2,64,384]{5,4,3,2,1,0:T(8,128)S(1)}, u32[]{:S(2)}, u32[]{:S(2)}) collective-permute-start(f32[1,2,2,2,64,384]{5,4,3,2,1,0:T(8,128)S(1)} %pad_maximum_fusion.3), channel_id=1, source_target_pairs={{0,2},{1,7},{2,0},{3,5},{4,6},{5,3},{6,4},{7,1},{8,10},{9,15},{10,... | collective-permute-start | bytes 2359304 | tf_op jit(solution)/shard_map/ppermute | solution.py:121
  119.2 12.1 %collective-permute-start.24 = (f32[2,1,2,2,64,384]{5,4,3,2,1,0:T(8,128)S(1)}, f32[2,1,2,2,64,384]{5,4,3,2,1,0:T(8,128)S(1)}, u32[]{:S(2)}, u32[]{:S(2)}) collective-permute-start(f32[2,1,2,2,64,384]{5,4,3,2,1,0:T(8,128)S(1)} %pad_maximum_fusion.4), channel_id=1, source_target_pairs={{0,8},{1,25},{2,10},{3,27},{4,12},{5,29},{6,14},{7,31},{8,0},{9,17... | collective-permute-start | bytes 2359304 | tf_op jit(solution)/shard_map/ppermute | solution.py:121

commit v2 on v1

--- a/solution.py
+++ b/solution.py
@@ -9,9 +9,26 @@
 HI = lax.Precision.HIGHEST
 
 
-S8=(8,128)
-def lb(x,c): return jnp.broadcast_to(x[:,c:c+1],S8)
-def sb(x,j): return jnp.broadcast_to(x[j:j+1,:],S8)
+S8 = (8, 128)
+F32 = jnp.float32
+LEFT = (((0,), (0,)), ((), ()))
+
+
+def lb(x, c):
+    return jnp.broadcast_to(x[:, c : c + 1], S8)
+
+
+def sb(x, j):
+    return jnp.broadcast_to(x[j : j + 1, :], S8)
+
+
+def mm(x, y):
+    return jnp.dot(x, y, precision=HI, preferred_element_type=F32)
+
+
+def mtm(x, y):
+    return lax.dot_general(x, y, LEFT, precision=HI, preferred_element_type=F32)
+
 
 def chol_inv_128(V, sub, lane):
     V=list(V)
@@ -54,40 +71,120 @@
                 V[m]=v; E[m]=e
     return out
 
-def kernel(g_ref, o_ref, a, u, stack):
-    a[...]=g_ref[...]
-    o_ref[...]=jnp.zeros_like(o_ref)
-    sub=lax.broadcasted_iota(jnp.int32,S8,0); lane=lax.broadcasted_iota(jnp.int32,S8,1)
-    d=stack
-    d[...]=g_ref[0:128,0:128]
-    T=(((0,),(0,)),((),()))
-    @pl.loop(0,4)
-    def _(p):
-        o=chol_inv_128([d[8*k:8*k+8,:] for k in range(16)],sub,lane)
-        for k in range(16): d[8*k:8*k+8,:]=o[k]
-        for q in range(4):
-            @pl.when(p==q)
-            def _():
-                lo,hi=128*q,128*(q+1)
-                linv=d[...]
-                if q<3:
-                    up=jnp.dot(linv,a[lo:hi,hi:],precision=HI,preferred_element_type=jnp.float32)
-                    d[...]=a[hi:hi+128,hi:hi+128]-lax.dot_general(up[:,:128],up[:,:128],T,precision=HI,preferred_element_type=jnp.float32)
-                    if q<2:
-                        a[hi:,hi:]=a[hi:,hi:]-lax.dot_general(up,up,T,precision=HI,preferred_element_type=jnp.float32)
-                o_ref[lo:hi,lo:hi]=linv
-                if q>0:
-                    o_ref[lo:hi,:lo]=jnp.dot(linv,o_ref[lo:hi,:lo],precision=HI,preferred_element_type=jnp.float32)
-                if q<3:
-                    o_ref[hi:,:hi]=o_ref[hi:,:hi]-lax.dot_general(up,o_ref[lo:hi,:hi],T,precision=HI,preferred_element_type=jnp.float32)
-
-def inverse_factor(g):
-    n=g.shape[0]
-    return pl.pallas_call(kernel,out_shape=jax.ShapeDtypeStruct((n,n),jnp.float32),
-        in_specs=[pl.BlockSpec(memory_space=pltpu.VMEM)],out_specs=pl.BlockSpec(memory_space=pltpu.VMEM),
-        scratch_shapes=[pltpu.VMEM((n,n),jnp.float32),pltpu.VMEM((8,128),jnp.float32),pltpu.VMEM((128,128),jnp.float32)],
-        compiler_params=pltpu.CompilerParams(vmem_limit_bytes=32*2**20),
-        cost_estimate=pl.CostEstimate(flops=300_000_000*6,bytes_accessed=2**21,transcendentals=0))(g)
+
+def vmem(*shape):
+    return jax.ShapeDtypeStruct(shape, F32)
+
+
+VMEM = pl.BlockSpec(memory_space=pltpu.VMEM)
+PARAMS = pltpu.CompilerParams(vmem_limit_bytes=40 * 2**20)
+
+
+def cost(flops, nbytes):
+    return pl.CostEstimate(flops=flops, bytes_accessed=nbytes, transcendentals=0)
+
+
+def factored(a_ref):
+    sub = lax.broadcasted_iota(jnp.int32, S8, 0)
+    lane = lax.broadcasted_iota(jnp.int32, S8, 1)
+    return chol_inv_128([a_ref[8 * k : 8 * k + 8, 0:128] for k in range(16)], sub, lane)
+
+
+def panel_kernel(a_ref, linv_ref, u_ref, next_ref):
+    for k, block in enumerate(factored(a_ref)):
+        linv_ref[8 * k : 8 * k + 8, :] = block
+    u = mm(linv_ref[...], a_ref[:128, 128:])
+    u_ref[...] = u
+    next_ref[...] = a_ref[128:, 128:] - mtm(u, u)
+
+
+def panel(a):
+    n = a.shape[0] - 128
+    return pl.pallas_call(
+        panel_kernel,
+        out_shape=(vmem(128, 128), vmem(128, n), vmem(n, n)),
+        in_specs=[VMEM],
+        out_specs=(VMEM, VMEM, VMEM),
+        compiler_params=PARAMS,
+        cost_estimate=cost(5_000_000_000, 1 << 20),
+        name="panel",
+    )(a)
+
+
+def last_kernel(a_ref, l0, l1, l2, u0, u1, u2, o_ref):
+    o_ref[...] = jnp.zeros_like(o_ref)
+    o_ref[0:128, 0:128] = l0[...]
+    o_ref[128:256, 128:256] = l1[...]
+    o_ref[256:384, 256:384] = l2[...]
+    o_ref[128:256, 0:128] = -mm(l1[...], mtm(u0[:, 0:128], l0[...]))
+    t = mtm(u0[:, 128:256], o_ref[0:128, 0:256]) + mtm(u1[:, 0:128], o_ref[128:256, 0:256])
+    o_ref[256:384, 0:256] = -mm(l2[...], t)
+    t = mtm(u0[:, 256:384], o_ref[0:128, 0:384]) + mtm(u1[:, 128:256], o_ref[128:256, 0:384])
+    t = t + mtm(u2[...], o_ref[256:384, 0:384])
+    for k, block in enumerate(factored(a_ref)):
+        o_ref[384 + 8 * k : 392 + 8 * k, 384:512] = block
+    o_ref[384:512, 0:384] = -mm(o_ref[384:512, 384:512], t)
+
+
+def last_panel(a, linvs, us):
+    return pl.pallas_call(
+        last_kernel,
+        out_shape=vmem(512, 512),
+        in_specs=[VMEM] * 7,
+        out_specs=VMEM,
+        compiler_params=PARAMS,
+        cost_estimate=cost(6_000_000_000, 1 << 20),
+        name="last_panel",
+    )(a, *linvs, *us)
+
+
+def two(x):
+    high = x.astype(jnp.bfloat16)
+    return high, (x - high.astype(F32)).astype(jnp.bfloat16)
+
+
+def product_kernel(core_ref, inverse_ref, *refs):
+    parts, out_ref, lh_ref, ll_ref, buf, sems = refs[:3], *refs[3:]
+    lh_ref[...], ll_ref[...] = two(inverse_ref[...])
+    width = out_ref.shape[1] // 2
+    dot = lambda x, y: jnp.dot(x, y, preferred_element_type=F32)
+    copies = []
+    for s in range(2):
+        at = s * width
+        for part in parts:
+            w = part.shape[-1]
+            xh, xl = two(part[s])
+            for r, n in ((0, 256), (256, 512)):
+                lh, ll = lh_ref[r : r + 256, :n], ll_ref[r : r + 256, :n]
+                y = dot(lh, xh[:n]) + (dot(lh, xl[:n]) + dot(ll, xh[:n]))
+                if at < LEAD:
+                    ids = core_ref[0] * 2 * width + at + lax.broadcasted_iota(jnp.int32, y.shape, 1)
+                    y = jnp.where(ids >= r + lax.broadcasted_iota(jnp.int32, y.shape, 0), y, 0.0)
+                buf[r : r + 256, at : at + w] = y
+            place = (slice(None), pl.ds(at, w))
+            copies.append(pltpu.make_async_copy(buf.at[place], out_ref.at[place], sems.at[len(copies)]))
+            copies[-1].start()
+            at += w
+    for copy in copies:
+        copy.wait()
+
+
+def product(core, inverse, parts):
+    return pl.pallas_call(
+        product_kernel,
+        out_shape=vmem(LEAD, 2048),
+        in_specs=[pl.BlockSpec(memory_space=pltpu.SMEM)] + [VMEM] * 4,
+        out_specs=pl.BlockSpec(memory_space=pl.ANY),
+        scratch_shapes=[
+            pltpu.VMEM((LEAD, LEAD), jnp.bfloat16),
+            pltpu.VMEM((LEAD, LEAD), jnp.bfloat16),
+            pltpu.VMEM((LEAD, 2048), F32),
+            pltpu.SemaphoreType.DMA((6,)),
+        ],
+        compiler_params=PARAMS,
+        cost_estimate=cost(3_000_000_000, 9 << 20),
+        name="product",
+    )(core.reshape(1), inverse, *parts)
 
 
 def flip(link):
@@ -189,7 +286,6 @@
     h = joined(h, swap(h, XP), XP, 1)
     got = across(h)
     g11 = jnp.concatenate([jnp.where(core == 0, h, got), jnp.where(core == 0, got, h)], axis=1)
-    inverse = inverse_factor(g11)
 
     rest = joined(rest, swap(rest, ZM), ZM, 0)
     rest = joined(rest, swap(rest, YM), YM, 0)
@@ -199,15 +295,15 @@
     order = ((XM, YP, ZP), (YP, ZP, XM), (ZP, XM, YP))
     axis_of = lambda part, link: 0 if link == XP else 1 + order[part].index(link)
     parts = [joined(u, v, XM, axis_of(i, XM)) for i, (u, v) in enumerate(zip(cut(rest), cut(got)))]
+    linvs, us, a = [], [], g11
     for step in ((YP, ZP, XP), (ZP, XP, YP), (XP, YP, ZP)):
         gots = [swap(parts[i], step[i]) for i in range(3)]
+        linv, u, a = panel(a)
+        linvs.append(linv)
+        us.append(u)
         parts = [joined(parts[i], gots[i], step[i], axis_of(i, step[i])) for i in range(3)]
-    parts = [x.reshape(2, LEAD, x.shape[-1]) for x in parts]
-    whole = jnp.concatenate([x[s] for s in range(2) for x in parts], axis=1)
-    projected = jnp.dot(inverse, whole, precision=HI)
-    column_ids = core * width + jnp.arange(width, dtype=jnp.int32)
-    keep = column_ids[None, :] >= jnp.arange(LEAD, dtype=jnp.int32)[:, None]
-    return jnp.where(keep, projected, 0.0)
+    inverse = last_panel(a, linvs, us)
+    return product(core, inverse, [x.reshape(2, LEAD, x.shape[-1]) for x in parts])
 
 
 def solution(mesh):

time: 141 us -> 140 us (level)
  matrix products: 10.9 us -> 2.3 us
  Pallas kernels: 20.7 us -> 28.1 us
  starting transfers between devices: 31.4 us -> 37.8 us
  waiting for transfers between devices: 70.2 us -> 64.1 us
    dot_general x1 -> x0, matrix products: 8.58 us -> none  [body(): projected = jnp.dot(inverse, whole, precision=HI)]
    pallas_call x1 -> x5, Pallas kernels: 20.7 us -> 28.1 us  [the longest x3 18.6 us: panel(): pl.pallas_call(panel_kernel, out_shape=(vmem(128, 128), vmem(128, n), vme...]
    ppermute x26, starting transfers between devices: 31.2 us -> 37.7 us  [swap(): return lax.ppermute(x, ('row', 'col'), flip(link))]
    ppermute x26, waiting for transfers between devices: 68.9 us -> 62.7 us  [swap(): return lax.ppermute(x, ('row', 'col'), flip(link))]
  transfers between devices with their start and end apart: 28 -> 28, of which waited for: 23 -> 20; matrix products, arithmetic and copies ran while one was open for 1% -> 1% of each run, Pallas kernels for 15% -> 17%
where the time goes in v2:
time: 140 us
  waiting for transfers between devices  64.1 us (46%)
  starting transfers between devices  37.8 us (27%)
  Pallas kernels  28.1 us (20%)
  other arithmetic  5.24 us (4%)
  matrix products  2.3 us (2%)
  between operations  1.72 us (1%)
    ppermute x26, waiting for transfers between devices, swap(): return lax.ppermute(x, ('row', 'col'), flip(link))  62.7 us
    ppermute x26, starting transfers between devices, swap(): return lax.ppermute(x, ('row', 'col'), flip(link))  37.7 us
    pallas_call x3, Pallas kernels, panel(): pl.pallas_call(panel_kernel, out_shape=(vmem(128, 128), vmem(128, n), vme...  18.6 us
    pallas_call x1, Pallas kernels, last_panel(): pl.pallas_call(last_kernel, out_shape=vmem(512, 512), in_specs=[VMEM] * 7...  5.3 us
    pallas_call x1, Pallas kernels, product(): pl.pallas_call(product_kernel, out_shape=vmem(LEAD, 2048), in_specs=[pl.B...  4.23 us
  transfers between devices with their start and end apart: 28, of which 20 were waited for; matrix products, arithmetic and copies ran while one was open for 1% of the time, Pallas kernels for 17%

profile of v2, /device:TPU:0, one launch (start us, length us, event | category | flops | bytes accessed | tf_op | source)
XLA Modules:
  0.0 139.5 jit_solution(7843131883916356537)
XLA Ops:
  0.7 1.4 select_bitcast_fusion
  2.1 0.1 collective-permute-start
  2.2 0.1 slice_select_fusion
  2.3 1.4 collective-permute-done
  3.8 1.7 %collective-permute-start.1 = (f32[128,1536]{1,0:T(8,128)S(1)}, f32[128,1536]{1,0:T(8,128)S(1)}, u32[]{:S(2)}, u32[]{:S(2)}) collective-permute-start(f32[128,1536]{1,0:T(8,128)S(1)} %pad_maximum_fusion.4), channel_id=1, source_target_pairs={{0,2},{1,7},{2,0},{3,5},{4,6},{5,3},{6,4},{7,1},{8,10},{9,15},{10,... | collective-permute-start | bytes 2359304 | tf_op jit(solution)/shard_map/ppermute | solution.py:218
  5.4 10.4 %collective-permute-done.1 = f32[128,1536]{1,0:T(8,128)S(1)} collective-permute-done((f32[128,1536]{1,0:T(8,128)S(1)}, f32[128,1536]{1,0:T(8,128)S(1)}, u32[]{:S(2)}, u32[]{:S(2)}) %collective-permute-start.1) | collective-permute-done | bytes 786464 | tf_op jit(solution)/shard_map/ppermute | solution.py:218
  15.9 2.3 %fusion = f32[512,1152]{1,0:T(8,128)S(1)} fusion(f32[256,128]{1,0:T(8,128)S(1)} %fusion.6, f32[128,1024]{1,0:T(8,128)S(1)} %slice.110, f32[128,1024]{1,0:T(8,128)S(1)} %get-tuple-element.37, f32[128,512]{1,0:T(8,128)S(1)} %slice.109, f32[128,512]{1,0:T(8,128)S(1)} %broadcast_select_fusion.14), kind=kOutput, calls=%fused_computation.2 | convolution fusion | flops 1812660224 | bytes 4063232 | tf_op jit(solution)/shard_map/rp,rc->pc/dot_general | solution.py:251
  18.3 0.1 slice_select_fusion.3
  18.4 2.9 %collective-permute-start.5 = (f32[256,384]{1,0:T(8,128)S(1)}, f32[256,384]{1,0:T(8,128)}, u32[]{:S(2)}, u32[]{:S(2)}) collective-permute-start(f32[256,384]{1,0:T(8,128)S(1)} %get-tuple-element.26), channel_id=1, source_target_pairs={{0,6},{1,3},{2,4},{3,1},{4,2},{5,7},{6,0},{7,5},{8,14},{9,11},{10,... | collective-permute-start | bytes 1179656 | tf_op jit(solution)/shard_map/ppermute | solution.py:218
  21.3 1.6 %collective-permute-start.8 = (f32[256,384]{1,0:T(8,128)S(1)}, f32[256,384]{1,0:T(8,128)}, u32[]{:S(2)}, u32[]{:S(2)}) collective-permute-start(f32[256,384]{1,0:T(8,128)S(1)} %get-tuple-element.27), channel_id=1, source_target_pairs={{0,8},{1,25},{2,10},{3,27},{4,12},{5,29},{6,14},{7,31},{8,0},{9,17... | collective-permute-start | bytes 1179656 | tf_op jit(solution)/shard_map/ppermute | solution.py:218
  22.9 1.9 %collective-permute-start.2 = (f32[256,384]{1,0:T(8,128)S(1)}, f32[256,384]{1,0:T(8,128)}, u32[]{:S(2)}, u32[]{:S(2)}) collective-permute-start(f32[256,384]{1,0:T(8,128)S(1)} %get-tuple-element.28), channel_id=1, source_target_pairs={{0,32},{1,97},{2,34},{3,99},{4,36},{5,101},{6,38},{7,103},{8,40},{... | collective-permute-start | bytes 1179656 | tf_op jit(solution)/shard_map/ppermute | solution.py:218
  24.8 2.8 %collective-permute-done.5 = f32[256,384]{1,0:T(8,128)} collective-permute-done((f32[256,384]{1,0:T(8,128)S(1)}, f32[256,384]{1,0:T(8,128)}, u32[]{:S(2)}, u32[]{:S(2)}) %collective-permute-start.5) | collective-permute-done | bytes 393248 | tf_op jit(solution)/shard_map/ppermute | solution.py:218
  27.6 1.6 %collective-permute-done.8 = f32[256,384]{1,0:T(8,128)} collective-permute-done((f32[256,384]{1,0:T(8,128)S(1)}, f32[256,384]{1,0:T(8,128)}, u32[]{:S(2)}, u32[]{:S(2)}) %collective-permute-start.8) | collective-permute-done | bytes 393248 | tf_op jit(solution)/shard_map/ppermute | solution.py:218
  29.2 1.6 %collective-permute-done.2 = f32[256,384]{1,0:T(8,128)} collective-permute-done((f32[256,384]{1,0:T(8,128)S(1)}, f32[256,384]{1,0:T(8,128)}, u32[]{:S(2)}, u32[]{:S(2)}) %collective-permute-start.2) | collective-permute-done | bytes 393248 | tf_op jit(solution)/shard_map/ppermute | solution.py:218
  30.8 1.4 %select_add_fusion.1 = (f32[256,384]{1,0:T(8,128)S(1)}, f32[256,384]{1,0:T(8,128)S(1)}, f32[256,384]{1,0:T(8,128)S(1)}) fusion(f32[256,384]{1,0:T(8,128)} %collective-permute-done.5, f32[512,1152]{1,0:T(8,128)S(1)} %fusion, pred[]{:T(512)S(6)} %eq.54, f32[256,384]{1,0:T(8,128)} %collective-permute-done.8, pred[]{:T(512)S(6)} %eq.55, ...), kind=kLoop, calls=%fused_computation.31 | loop fusion | flops 589824 | bytes 4718595 | tf_op jit(solution)/shard_map/add | solution.py:258
  32.3 2.0 %collective-permute-start.9 = (f32[128,384]{1,0:T(8,128)S(1)}, f32[128,384]{1,0:T(8,128)S(1)}, u32[]{:S(2)}, u32[]{:S(2)}) collective-permute-start(f32[128,384]{1,0:T(8,128)S(1)} %slice_select_fusion.5), channel_id=1, source_target_pairs={{0,32},{1,97},{2,34},{3,99},{4,36},{5,101},{6,38},{7,103},{8,40},{... | collective-permute-start | bytes 589832 | tf_op jit(solution)/shard_map/ppermute | solution.py:218
  34.3 0.5 collective-permute-start.6
  34.8 0.8 collective-permute-start.3
  35.7 2.3 %collective-permute-done.9 = f32[128,384]{1,0:T(8,128)S(1)} collective-permute-done((f32[128,384]{1,0:T(8,128)S(1)}, f32[128,384]{1,0:T(8,128)S(1)}, u32[]{:S(2)}, u32[]{:S(2)}) %collective-permute-start.9) | collective-permute-done | bytes 196640 | tf_op jit(solution)/shard_map/ppermute | solution.py:218
  38.1 0.6 collective-permute-start.10
  38.6 1.4 collective-permute-done.6
  40.1 0.6 collective-permute-start.7
  40.7 1.8 %collective-permute-done.3 = f32[128,512]{1,0:T(8,128)S(1)} collective-permute-done((f32[128,512]{1,0:T(8,128)S(1)}, f32[128,512]{1,0:T(8,128)S(1)}, u32[]{:S(2)}, u32[]{:S(2)}) %collective-permute-start.3) | collective-permute-done | bytes 262176 | tf_op jit(solution)/shard_map/ppermute | solution.py:218
  42.6 1.7 %collective-permute-start.4 = (f32[64,768]{1,0:T(8,128)S(1)}, f32[64,768]{1,0:T(8,128)S(1)}, u32[]{:S(2)}, u32[]{:S(2)}) collective-permute-start(f32[64,768]{1,0:T(8,128)S(1)} %constant_dynamic-update-slice_fusion), channel_id=1, source_target_pairs={{0,8},{1,25},{2,10},{3,27},{4,12},{5,29},{6,14},{7,31},{8,0},{9,17... | collective-permute-start | bytes 589832 | tf_op jit(solution)/shard_map/ppermute | solution.py:218
  44.3 0.5 collective-permute-done.7
  44.8 3.6 %collective-permute-done.4 = f32[64,768]{1,0:T(8,128)S(1)} collective-permute-done((f32[64,768]{1,0:T(8,128)S(1)}, f32[64,768]{1,0:T(8,128)S(1)}, u32[]{:S(2)}, u32[]{:S(2)}) %collective-permute-start.4) | collective-permute-done | bytes 196640 | tf_op jit(solution)/shard_map/ppermute | solution.py:218
  48.6 3.1 %collective-permute-start.11 = (f32[64,1024]{1,0:T(8,128)S(1)}, f32[64,1024]{1,0:T(8,128)S(1)}, u32[]{:S(2)}, u32[]{:S(2)}) collective-permute-start(f32[64,1024]{1,0:T(8,128)S(1)} %pad_maximum_fusion.16), channel_id=1, source_target_pairs={{0,24},{1,9},{2,26},{3,11},{4,28},{5,13},{6,30},{7,15},{8,16},{9,1... | collective-permute-start | bytes 786440 | tf_op jit(solution)/shard_map/ppermute | solution.py:218
  51.7 4.6 %collective-permute-done.11 = f32[64,1024]{1,0:T(8,128)S(1)} collective-permute-done((f32[64,1024]{1,0:T(8,128)S(1)}, f32[64,1024]{1,0:T(8,128)S(1)}, u32[]{:S(2)}, u32[]{:S(2)}) %collective-permute-start.11) | collective-permute-done | bytes 262176 | tf_op jit(solution)/shard_map/ppermute | solution.py:218
  56.5 2.8 %collective-permute-start.12 = (f32[48,1024]{1,0:T(8,128)S(1)}, f32[48,1024]{1,0:T(8,128)S(1)}, u32[]{:S(2)}, u32[]{:S(2)}) collective-permute-start(f32[48,1024]{1,0:T(8,128)S(1)} %pad_maximum_fusion.19), channel_id=1, source_target_pairs={{0,96},{1,33},{2,98},{3,35},{4,100},{5,37},{6,102},{7,39},{8,104},... | collective-permute-start | bytes 589832 | tf_op jit(solution)/shard_map/ppermute | solution.py:218
  59.4 4.6 %collective-permute-done.12 = f32[48,1024]{1,0:T(8,128)S(1)} collective-permute-done((f32[48,1024]{1,0:T(8,128)S(1)}, f32[48,1024]{1,0:T(8,128)S(1)}, u32[]{:S(2)}, u32[]{:S(2)}) %collective-permute-start.12) | collective-permute-done | bytes 196640 | tf_op jit(solution)/shard_map/ppermute | solution.py:218
  63.9 3.7 %collective-permute-start.16 = (f32[16,1024]{1,0:T(8,128)S(1)}, f32[16,1024]{1,0:T(8,128)S(1)}, u32[]{:S(2)}, u32[]{:S(2)}) collective-permute-start(f32[16,1024]{1,0:T(8,128)S(1)} %slice_add_fusion.3), channel_id=1, source_target_pairs={{0,96},{1,33},{2,98},{3,35},{4,100},{5,37},{6,102},{7,39},{8,104},... | collective-permute-start | bytes 196616 | tf_op jit(solution)/shard_map/ppermute | solution.py:218
  67.7 0.7 collective-permute-start.13
  68.4 1.4 %collective-permute-done.16 = f32[16,1024]{1,0:T(8,128)S(1)} collective-permute-done((f32[16,1024]{1,0:T(8,128)S(1)}, f32[16,1024]{1,0:T(8,128)S(1)}, u32[]{:S(2)}, u32[]{:S(2)}) %collective-permute-start.16) | collective-permute-done | bytes 65568 | tf_op jit(solution)/shard_map/ppermute | solution.py:218
  69.9 3.5 %collective-permute-start.17 = (f32[32,1024]{1,0:T(8,128)S(1)}, f32[32,1024]{1,0:T(8,128)S(1)}, u32[]{:S(2)}, u32[]{:S(2)}) collective-permute-start(f32[32,1024]{1,0:T(8,128)S(1)} %pad_maximum_fusion.22), channel_id=1, source_target_pairs={{0,24},{1,9},{2,26},{3,11},{4,28},{5,13},{6,30},{7,15},{8,16},{9,1... | collective-permute-start | bytes 393224 | tf_op jit(solution)/shard_map/ppermute | solution.py:218
  73.5 0.1 collective-permute-start.14
  73.5 2.8 %collective-permute-done.17 = f32[32,1024]{1,0:T(8,128)S(1)} collective-permute-done((f32[32,1024]{1,0:T(8,128)S(1)}, f32[32,1024]{1,0:T(8,128)S(1)}, u32[]{:S(2)}, u32[]{:S(2)}) %collective-permute-start.17) | collective-permute-done | bytes 131104 | tf_op jit(solution)/shard_map/ppermute | solution.py:218
  76.4 0.1 collective-permute-start.18
  76.5 3.4 %collective-permute-done.14 = f32[512,128]{1,0:T(8,128)S(1)} collective-permute-done((f32[512,128]{1,0:T(8,128)S(1)}, f32[512,128]{1,0:T(8,128)S(1)}, u32[]{:S(2)}, u32[]{:S(2)}) %collective-permute-start.14) | collective-permute-done | bytes 262176 | tf_op jit(solution)/shard_map/ppermute | solution.py:218
  80.0 0.1 collective-permute-start.15
  80.1 4.0 %collective-permute-done.18 = f32[64,1024]{1,0:T(8,128)S(1)} collective-permute-done((f32[64,1024]{1,0:T(8,128)S(1)}, f32[64,1024]{1,0:T(8,128)S(1)}, u32[]{:S(2)}, u32[]{:S(2)}) %collective-permute-start.18) | collective-permute-done | bytes 262176 | tf_op jit(solution)/shard_map/ppermute | solution.py:218
  84.1 0.1 collective-permute-start.25
  84.3 0.1 collective-permute-start.19
  84.4 2.2 %collective-permute-start.22 = (f32[1,1,1,2,64,384]{5,4,3,2,1,0:T(8,128)S(1)}, f32[1,1,1,2,64,384]{5,4,3,2,1,0:T(8,128)S(1)}, u32[]{:S(2)}, u32[]{:S(2)}) collective-permute-start(f32[1,1,1,2,64,384]{5,4,3,2,1,0:T(8,128)S(1)} %pad_maximum_fusion.21), channel_id=1, source_target_pairs={{0,32},{1,97},{2,34},{3,99},{4,36},{5,101},{6,38},{7,103},{8,40},{... | collective-permute-start | bytes 589832 | tf_op jit(solution)/shard_map/ppermute | solution.py:218
  86.6 2.5 %collective-permute-done.25 = f32[1,1,2,1,64,256]{5,4,3,2,1,0:T(8,128)S(1)} collective-permute-done((f32[1,1,2,1,64,256]{5,4,3,2,1,0:T(8,128)S(1)}, f32[1,1,2,1,64,256]{5,4,3,2,1,0:T(8,128)S(1)}, u32[]{:S(2)}, u32[]{:S(2)}) %collective-permute-start.25) | collective-permute-done | bytes 131104 | tf_op jit(solution)/shard_map/ppermute | solution.py:218
  89.2 0.1 collective-permute-start.26
  89.3 0.7 collective-permute-done.19
  90.1 2.2 %collective-permute-start.20 = (f32[1,2,2,1,64,384]{5,4,3,2,1,0:T(8,128)S(1)}, f32[1,2,2,1,64,384]{5,4,3,2,1,0:T(8,128)S(1)}, u32[]{:S(2)}, u32[]{:S(2)}) collective-permute-start(f32[1,2,2,1,64,384]{5,4,3,2,1,0:T(8,128)S(1)} %pad_maximum_fusion.12), channel_id=1, source_target_pairs={{0,32},{1,97},{2,34},{3,99},{4,36},{5,101},{6,38},{7,103},{8,40},{... | collective-permute-start | bytes 1179656 | tf_op jit(solution)/shard_map/ppermute | solution.py:218
  92.4 2.1 %collective-permute-start.23 = (f32[1,1,2,2,64,384]{5,4,3,2,1,0:T(8,128)S(1)}, f32[1,1,2,2,64,384]{5,4,3,2,1,0:T(8,128)S(1)}, u32[]{:S(2)}, u32[]{:S(2)}) collective-permute-start(f32[1,1,2,2,64,384]{5,4,3,2,1,0:T(8,128)S(1)} %pad_maximum_fusion.13), channel_id=1, source_target_pairs={{0,2},{1,7},{2,0},{3,5},{4,6},{5,3},{6,4},{7,1},{8,10},{9,15},{10,... | collective-permute-start | bytes 1179656 | tf_op jit(solution)/shard_map/ppermute | solution.py:218
  94.5 1.2 collective-permute-done.26
  95.7 2.4 %collective-permute-start.27 = (f32[2,1,2,2,64,256]{5,4,3,2,1,0:T(8,128)S(1)}, f32[2,1,2,2,64,256]{5,4,3,2,1,0:T(8,128)S(1)}, u32[]{:S(2)}, u32[]{:S(2)}) collective-permute-start(f32[2,1,2,2,64,256]{5,4,3,2,1,0:T(8,128)S(1)} %pad_maximum_fusion.10), channel_id=1, source_target_pairs={{0,32},{1,97},{2,34},{3,99},{4,36},{5,101},{6,38},{7,103},{8,40},{... | collective-permute-start | bytes 1572872 | tf_op jit(solution)/shard_map/ppermute | solution.py:218
  98.2 0.1 broadcast_select_fusion.7
  98.2 0.1 pad_maximum_fusion.2.a_ref
  98.4 6.5 %panel.3 = (f32[128,128]{1,0:T(8,128)S(1)}, f32[128,384]{1,0:T(8,128)S(1)}, f32[384,384]{1,0:T(8,128)S(1)}) custom-call(f32[512,512]{1,0:T(8,128)S(1)} %pad_maximum_fusion.2.a_ref), custom_call_target="tpu_custom_call" | custom-call | flops 5000000000 | bytes 1048576 | tf_op jit(solution)/shard_map/panel/pallas_call | solution.py:103
  104.9 6.2 %panel.4 = (f32[128,128]{1,0:T(8,128)S(1)}, f32[128,256]{1,0:T(8,128)S(1)}, f32[256,256]{1,0:T(8,128)S(1)}) custom-call(f32[384,384]{1,0:T(8,128)S(1)} %get-tuple-element.14.a_ref), custom_call_target="tpu_custom_call" | custom-call | flops 5000000000 | bytes 1048576 | tf_op jit(solution)/shard_map/panel/pallas_call | solution.py:103
  111.1 5.9 %panel.5 = (f32[128,128]{1,0:T(8,128)S(1)}, f32[128,128]{1,0:T(8,128)S(1)}, f32[128,128]{1,0:T(8,128)S(1)}) custom-call(f32[256,256]{1,0:T(8,128)S(1)} %get-tuple-element.15.a_ref), custom_call_target="tpu_custom_call" | custom-call | flops 5000000000 | bytes 1048576 | tf_op jit(solution)/shard_map/panel/pallas_call | solution.py:103
  117.0 5.3 %last_panel.1.inverse_ref = f32[512,512]{1,0:T(8,128)S(1)} custom-call(f32[128,128]{1,0:T(8,128)S(1)} %get-tuple-element.16.a_ref, f32[128,128]{1,0:T(8,128)S(1)} %get-tuple-element.17.l0, f32[128,128]{1,0:T(8,128)S(1)} %get-tuple-element.18.l1, f32[128,128]{1,0:T(8,128)S(1)} %get-tuple-element.19.l2, f32[128,384]{1,0:T(8,128)S(1)} %get-tuple-element.20.u0, ...), custom_call_target="tpu_custom_call" | custom-call | flops 6000000000 | bytes 1048576 | tf_op jit(solution)/shard_map/last_panel/pallas_call | solution.py:130
  122.5 0.1 collective-permute-start.21
  122.7 0.1 collective-permute-start.24
  123.0 11.6 %collective-permute-done.21 = f32[1,2,2,2,64,384]{5,4,3,2,1,0:T(8,128)S(1)} collective-permute-done((f32[1,2,2,2,64,384]{5,4,3,2,1,0:T(8,128)S(1)}, f32[1,2,2,2,64,384]{5,4,3,2,1,0:T(8,128)S(1)}, u32[]{:S(2)}, u32[]{:S(2)}) %collective-permute-start.21) | collective-permute-done | bytes 786464 | tf_op jit(solution)/shard_map/ppermute | solution.py:218
  134.5 0.1 broadcast_select_fusion.3
  134.7 0.2 pad_maximum_fusion
  134.8 0.2 broadcast_select_fusion.1
  135.0 0.1 pad_maximum_fusion.1
  135.1 4.2 %product.1 = f32[512,2048]{1,0:T(8,128)} custom-call(s32[1]{0:T(128)} %bitcast.core_ref, f32[512,512]{1,0:T(8,128)S(1)} %last_panel.1.inverse_ref, f32[2,512,384]{2,1,0:T(8,128)S(1)} %bitcast.20, f32[2,512,384]{2,1,0:T(8,128)S(1)} %bitcast.21, f32[2,512,256]{2,1,0:T(8,128)S(1)} %bitcast.22), custom_call_target="tpu_custom_call" | custom-call | flops 3000000000 | bytes 9437184 | tf_op jit(solution)/shard_map/product/pallas_call | solution.py:173
  (105 shorter events, 1.7 us)
Async XLA Ops:
  2.1 1.6 %collective-permute-start = (f32[128,512]{1,0:T(8,128)S(1)}, f32[128,512]{1,0:T(8,128)S(1)}, u32[]{:S(2)}, u32[]{:S(2)}) collective-permute-start(f32[128,512]{1,0:T(8,128)S(1)} %slice.106), channel_id=1, source_target_pairs={{0,1},{1,0},{2,3},{3,2},{4,5},{5,4},{6,7},{7,6},{8,9},{9,8},{10,11... | collective-permute-start | bytes 786440 | tf_op jit(solution)/shard_map/ppermute | solution.py:221
  3.8 12.1 %collective-permute-start.1 = (f32[128,1536]{1,0:T(8,128)S(1)}, f32[128,1536]{1,0:T(8,128)S(1)}, u32[]{:S(2)}, u32[]{:S(2)}) collective-permute-start(f32[128,1536]{1,0:T(8,128)S(1)} %pad_maximum_fusion.4), channel_id=1, source_target_pairs={{0,2},{1,7},{2,0},{3,5},{4,6},{5,3},{6,4},{7,1},{8,10},{9,15},{10,... | collective-permute-start | bytes 2359304 | tf_op jit(solution)/shard_map/ppermute | solution.py:218
  18.4 9.2 %collective-permute-start.5 = (f32[256,384]{1,0:T(8,128)S(1)}, f32[256,384]{1,0:T(8,128)}, u32[]{:S(2)}, u32[]{:S(2)}) collective-permute-start(f32[256,384]{1,0:T(8,128)S(1)} %get-tuple-element.26), channel_id=1, source_target_pairs={{0,6},{1,3},{2,4},{3,1},{4,2},{5,7},{6,0},{7,5},{8,14},{9,11},{10,... | collective-permute-start | bytes 1179656 | tf_op jit(solution)/shard_map/ppermute | solution.py:218
  21.3 7.9 %collective-permute-start.8 = (f32[256,384]{1,0:T(8,128)S(1)}, f32[256,384]{1,0:T(8,128)}, u32[]{:S(2)}, u32[]{:S(2)}) collective-permute-start(f32[256,384]{1,0:T(8,128)S(1)} %get-tuple-element.27), channel_id=1, source_target_pairs={{0,8},{1,25},{2,10},{3,27},{4,12},{5,29},{6,14},{7,31},{8,0},{9,17... | collective-permute-start | bytes 1179656 | tf_op jit(solution)/shard_map/ppermute | solution.py:218
  22.9 7.9 %collective-permute-start.2 = (f32[256,384]{1,0:T(8,128)S(1)}, f32[256,384]{1,0:T(8,128)}, u32[]{:S(2)}, u32[]{:S(2)}) collective-permute-start(f32[256,384]{1,0:T(8,128)S(1)} %get-tuple-element.28), channel_id=1, source_target_pairs={{0,32},{1,97},{2,34},{3,99},{4,36},{5,101},{6,38},{7,103},{8,40},{... | collective-permute-start | bytes 1179656 | tf_op jit(solution)/shard_map/ppermute | solution.py:218
  32.3 5.8 %collective-permute-start.9 = (f32[128,384]{1,0:T(8,128)S(1)}, f32[128,384]{1,0:T(8,128)S(1)}, u32[]{:S(2)}, u32[]{:S(2)}) collective-permute-start(f32[128,384]{1,0:T(8,128)S(1)} %slice_select_fusion.5), channel_id=1, source_target_pairs={{0,32},{1,97},{2,34},{3,99},{4,36},{5,101},{6,38},{7,103},{8,40},{... | collective-permute-start | bytes 589832 | tf_op jit(solution)/shard_map/ppermute | solution.py:218
  34.3 5.7 %collective-permute-start.6 = (f32[128,384]{1,0:T(8,128)S(1)}, f32[128,384]{1,0:T(8,128)S(1)}, u32[]{:S(2)}, u32[]{:S(2)}) collective-permute-start(f32[128,384]{1,0:T(8,128)S(1)} %slice_select_fusion.6), channel_id=1, source_target_pairs={{0,8},{1,25},{2,10},{3,27},{4,12},{5,29},{6,14},{7,31},{8,0},{9,17... | collective-permute-start | bytes 589832 | tf_op jit(solution)/shard_map/ppermute | solution.py:218
  34.8 7.7 %collective-permute-start.3 = (f32[128,512]{1,0:T(8,128)S(1)}, f32[128,512]{1,0:T(8,128)S(1)}, u32[]{:S(2)}, u32[]{:S(2)}) collective-permute-start(f32[128,512]{1,0:T(8,128)S(1)} %pad_maximum_fusion.14), channel_id=1, source_target_pairs={{0,6},{1,3},{2,4},{3,1},{4,2},{5,7},{6,0},{7,5},{8,14},{9,11},{10,... | collective-permute-start | bytes 786440 | tf_op jit(solution)/shard_map/ppermute | solution.py:218
  38.1 6.2 %collective-permute-start.10 = (f32[64,384]{1,0:T(8,128)S(1)}, f32[64,384]{1,0:T(8,128)S(1)}, u32[]{:S(2)}, u32[]{:S(2)}) collective-permute-start(f32[64,384]{1,0:T(8,128)S(1)} %slice_select_fusion.9), channel_id=1, source_target_pairs={{0,6},{1,3},{2,4},{3,1},{4,2},{5,7},{6,0},{7,5},{8,14},{9,11},{10,... | collective-permute-start | bytes 294920 | tf_op jit(solution)/shard_map/ppermute | solution.py:218
  40.1 4.7 %collective-permute-start.7 = (f32[64,384]{1,0:T(8,128)S(1)}, f32[64,384]{1,0:T(8,128)S(1)}, u32[]{:S(2)}, u32[]{:S(2)}) collective-permute-start(f32[64,384]{1,0:T(8,128)S(1)} %slice_select_fusion.10), channel_id=1, source_target_pairs={{0,32},{1,97},{2,34},{3,99},{4,36},{5,101},{6,38},{7,103},{8,40},{... | collective-permute-start | bytes 294920 | tf_op jit(solution)/shard_map/ppermute | solution.py:218
  42.6 5.7 %collective-permute-start.4 = (f32[64,768]{1,0:T(8,128)S(1)}, f32[64,768]{1,0:T(8,128)S(1)}, u32[]{:S(2)}, u32[]{:S(2)}) collective-permute-start(f32[64,768]{1,0:T(8,128)S(1)} %constant_dynamic-update-slice_fusion), channel_id=1, source_target_pairs={{0,8},{1,25},{2,10},{3,27},{4,12},{5,29},{6,14},{7,31},{8,0},{9,17... | collective-permute-start | bytes 589832 | tf_op jit(solution)/shard_map/ppermute | solution.py:218
  48.6 7.7 %collective-permute-start.11 = (f32[64,1024]{1,0:T(8,128)S(1)}, f32[64,1024]{1,0:T(8,128)S(1)}, u32[]{:S(2)}, u32[]{:S(2)}) collective-permute-start(f32[64,1024]{1,0:T(8,128)S(1)} %pad_maximum_fusion.16), channel_id=1, source_target_pairs={{0,24},{1,9},{2,26},{3,11},{4,28},{5,13},{6,30},{7,15},{8,16},{9,1... | collective-permute-start | bytes 786440 | tf_op jit(solution)/shard_map/ppermute | solution.py:218
  56.5 7.4 %collective-permute-start.12 = (f32[48,1024]{1,0:T(8,128)S(1)}, f32[48,1024]{1,0:T(8,128)S(1)}, u32[]{:S(2)}, u32[]{:S(2)}) collective-permute-start(f32[48,1024]{1,0:T(8,128)S(1)} %pad_maximum_fusion.19), channel_id=1, source_target_pairs={{0,96},{1,33},{2,98},{3,35},{4,100},{5,37},{6,102},{7,39},{8,104},... | collective-permute-start | bytes 589832 | tf_op jit(solution)/shard_map/ppermute | solution.py:218
  63.9 5.9 %collective-permute-start.16 = (f32[16,1024]{1,0:T(8,128)S(1)}, f32[16,1024]{1,0:T(8,128)S(1)}, u32[]{:S(2)}, u32[]{:S(2)}) collective-permute-start(f32[16,1024]{1,0:T(8,128)S(1)} %slice_add_fusion.3), channel_id=1, source_target_pairs={{0,96},{1,33},{2,98},{3,35},{4,100},{5,37},{6,102},{7,39},{8,104},... | collective-permute-start | bytes 196616 | tf_op jit(solution)/shard_map/ppermute | solution.py:218
  67.7 5.7 %collective-permute-start.13 = (f32[256,128]{1,0:T(8,128)S(1)}, f32[256,128]{1,0:T(8,128)S(1)}, u32[]{:S(2)}, u32[]{:S(2)}) collective-permute-start(f32[256,128]{1,0:T(8,128)S(1)} %add.117), channel_id=1, source_target_pairs={{0,32},{1,97},{2,34},{3,99},{4,36},{5,101},{6,38},{7,103},{8,40},{... | collective-permute-start | bytes 393224 | tf_op jit(solution)/shard_map/ppermute | solution.py:218
  69.9 6.5 %collective-permute-start.17 = (f32[32,1024]{1,0:T(8,128)S(1)}, f32[32,1024]{1,0:T(8,128)S(1)}, u32[]{:S(2)}, u32[]{:S(2)}) collective-permute-start(f32[32,1024]{1,0:T(8,128)S(1)} %pad_maximum_fusion.22), channel_id=1, source_target_pairs={{0,24},{1,9},{2,26},{3,11},{4,28},{5,13},{6,30},{7,15},{8,16},{9,1... | collective-permute-start | bytes 393224 | tf_op jit(solution)/shard_map/ppermute | solution.py:218
  73.5 6.5 %collective-permute-start.14 = (f32[512,128]{1,0:T(8,128)S(1)}, f32[512,128]{1,0:T(8,128)S(1)}, u32[]{:S(2)}, u32[]{:S(2)}) collective-permute-start(f32[512,128]{1,0:T(8,128)S(1)} %pad_maximum_fusion.17), channel_id=1, source_target_pairs={{0,2},{1,7},{2,0},{3,5},{4,6},{5,3},{6,4},{7,1},{8,10},{9,15},{10,... | collective-permute-start | bytes 786440 | tf_op jit(solution)/shard_map/ppermute | solution.py:218
  76.4 7.7 %collective-permute-start.18 = (f32[64,1024]{1,0:T(8,128)S(1)}, f32[64,1024]{1,0:T(8,128)S(1)}, u32[]{:S(2)}, u32[]{:S(2)}) collective-permute-start(f32[64,1024]{1,0:T(8,128)S(1)} %pad_maximum_fusion.11), channel_id=1, source_target_pairs={{0,6},{1,3},{2,4},{3,1},{4,2},{5,7},{6,0},{7,5},{8,14},{9,11},{10,... | collective-permute-start | bytes 786440 | tf_op jit(solution)/shard_map/ppermute | solution.py:218
  80.0 18.2 %collective-permute-start.15 = (f32[512,256]{1,0:T(8,128)S(1)}, f32[512,256]{1,0:T(8,128)S(1)}, u32[]{:S(2)}, u32[]{:S(2)}) collective-permute-start(f32[512,256]{1,0:T(8,128)S(1)} %pad_maximum_fusion.9), channel_id=1, source_target_pairs={{0,1},{1,0},{2,3},{3,2},{4,5},{5,4},{6,7},{7,6},{8,9},{9,8},{10,11... | collective-permute-start | bytes 1572872 | tf_op jit(solution)/shard_map/ppermute | solution.py:221
  84.1 5.0 %collective-permute-start.25 = (f32[1,1,2,1,64,256]{5,4,3,2,1,0:T(8,128)S(1)}, f32[1,1,2,1,64,256]{5,4,3,2,1,0:T(8,128)S(1)}, u32[]{:S(2)}, u32[]{:S(2)}) collective-permute-start(f32[1,1,2,1,64,256]{5,4,3,2,1,0:T(8,128)S(1)} %pad_maximum_fusion.23), channel_id=1, source_target_pairs={{0,2},{1,7},{2,0},{3,5},{4,6},{5,3},{6,4},{7,1},{8,10},{9,15},{10,... | collective-permute-start | bytes 393224 | tf_op jit(solution)/shard_map/ppermute | solution.py:218
  84.3 5.7 %collective-permute-start.19 = (f32[1,2,1,1,64,384]{5,4,3,2,1,0:T(8,128)S(1)}, f32[1,2,1,1,64,384]{5,4,3,2,1,0:T(8,128)S(1)}, u32[]{:S(2)}, u32[]{:S(2)}) collective-permute-start(f32[1,2,1,1,64,384]{5,4,3,2,1,0:T(8,128)S(1)} %pad_maximum_fusion.20), channel_id=1, source_target_pairs={{0,8},{1,25},{2,10},{3,27},{4,12},{5,29},{6,14},{7,31},{8,0},{9,17... | collective-permute-start | bytes 589832 | tf_op jit(solution)/shard_map/ppermute | solution.py:218
  84.4 7.9 %collective-permute-start.22 = (f32[1,1,1,2,64,384]{5,4,3,2,1,0:T(8,128)S(1)}, f32[1,1,1,2,64,384]{5,4,3,2,1,0:T(8,128)S(1)}, u32[]{:S(2)}, u32[]{:S(2)}) collective-permute-start(f32[1,1,1,2,64,384]{5,4,3,2,1,0:T(8,128)S(1)} %pad_maximum_fusion.21), channel_id=1, source_target_pairs={{0,32},{1,97},{2,34},{3,99},{4,36},{5,101},{6,38},{7,103},{8,40},{... | collective-permute-start | bytes 589832 | tf_op jit(solution)/shard_map/ppermute | solution.py:218
  89.2 6.5 %collective-permute-start.26 = (f32[2,1,2,1,64,256]{5,4,3,2,1,0:T(8,128)S(1)}, f32[2,1,2,1,64,256]{5,4,3,2,1,0:T(8,128)S(1)}, u32[]{:S(2)}, u32[]{:S(2)}) collective-permute-start(f32[2,1,2,1,64,256]{5,4,3,2,1,0:T(8,128)S(1)} %pad_maximum_fusion.18), channel_id=1, source_target_pairs={{0,8},{1,25},{2,10},{3,27},{4,12},{5,29},{6,14},{7,31},{8,0},{9,17... | collective-permute-start | bytes 786440 | tf_op jit(solution)/shard_map/ppermute | solution.py:218
  90.1 32.3 %collective-permute-start.20 = (f32[1,2,2,1,64,384]{5,4,3,2,1,0:T(8,128)S(1)}, f32[1,2,2,1,64,384]{5,4,3,2,1,0:T(8,128)S(1)}, u32[]{:S(2)}, u32[]{:S(2)}) collective-permute-start(f32[1,2,2,1,64,384]{5,4,3,2,1,0:T(8,128)S(1)} %pad_maximum_fusion.12), channel_id=1, source_target_pairs={{0,32},{1,97},{2,34},{3,99},{4,36},{5,101},{6,38},{7,103},{8,40},{... | collective-permute-start | bytes 1179656 | tf_op jit(solution)/shard_map/ppermute | solution.py:218
  92.4 30.2 %collective-permute-start.23 = (f32[1,1,2,2,64,384]{5,4,3,2,1,0:T(8,128)S(1)}, f32[1,1,2,2,64,384]{5,4,3,2,1,0:T(8,128)S(1)}, u32[]{:S(2)}, u32[]{:S(2)}) collective-permute-start(f32[1,1,2,2,64,384]{5,4,3,2,1,0:T(8,128)S(1)} %pad_maximum_fusion.13), channel_id=1, source_target_pairs={{0,2},{1,7},{2,0},{3,5},{4,6},{5,3},{6,4},{7,1},{8,10},{9,15},{10,... | collective-permute-start | bytes 1179656 | tf_op jit(solution)/shard_map/ppermute | solution.py:218
  95.7 27.1 %collective-permute-start.27 = (f32[2,1,2,2,64,256]{5,4,3,2,1,0:T(8,128)S(1)}, f32[2,1,2,2,64,256]{5,4,3,2,1,0:T(8,128)S(1)}, u32[]{:S(2)}, u32[]{:S(2)}) collective-permute-start(f32[2,1,2,2,64,256]{5,4,3,2,1,0:T(8,128)S(1)} %pad_maximum_fusion.10), channel_id=1, source_target_pairs={{0,32},{1,97},{2,34},{3,99},{4,36},{5,101},{6,38},{7,103},{8,40},{... | collective-permute-start | bytes 1572872 | tf_op jit(solution)/shard_map/ppermute | solution.py:218
  122.5 12.1 %collective-permute-start.21 = (f32[1,2,2,2,64,384]{5,4,3,2,1,0:T(8,128)S(1)}, f32[1,2,2,2,64,384]{5,4,3,2,1,0:T(8,128)S(1)}, u32[]{:S(2)}, u32[]{:S(2)}) collective-permute-start(f32[1,2,2,2,64,384]{5,4,3,2,1,0:T(8,128)S(1)} %pad_maximum_fusion.5), channel_id=1, source_target_pairs={{0,2},{1,7},{2,0},{3,5},{4,6},{5,3},{6,4},{7,1},{8,10},{9,15},{10,... | collective-permute-start | bytes 2359304 | tf_op jit(solution)/shard_map/ppermute | solution.py:218
  122.7 12.1 %collective-permute-start.24 = (f32[2,1,2,2,64,384]{5,4,3,2,1,0:T(8,128)S(1)}, f32[2,1,2,2,64,384]{5,4,3,2,1,0:T(8,128)S(1)}, u32[]{:S(2)}, u32[]{:S(2)}) collective-permute-start(f32[2,1,2,2,64,384]{5,4,3,2,1,0:T(8,128)S(1)} %pad_maximum_fusion.6), channel_id=1, source_target_pairs={{0,8},{1,25},{2,10},{3,27},{4,12},{5,29},{6,14},{7,31},{8,0},{9,17... | collective-permute-start | bytes 2359304 | tf_op jit(solution)/shard_map/ppermute | solution.py:218

commit v3 on v0

v3 whole, which is shorter than its diff:
```python
import jax
import jax.numpy as jnp
from jax import lax
from jax.experimental import pallas as pl
from jax.experimental.pallas import tpu as pltpu
from jax.sharding import PartitionSpec as P

LEAD = 512
HI = lax.Precision.HIGHEST


S8 = (8, 128)
F32 = jnp.float32
LEFT = (((0,), (0,)), ((), ()))


def lb(x, c):
    return jnp.broadcast_to(x[:, c : c + 1], S8)


def sb(x, j):
    return jnp.broadcast_to(x[j : j + 1, :], S8)


def mm(x, y):
    return jnp.dot(x, y, precision=HI, preferred_element_type=F32)


def mtm(x, y):
    return lax.dot_general(x, y, LEFT, precision=HI, preferred_element_type=F32)


def chol_inv_128(V, sub, lane):
    V=list(V)
    E=[jnp.where(lane==sub+8*k,1.0,0.0) for k in range(16)]
    out=[]
    for k in range(16):
        X=V[k]
        LB=[lb(X,8*k+j) for j in range(8)]
        S=[[sb(LB[j],i) if i>=j else None for j in range(8)] for i in range(8)]
        R=[sb(X,j) for j in range(8)]
        F=[sb(E[k],j) for j in range(8)]
        l=[[None]*8 for _ in range(8)]
        inv=[None]*8
        for j in range(8):
            inv[j]=1.0/S[j][j]
            for i in range(j+1,8):
                l[i][j]=S[i][j]*inv[j]
                for m in range(j+1,i+1):
                    S[i][m]=S[i][m]-l[i][j]*S[m][j]
            for i in range(j+1,8):
                R[i]=R[i]-l[i][j]*R[j]
                F[i]=F[i]-l[i][j]*F[j]
        o=F[0]*lax.rsqrt(S[0][0])
        for j in range(1,8):
            o=jnp.where(sub==j,F[j]*lax.rsqrt(S[j][j]),o)
        out.append(o)
        if k<15:
            W=[R[j]*inv[j] for j in range(8)]
            H=[F[j]*inv[j] for j in range(8)]
            for i in range(7,0,-1):
                for j in range(i):
                    W[j]=W[j]-l[i][j]*W[i]
                    H[j]=H[j]-l[i][j]*H[i]
            for m in range(k+1,16):
                Y=V[m]; v=Y; e=E[m]
                for j in range(7,-1,-1):
                    c=lb(Y,8*k+j)
                    v=v-c*W[j]
                    e=e-c*H[j]
                V[m]=v; E[m]=e
    return out


def vmem(*shape):
    return jax.ShapeDtypeStruct(shape, F32)


VMEM = pl.BlockSpec(memory_space=pltpu.VMEM)
PARAMS = pltpu.CompilerParams(vmem_limit_bytes=40 * 2**20)


def cost(flops, nbytes):
    return pl.CostEstimate(flops=flops, bytes_accessed=nbytes, transcendentals=0)


def indexed(ref):
    return ref[0], ref[1], ref[2]


def aligned(i, n):
    return pl.ds(pl.multiple_of(i * n, n), n)


def call(kernel, out, index, args, flops=0, nbytes=1 << 20, scratch=(), out_specs=None, name=None):
    return pl.pallas_call(
        kernel,
        out_shape=out,
        in_specs=[pl.BlockSpec(memory_space=pltpu.SMEM)] + [VMEM] * len(args),
        out_specs=out_specs or jax.tree.map(lambda _: VMEM, out),
        scratch_shapes=list(scratch),
        compiler_params=PARAMS,
        cost_estimate=cost(flops, nbytes),
        name=name,
    )(index, *args)


def pack_kernel(index, x_ref, lead_ref, *outs):
    _, j, _ = indexed(index)
    for m, out in enumerate(outs):
        out[:, :LEAD] = lead_ref[...]
        out[:, LEAD:] = x_ref[:, aligned(j ^ m, 256)]


def gram_kernel(index, *refs):
    ins, outs, (lead, columns, gram) = refs[:8], refs[8:16], refs[16:]
    core, j, k = indexed(index)
    for m, ref in enumerate(ins):
        lead[128 * m : 128 * m + 128, :] = ref[:, :LEAD]
        columns[128 * m : 128 * m + 128, :] = ref[:, LEAD:]
    square = mtm(lead[:, aligned(j // 2, 128)], lead[:, aligned(core * 2 + j % 2, 128)])
    for out in outs:
        out[64:, :128] = square[:64]
        out[64:, 128:] = square[64:]
    gram[...] = mtm(lead[...], columns[...])
    for m, out in enumerate(outs):
        out[:64, :] = gram[aligned(k ^ m, 64), :]


def rows_kernel(index, *refs):
    _, _, k = indexed(index)
    for m in range(8):
        refs[8][aligned(k ^ m, 64), :] = refs[m][...]


def inverse_kernel(index, own, other, o_ref, a, d):
    core, j, k = indexed(index)
    for side, place, ref in ((core, j, own), (1 - core, k, other)):
        for m in range(8):
            at = place ^ m
            columns = aligned(side * 2 + at % 2, 128)
            a[aligned(at // 2 * 2, 64), columns] = ref[64 * m : 64 * m + 64, :128]
            a[aligned(at // 2 * 2 + 1, 64), columns] = ref[64 * m : 64 * m + 64, 128:]
    sub = lax.broadcasted_iota(jnp.int32, S8, 0)
    lane = lax.broadcasted_iota(jnp.int32, S8, 1)
    o_ref[...] = jnp.zeros_like(o_ref)
    d[...] = a[0:128, 0:128]

    @pl.loop(0, 4)
    def _(p):
        blocks = chol_inv_128([d[8 * i : 8 * i + 8, :] for i in range(16)], sub, lane)
        for i, block in enumerate(blocks):
            d[8 * i : 8 * i + 8, :] = block
        for q in range(4):

            @pl.when(p == q)
            def _():
                lo, hi = 128 * q, 128 * (q + 1)
                linv = d[...]
                if q < 3:
                    up = mm(linv, a[lo:hi, hi:])
                    d[...] = a[hi : hi + 128, hi : hi + 128] - mtm(up[:, :128], up[:, :128])
                    if q < 2:
                        a[hi:, hi:] = a[hi:, hi:] - mtm(up, up)
                o_ref[lo:hi, lo:hi] = linv
                if q > 0:
                    o_ref[lo:hi, :lo] = mm(linv, o_ref[lo:hi, :lo])
                if q < 3:
                    o_ref[hi:, :hi] = o_ref[hi:, :hi] - mtm(up, o_ref[lo:hi, :hi])


def two(x):
    high = x.astype(jnp.bfloat16)
    return high, (x - high.astype(F32)).astype(jnp.bfloat16)


def product_kernel(index, inverse_ref, *refs):
    parts, (out_ref, lh_ref, ll_ref, buf, sems) = refs[:8], refs[8:]
    core, j, _ = indexed(index)
    lh_ref[...], ll_ref[...] = two(inverse_ref[...])
    dot = lambda x, y: jnp.dot(x, y, preferred_element_type=F32)
    copies = []
    for m, part in enumerate(parts):
        xh, xl = two(part[...])
        for r, n in ((0, 256), (256, 512)):
            lh, ll = lh_ref[r : r + 256, :n], ll_ref[r : r + 256, :n]
            y = dot(lh, xh[:n]) + (dot(lh, xl[:n]) + dot(ll, xh[:n]))
            ids = core * 2048 + (j ^ m) * 256 + lax.broadcasted_iota(jnp.int32, y.shape, 1)
            y = jnp.where(ids >= r + lax.broadcasted_iota(jnp.int32, y.shape, 0), y, 0.0)
            buf[m, r : r + 256, :] = y
        copies.append(pltpu.make_async_copy(buf.at[m], out_ref.at[:, aligned(j ^ m, 256)], sems.at[m]))
        copies[-1].start()
    for copy in copies:
        copy.wait()


def flip(kind, mask):
    pairs = []
    for chip in range(64):
        for core in range(2):
            to = [chip % 4, chip // 4 % 4, chip // 16]
            for axis in range(3):
                if mask >> axis & 1:
                    to[axis] ^= (1, 3)[kind ^ core]
            pairs.append((chip * 2 + core, (to[0] + 4 * to[1] + 16 * to[2]) * 2 + core))
    return pairs


PLUS, MINUS = 0, 1


def exchange(kind, send):
    return [send(m) if m == 0 else lax.ppermute(send(m), ("row", "col"), flip(kind, m)) for m in range(8)]


def body(contributions, valid_rows):
    blocks, height, width = contributions.shape
    core = lax.axis_index("col")
    row = lax.axis_index("row")
    gray, high = 0, 0
    for axis, at in enumerate((row % 4, row // 4 % 4, row // 16)):
        high += at // 2 << axis
        gray += (at // 2 ^ at % 2) << axis
    index = jnp.stack([core, jnp.where(core == 0, gray, high), jnp.where(core == 0, high, gray)]).astype(jnp.int32)

    def across(x):
        return lax.ppermute(x, "col", [(0, 1), (1, 0)])

    live = jnp.arange(height, dtype=jnp.int32)[None, :] < valid_rows[:, None]
    frontal = jnp.where(live[:, :, None], contributions, 0.0).reshape(blocks * height, width)
    own = frontal[:, :LEAD]
    lead = jnp.where(core == 0, own, across(own))
    packed = call(pack_kernel, (vmem(128, 768),) * 8, index, (frontal, lead), name="pack")
    packed = exchange(PLUS, lambda m: packed[m])
    scratch = (pltpu.VMEM((1024, LEAD), F32), pltpu.VMEM((1024, 256), F32), pltpu.VMEM((LEAD, 256), F32))
    grams = call(gram_kernel, (vmem(128, 256),) * 8, index, packed, 1 << 30, 4 << 20, scratch, name="gram")
    g = exchange(MINUS, lambda m: grams[m])
    mine = ((g[0] + g[1]) + (g[2] + g[3])) + ((g[4] + g[5]) + (g[6] + g[7]))
    rest, square = mine[:64], mine[64:]
    square = jnp.concatenate(exchange(PLUS, lambda m: square), axis=0)
    rest = exchange(MINUS, lambda m: rest)
    rest = call(rows_kernel, vmem(LEAD, 256), index, rest, name="rows")
    scratch = (pltpu.VMEM((LEAD, LEAD), F32), pltpu.VMEM((128, 128), F32))
    inverse = call(inverse_kernel, vmem(LEAD, LEAD), index, (square, across(square)), 20 * 10**9, 2 << 20, scratch, name="inverse")
    parts = exchange(PLUS, lambda m: rest)
    scratch = (
        pltpu.VMEM((LEAD, LEAD), jnp.bfloat16),
        pltpu.VMEM((LEAD, LEAD), jnp.bfloat16),
        pltpu.VMEM((8, LEAD, 256), F32),
        pltpu.SemaphoreType.DMA((8,)),
    )
    spec = pl.BlockSpec(memory_space=pl.ANY)
    return call(product_kernel, vmem(LEAD, width), index, (inverse, *parts), 3 << 30, 9 << 20, scratch, spec, "product")


def solution(mesh):
    return jax.shard_map(
        body,
        mesh=mesh,
        in_specs=(P(("front", "row"), None, "col"), P(("front", "row"))),
        out_specs=P("front", "col"),
        check_vma=False,
    )
```

time: 171 us -> 149 us (0.87)
  blocking collectives: 64.3 us -> 0 us
  starting transfers between devices: 5.97 us -> 59.8 us
  matrix products: 13.6 us -> 0 us
  between operations: 14.1 us -> 1.19 us
  waiting for transfers between devices: 44.5 us -> 55.8 us
  Pallas kernels: 20.7 us -> 30.4 us
  local copies, waits for them, and re-layouts: 3.39 us -> 0.08 us
  other arithmetic: 3.83 us -> 1.55 us
    all_to_all x1 -> x0, blocking collectives: 64.3 us -> none  [body(): pieces = lax.all_to_all(gram.reshape(64, LEAD // 64, width), 'row', 0, 0)]
    ppermute x2 -> x37, starting transfers between devices: 0.09 us -> 59.8 us  [the longest x35 59.6 us: exchange(): lax.ppermute(send(m), ('row', 'col'), flip(kind, m))]
    ppermute x2 -> x37, waiting for transfers between devices: 2.7 us -> 55.8 us  [the longest x35 54.5 us: exchange(): lax.ppermute(send(m), ('row', 'col'), flip(kind, m))]
    all_gather x1 -> x0, waiting for transfers between devices: 22.3 us -> none  [body(): gram_all = lax.all_gather(mine, 'row', axis=0, tiled=True)]
    all_to_all x1 -> x0, waiting for transfers between devices: 19.5 us -> none  [body(): lax.all_to_all(jnp.broadcast_to(mine11[None], (64, LEAD // 64, LEAD)), 'r...]
    dot_general x2 -> x0, matrix products: 13.6 us -> none  [the longest x1 10.1 us: body(): projected = jnp.dot(inverse, gram_all, precision=HI)]
    pallas_call x1 -> x5, Pallas kernels: 20.7 us -> 30.4 us  [call(): pl.pallas_call(kernel, out_shape=out, in_specs=[pl.BlockSpec(memory_space...]
    all_to_all x1 -> x0, starting transfers between devices: 5.88 us -> none  [body(): lax.all_to_all(jnp.broadcast_to(mine11[None], (64, LEAD // 64, LEAD)), 'r...]
  transfers between devices with their start and end apart: 4 -> 37, of which waited for: 4 -> 13; matrix products, arithmetic and copies ran while one was open for 1% -> 0% of each run, Pallas kernels for 12% -> 15%
where the time goes in v3:
time: 149 us
  starting transfers between devices  59.8 us (40%)
  waiting for transfers between devices  55.8 us (37%)
  Pallas kernels  30.4 us (20%)
  other arithmetic  1.55 us (1%)
    ppermute x35, starting transfers between devices, exchange(): lax.ppermute(send(m), ('row', 'col'), flip(kind, m))  59.6 us
    ppermute x35, waiting for transfers between devices, exchange(): lax.ppermute(send(m), ('row', 'col'), flip(kind, m))  54.5 us
    pallas_call x5, Pallas kernels, call(): pl.pallas_call(kernel, out_shape=out, in_specs=[pl.BlockSpec(memory_space...  30.4 us
  transfers between devices with their start and end apart: 37, of which 13 were waited for; matrix products, arithmetic and copies ran while one was open for 0% of the time, Pallas kernels for 15%

profile of v3, /device:TPU:0, one launch (start us, length us, event | category | flops | bytes accessed | tf_op | source)
XLA Modules:
  0.0 148.8 jit_solution(2515838816777845174)
XLA Ops:
  0.7 1.4 select_bitcast_fusion.x_ref
  2.1 0.1 collective-permute-start
  2.3 0.1 pad_add_fusion.index
  2.4 1.3 collective-permute-done
  3.7 0.7 pack.1
  4.5 1.7 %collective-permute-start.1 = (f32[128,768]{1,0:T(8,128)S(1)}, f32[128,768]{1,0:T(8,128)S(1)}, u32[]{:S(2)}, u32[]{:S(2)}) collective-permute-start(f32[128,768]{1,0:T(8,128)S(1)} %get-tuple-element.22), channel_id=1, source_target_pairs={{0,2},{1,7},{2,0},{3,5},{4,6},{5,3},{6,4},{7,1},{8,10},{9,15},{10,... | collective-permute-start | bytes 1179656 | tf_op jit(solution)/shard_map/ppermute | solution.py:213
  6.1 1.6 %collective-permute-start.2 = (f32[128,768]{1,0:T(8,128)S(1)}, f32[128,768]{1,0:T(8,128)S(1)}, u32[]{:S(2)}, u32[]{:S(2)}) collective-permute-start(f32[128,768]{1,0:T(8,128)S(1)} %get-tuple-element.23), channel_id=1, source_target_pairs={{0,8},{1,25},{2,10},{3,27},{4,12},{5,29},{6,14},{7,31},{8,0},{9,17... | collective-permute-start | bytes 1179656 | tf_op jit(solution)/shard_map/ppermute | solution.py:213
  7.7 0.3 collective-permute-start.3
  8.0 2.0 %collective-permute-start.4 = (f32[128,768]{1,0:T(8,128)S(1)}, f32[128,768]{1,0:T(8,128)S(1)}, u32[]{:S(2)}, u32[]{:S(2)}) collective-permute-start(f32[128,768]{1,0:T(8,128)S(1)} %get-tuple-element.25), channel_id=1, source_target_pairs={{0,32},{1,97},{2,34},{3,99},{4,36},{5,101},{6,38},{7,103},{8,40},{... | collective-permute-start | bytes 1179656 | tf_op jit(solution)/shard_map/ppermute | solution.py:213
  10.0 1.0 collective-permute-start.5
  11.1 1.2 collective-permute-done.1.refs_1_
  12.3 3.0 %collective-permute-start.6 = (f32[128,768]{1,0:T(8,128)S(1)}, f32[128,768]{1,0:T(8,128)S(1)}, u32[]{:S(2)}, u32[]{:S(2)}) collective-permute-start(f32[128,768]{1,0:T(8,128)S(1)} %get-tuple-element.27), channel_id=1, source_target_pairs={{0,40},{1,121},{2,42},{3,123},{4,44},{5,125},{6,46},{7,127},{8,32}... | collective-permute-start | bytes 1179656 | tf_op jit(solution)/shard_map/ppermute | solution.py:213
  15.3 2.8 %collective-permute-done.2.refs_2_ = f32[128,768]{1,0:T(8,128)S(1)} collective-permute-done((f32[128,768]{1,0:T(8,128)S(1)}, f32[128,768]{1,0:T(8,128)S(1)}, u32[]{:S(2)}, u32[]{:S(2)}) %collective-permute-start.2) | collective-permute-done | bytes 393248 | tf_op jit(solution)/shard_map/ppermute | solution.py:213
  18.1 2.9 %collective-permute-start.7 = (f32[128,768]{1,0:T(8,128)S(1)}, f32[128,768]{1,0:T(8,128)S(1)}, u32[]{:S(2)}, u32[]{:S(2)}) collective-permute-start(f32[128,768]{1,0:T(8,128)S(1)} %get-tuple-element.28), channel_id=1, source_target_pairs={{0,42},{1,127},{2,40},{3,125},{4,46},{5,123},{6,44},{7,121},{8,34}... | collective-permute-start | bytes 1179656 | tf_op jit(solution)/shard_map/ppermute | solution.py:213
  21.0 0.0 collective-permute-done.4.refs_4_
  21.0 4.0 %collective-permute-done.5.refs_5_ = f32[128,768]{1,0:T(8,128)S(1)} collective-permute-done((f32[128,768]{1,0:T(8,128)S(1)}, f32[128,768]{1,0:T(8,128)S(1)}, u32[]{:S(2)}, u32[]{:S(2)}) %collective-permute-start.5) | collective-permute-done | bytes 393248 | tf_op jit(solution)/shard_map/ppermute | solution.py:213
  25.0 5.7 %collective-permute-done.6.refs_6_ = f32[128,768]{1,0:T(8,128)S(1)} collective-permute-done((f32[128,768]{1,0:T(8,128)S(1)}, f32[128,768]{1,0:T(8,128)S(1)}, u32[]{:S(2)}, u32[]{:S(2)}) %collective-permute-start.6) | collective-permute-done | bytes 393248 | tf_op jit(solution)/shard_map/ppermute | solution.py:213
  30.7 0.0 collective-permute-done.7.refs_7_
  30.7 3.2 %gram.1 = (f32[128,256]{1,0:T(8,128)S(1)}, f32[128,256]{1,0:T(8,128)S(1)}, f32[128,256]{1,0:T(8,128)S(1)}, f32[128,256]{1,0:T(8,128)S(1)}, f32[128,256]{1,0:T(8,...) custom-call(s32[3]{0:T(128)S(1)} %pad_add_fusion.index, ...), custom_call_target="tpu_custom_call" | custom-call | flops 1073741824 | bytes 4194304 | tf_op jit(solution)/shard_map/gram/pallas_call | solution.py:96
  33.9 2.7 %collective-permute-start.8 = (f32[128,256]{1,0:T(8,128)S(1)}, f32[128,256]{1,0:T(8,128)S(1)}, u32[]{:S(2)}, u32[]{:S(2)}) collective-permute-start(f32[128,256]{1,0:T(8,128)S(1)} %get-tuple-element.30), channel_id=1, source_target_pairs={{0,6},{1,3},{2,4},{3,1},{4,2},{5,7},{6,0},{7,5},{8,14},{9,11},{10,... | collective-permute-start | bytes 393224 | tf_op jit(solution)/shard_map/ppermute | solution.py:213
  36.6 3.1 %collective-permute-start.9 = (f32[128,256]{1,0:T(8,128)S(1)}, f32[128,256]{1,0:T(8,128)S(1)}, u32[]{:S(2)}, u32[]{:S(2)}) collective-permute-start(f32[128,256]{1,0:T(8,128)S(1)} %get-tuple-element.31), channel_id=1, source_target_pairs={{0,24},{1,9},{2,26},{3,11},{4,28},{5,13},{6,30},{7,15},{8,16},{9,1... | collective-permute-start | bytes 393224 | tf_op jit(solution)/shard_map/ppermute | solution.py:213
  39.8 0.1 collective-permute-start.10
  39.9 2.5 %collective-permute-start.11 = (f32[128,256]{1,0:T(8,128)S(1)}, f32[128,256]{1,0:T(8,128)S(1)}, u32[]{:S(2)}, u32[]{:S(2)}) collective-permute-start(f32[128,256]{1,0:T(8,128)S(1)} %get-tuple-element.33), channel_id=1, source_target_pairs={{0,96},{1,33},{2,98},{3,35},{4,100},{5,37},{6,102},{7,39},{8,104},... | collective-permute-start | bytes 393224 | tf_op jit(solution)/shard_map/ppermute | solution.py:213
  42.4 2.8 %collective-permute-start.12 = (f32[128,256]{1,0:T(8,128)S(1)}, f32[128,256]{1,0:T(8,128)S(1)}, u32[]{:S(2)}, u32[]{:S(2)}) collective-permute-start(f32[128,256]{1,0:T(8,128)S(1)} %get-tuple-element.34), channel_id=1, source_target_pairs={{0,102},{1,35},{2,100},{3,33},{4,98},{5,39},{6,96},{7,37},{8,110},... | collective-permute-start | bytes 393224 | tf_op jit(solution)/shard_map/ppermute | solution.py:213
  45.2 0.0 collective-permute-done.8
  45.2 5.1 %collective-permute-start.13 = (f32[128,256]{1,0:T(8,128)S(1)}, f32[128,256]{1,0:T(8,128)S(1)}, u32[]{:S(2)}, u32[]{:S(2)}) collective-permute-start(f32[128,256]{1,0:T(8,128)S(1)} %get-tuple-element.35), channel_id=1, source_target_pairs={{0,120},{1,41},{2,122},{3,43},{4,124},{5,45},{6,126},{7,47},{8,112... | collective-permute-start | bytes 393224 | tf_op jit(solution)/shard_map/ppermute | solution.py:213
  50.3 0.0 collective-permute-done.9
  50.3 0.3 collective-permute-start.14
  50.6 0.1 collective-permute-done.12
  50.7 2.8 %collective-permute-done.13 = f32[128,256]{1,0:T(8,128)S(1)} collective-permute-done((f32[128,256]{1,0:T(8,128)S(1)}, f32[128,256]{1,0:T(8,128)S(1)}, u32[]{:S(2)}, u32[]{:S(2)}) %collective-permute-start.13) | collective-permute-done | bytes 131104 | tf_op jit(solution)/shard_map/ppermute | solution.py:213
  53.5 7.2 %collective-permute-done.14 = f32[128,256]{1,0:T(8,128)S(1)} collective-permute-done((f32[128,256]{1,0:T(8,128)S(1)}, f32[128,256]{1,0:T(8,128)S(1)}, u32[]{:S(2)}, u32[]{:S(2)}) %collective-permute-start.14) | collective-permute-done | bytes 131104 | tf_op jit(solution)/shard_map/ppermute | solution.py:213
  60.7 0.1 add_add_fusion
  60.8 0.4 collective-permute-start.29
  61.2 5.0 %collective-permute-start.28 = (f32[64,256]{1,0:T(8,128)S(1)}, f32[64,256]{1,0:T(8,128)S(1)}, u32[]{:S(2)}, u32[]{:S(2)}) collective-permute-start(f32[64,256]{1,0:T(8,128)S(1)} %get-tuple-element.37.refs_0_), channel_id=1, source_target_pairs={{0,120},{1,41},{2,122},{3,43},{4,124},{5,45},{6,126},{7,47},{8,112... | collective-permute-start | bytes 196616 | tf_op jit(solution)/shard_map/ppermute | solution.py:213
  66.1 2.9 %collective-permute-start.27 = (f32[64,256]{1,0:T(8,128)S(1)}, f32[64,256]{1,0:T(8,128)S(1)}, u32[]{:S(2)}, u32[]{:S(2)}) collective-permute-start(f32[64,256]{1,0:T(8,128)S(1)} %get-tuple-element.37.refs_0_), channel_id=1, source_target_pairs={{0,102},{1,35},{2,100},{3,33},{4,98},{5,39},{6,96},{7,37},{8,110},... | collective-permute-start | bytes 196616 | tf_op jit(solution)/shard_map/ppermute | solution.py:213
  69.0 2.5 %collective-permute-start.26 = (f32[64,256]{1,0:T(8,128)S(1)}, f32[64,256]{1,0:T(8,128)S(1)}, u32[]{:S(2)}, u32[]{:S(2)}) collective-permute-start(f32[64,256]{1,0:T(8,128)S(1)} %get-tuple-element.37.refs_0_), channel_id=1, source_target_pairs={{0,96},{1,33},{2,98},{3,35},{4,100},{5,37},{6,102},{7,39},{8,104},... | collective-permute-start | bytes 196616 | tf_op jit(solution)/shard_map/ppermute | solution.py:213
  71.6 0.1 collective-permute-start.25
  71.7 3.0 %collective-permute-start.24 = (f32[64,256]{1,0:T(8,128)S(1)}, f32[64,256]{1,0:T(8,128)S(1)}, u32[]{:S(2)}, u32[]{:S(2)}) collective-permute-start(f32[64,256]{1,0:T(8,128)S(1)} %get-tuple-element.37.refs_0_), channel_id=1, source_target_pairs={{0,24},{1,9},{2,26},{3,11},{4,28},{5,13},{6,30},{7,15},{8,16},{9,1... | collective-permute-start | bytes 196616 | tf_op jit(solution)/shard_map/ppermute | solution.py:213
  74.7 0.0 collective-permute-done.28.refs_6_
  74.7 2.8 %collective-permute-start.23 = (f32[64,256]{1,0:T(8,128)S(1)}, f32[64,256]{1,0:T(8,128)S(1)}, u32[]{:S(2)}, u32[]{:S(2)}) collective-permute-start(f32[64,256]{1,0:T(8,128)S(1)} %get-tuple-element.37.refs_0_), channel_id=1, source_target_pairs={{0,6},{1,3},{2,4},{3,1},{4,2},{5,7},{6,0},{7,5},{8,14},{9,11},{10,... | collective-permute-start | bytes 196616 | tf_op jit(solution)/shard_map/ppermute | solution.py:213
  77.5 0.1 collective-permute-start.21
  77.6 1.9 %collective-permute-done.25.refs_3_ = f32[64,256]{1,0:T(8,128)S(1)} collective-permute-done((f32[64,256]{1,0:T(8,128)S(1)}, f32[64,256]{1,0:T(8,128)S(1)}, u32[]{:S(2)}, u32[]{:S(2)}) %collective-permute-start.25) | collective-permute-done | bytes 65568 | tf_op jit(solution)/shard_map/ppermute | solution.py:213
  79.5 2.4 %collective-permute-start.20 = (f32[64,256]{1,0:T(8,128)S(1)}, f32[64,256]{1,0:T(8,128)S(1)}, u32[]{:S(2)}, u32[]{:S(2)}) collective-permute-start(f32[64,256]{1,0:T(8,128)S(1)} %get-tuple-element.39), channel_id=1, source_target_pairs={{0,40},{1,121},{2,42},{3,123},{4,44},{5,125},{6,46},{7,127},{8,32}... | collective-permute-start | bytes 196616 | tf_op jit(solution)/shard_map/ppermute | solution.py:213
  81.9 0.0 collective-permute-done.24.refs_2_
  81.9 0.0 collective-permute-start.19
  81.9 0.0 collective-permute-done.23.refs_1_
  81.9 1.5 %collective-permute-start.18 = (f32[64,256]{1,0:T(8,128)S(1)}, f32[64,256]{1,0:T(8,128)S(1)}, u32[]{:S(2)}, u32[]{:S(2)}) collective-permute-start(f32[64,256]{1,0:T(8,128)S(1)} %get-tuple-element.39), channel_id=1, source_target_pairs={{0,32},{1,97},{2,34},{3,99},{4,36},{5,101},{6,38},{7,103},{8,40},{... | collective-permute-start | bytes 196616 | tf_op jit(solution)/shard_map/ppermute | solution.py:213
  83.4 0.6 rows.1.refs_0_
  84.0 0.1 collective-permute-start.16
  84.2 4.2 %collective-permute-done.16 = f32[64,256]{1,0:T(8,128)S(1)} collective-permute-done((f32[64,256]{1,0:T(8,128)S(1)}, f32[64,256]{1,0:T(8,128)S(1)}, u32[]{:S(2)}, u32[]{:S(2)}) %collective-permute-start.16) | collective-permute-done | bytes 65568 | tf_op jit(solution)/shard_map/ppermute | solution.py:213
  88.4 1.4 collective-permute-start.17
  89.8 3.8 %collective-permute-done.17 = f32[64,256]{1,0:T(8,128)S(1)} collective-permute-done((f32[64,256]{1,0:T(8,128)S(1)}, f32[64,256]{1,0:T(8,128)S(1)}, u32[]{:S(2)}, u32[]{:S(2)}) %collective-permute-start.17) | collective-permute-done | bytes 65568 | tf_op jit(solution)/shard_map/ppermute | solution.py:213
  93.6 1.9 %collective-permute-start.36 = (f32[512,256]{1,0:T(8,128)S(1)}, f32[512,256]{1,0:T(8,128)S(1)}, u32[]{:S(2)}, u32[]{:S(2)}) collective-permute-start(f32[512,256]{1,0:T(8,128)S(1)} %rows.1.refs_0_), channel_id=1, source_target_pairs={{0,42},{1,127},{2,40},{3,125},{4,46},{5,123},{6,44},{7,121},{8,34}... | collective-permute-start | bytes 1572872 | tf_op jit(solution)/shard_map/ppermute | solution.py:213
  95.5 2.6 %collective-permute-start.35 = (f32[512,256]{1,0:T(8,128)S(1)}, f32[512,256]{1,0:T(8,128)S(1)}, u32[]{:S(2)}, u32[]{:S(2)}) collective-permute-start(f32[512,256]{1,0:T(8,128)S(1)} %rows.1.refs_0_), channel_id=1, source_target_pairs={{0,40},{1,121},{2,42},{3,123},{4,44},{5,125},{6,46},{7,127},{8,32}... | collective-permute-start | bytes 1572872 | tf_op jit(solution)/shard_map/ppermute | solution.py:213
  98.1 0.0 collective-permute-done.19
  98.2 0.1 collective-permute-start.22
  98.3 0.2 collective-permute-start.34
  98.5 1.5 collective-permute-start.33
  99.9 5.8 %collective-permute-done.36.refs_7_ = f32[512,256]{1,0:T(8,128)S(1)} collective-permute-done((f32[512,256]{1,0:T(8,128)S(1)}, f32[512,256]{1,0:T(8,128)S(1)}, u32[]{:S(2)}, u32[]{:S(2)}) %collective-permute-start.36) | collective-permute-done | bytes 524320 | tf_op jit(solution)/shard_map/ppermute | solution.py:213
  105.7 0.4 collective-permute-start.32
  106.1 14.9 %collective-permute-done.35.refs_6_ = f32[512,256]{1,0:T(8,128)S(1)} collective-permute-done((f32[512,256]{1,0:T(8,128)S(1)}, f32[512,256]{1,0:T(8,128)S(1)}, u32[]{:S(2)}, u32[]{:S(2)}) %collective-permute-start.35) | collective-permute-done | bytes 524320 | tf_op jit(solution)/shard_map/ppermute | solution.py:213
  121.1 1.7 %collective-permute-start.30 = (f32[512,256]{1,0:T(8,128)S(1)}, f32[512,256]{1,0:T(8,128)S(1)}, u32[]{:S(2)}, u32[]{:S(2)}) collective-permute-start(f32[512,256]{1,0:T(8,128)S(1)} %rows.1.refs_0_), channel_id=1, source_target_pairs={{0,2},{1,7},{2,0},{3,5},{4,6},{5,3},{6,4},{7,1},{8,10},{9,15},{10,... | collective-permute-start | bytes 1572872 | tf_op jit(solution)/shard_map/ppermute | solution.py:213
  122.7 21.3 %inverse.1.inverse_ref = f32[512,512]{1,0:T(8,128)S(1)} custom-call(s32[3]{0:T(128)S(1)} %pad_add_fusion.index, f32[512,256]{1,0:T(8,128)S(1)} %constant_dynamic-update-slice_fusion.own, f32[512,256]{1,0:T(8,128)S(1)} %collective-permute-done.22.other), custom_call_target="tpu_custom_call" | custom-call | flops 20000000000 | bytes 2097152 | tf_op jit(solution)/shard_map/inverse/pallas_call | solution.py:96
  144.1 4.6 %product.1 = f32[512,2048]{1,0:T(8,128)} custom-call(s32[3]{0:T(128)S(1)} %pad_add_fusion.index, f32[512,512]{1,0:T(8,128)S(1)} %inverse.1.inverse_ref, f32[512,256]{1,0:T(8,128)S(1)} %rows.1.refs_0_, f32[512,256]{1,0:T(8,128)S(1)} %collective-permute-done.30.refs_1_, f32[512,256]{1,0:T(8,128)S(1)} %collective-permute-done.31.refs_2_, ...), custom_call_target="tpu_custom_call" | custom-call | flops 3221225472 | bytes 9437184 | tf_op jit(solution)/shard_map/product/pallas_call | solution.py:96
  (29 shorter events, 0.2 us)
Async XLA Ops:
  2.1 1.6 %collective-permute-start = (f32[128,512]{1,0:T(8,128)S(1)}, f32[128,512]{1,0:T(8,128)S(1)}, u32[]{:S(2)}, u32[]{:S(2)}) collective-permute-start(f32[128,512]{1,0:T(8,128)S(1)} %slice.12), channel_id=1, source_target_pairs={{0,1},{1,0},{2,3},{3,2},{4,5},{5,4},{6,7},{7,6},{8,9},{9,8},{10,11... | collective-permute-start | bytes 786440 | tf_op jit(solution)/shard_map/ppermute | solution.py:227
  4.5 7.9 %collective-permute-start.1 = (f32[128,768]{1,0:T(8,128)S(1)}, f32[128,768]{1,0:T(8,128)S(1)}, u32[]{:S(2)}, u32[]{:S(2)}) collective-permute-start(f32[128,768]{1,0:T(8,128)S(1)} %get-tuple-element.22), channel_id=1, source_target_pairs={{0,2},{1,7},{2,0},{3,5},{4,6},{5,3},{6,4},{7,1},{8,10},{9,15},{10,... | collective-permute-start | bytes 1179656 | tf_op jit(solution)/shard_map/ppermute | solution.py:213
  6.1 12.0 %collective-permute-start.2 = (f32[128,768]{1,0:T(8,128)S(1)}, f32[128,768]{1,0:T(8,128)S(1)}, u32[]{:S(2)}, u32[]{:S(2)}) collective-permute-start(f32[128,768]{1,0:T(8,128)S(1)} %get-tuple-element.23), channel_id=1, source_target_pairs={{0,8},{1,25},{2,10},{3,27},{4,12},{5,29},{6,14},{7,31},{8,0},{9,17... | collective-permute-start | bytes 1179656 | tf_op jit(solution)/shard_map/ppermute | solution.py:213
  7.7 13.3 %collective-permute-start.3 = (f32[128,768]{1,0:T(8,128)S(1)}, f32[128,768]{1,0:T(8,128)S(1)}, u32[]{:S(2)}, u32[]{:S(2)}) collective-permute-start(f32[128,768]{1,0:T(8,128)S(1)} %get-tuple-element.24), channel_id=1, source_target_pairs={{0,10},{1,31},{2,8},{3,29},{4,14},{5,27},{6,12},{7,25},{8,2},{9,23... | collective-permute-start | bytes 1179656 | tf_op jit(solution)/shard_map/ppermute | solution.py:213
  8.0 13.0 %collective-permute-start.4 = (f32[128,768]{1,0:T(8,128)S(1)}, f32[128,768]{1,0:T(8,128)S(1)}, u32[]{:S(2)}, u32[]{:S(2)}) collective-permute-start(f32[128,768]{1,0:T(8,128)S(1)} %get-tuple-element.25), channel_id=1, source_target_pairs={{0,32},{1,97},{2,34},{3,99},{4,36},{5,101},{6,38},{7,103},{8,40},{... | collective-permute-start | bytes 1179656 | tf_op jit(solution)/shard_map/ppermute | solution.py:213
  10.0 15.0 %collective-permute-start.5 = (f32[128,768]{1,0:T(8,128)S(1)}, f32[128,768]{1,0:T(8,128)S(1)}, u32[]{:S(2)}, u32[]{:S(2)}) collective-permute-start(f32[128,768]{1,0:T(8,128)S(1)} %get-tuple-element.26), channel_id=1, source_target_pairs={{0,34},{1,103},{2,32},{3,101},{4,38},{5,99},{6,36},{7,97},{8,42},{... | collective-permute-start | bytes 1179656 | tf_op jit(solution)/shard_map/ppermute | solution.py:213
  12.3 18.3 %collective-permute-start.6 = (f32[128,768]{1,0:T(8,128)S(1)}, f32[128,768]{1,0:T(8,128)S(1)}, u32[]{:S(2)}, u32[]{:S(2)}) collective-permute-start(f32[128,768]{1,0:T(8,128)S(1)} %get-tuple-element.27), channel_id=1, source_target_pairs={{0,40},{1,121},{2,42},{3,123},{4,44},{5,125},{6,46},{7,127},{8,32}... | collective-permute-start | bytes 1179656 | tf_op jit(solution)/shard_map/ppermute | solution.py:213
  18.1 12.5 %collective-permute-start.7 = (f32[128,768]{1,0:T(8,128)S(1)}, f32[128,768]{1,0:T(8,128)S(1)}, u32[]{:S(2)}, u32[]{:S(2)}) collective-permute-start(f32[128,768]{1,0:T(8,128)S(1)} %get-tuple-element.28), channel_id=1, source_target_pairs={{0,42},{1,127},{2,40},{3,125},{4,46},{5,123},{6,44},{7,121},{8,34}... | collective-permute-start | bytes 1179656 | tf_op jit(solution)/shard_map/ppermute | solution.py:213
  33.9 11.3 %collective-permute-start.8 = (f32[128,256]{1,0:T(8,128)S(1)}, f32[128,256]{1,0:T(8,128)S(1)}, u32[]{:S(2)}, u32[]{:S(2)}) collective-permute-start(f32[128,256]{1,0:T(8,128)S(1)} %get-tuple-element.30), channel_id=1, source_target_pairs={{0,6},{1,3},{2,4},{3,1},{4,2},{5,7},{6,0},{7,5},{8,14},{9,11},{10,... | collective-permute-start | bytes 393224 | tf_op jit(solution)/shard_map/ppermute | solution.py:213
  36.6 13.7 %collective-permute-start.9 = (f32[128,256]{1,0:T(8,128)S(1)}, f32[128,256]{1,0:T(8,128)S(1)}, u32[]{:S(2)}, u32[]{:S(2)}) collective-permute-start(f32[128,256]{1,0:T(8,128)S(1)} %get-tuple-element.31), channel_id=1, source_target_pairs={{0,24},{1,9},{2,26},{3,11},{4,28},{5,13},{6,30},{7,15},{8,16},{9,1... | collective-permute-start | bytes 393224 | tf_op jit(solution)/shard_map/ppermute | solution.py:213
  39.8 10.8 %collective-permute-start.10 = (f32[128,256]{1,0:T(8,128)S(1)}, f32[128,256]{1,0:T(8,128)S(1)}, u32[]{:S(2)}, u32[]{:S(2)}) collective-permute-start(f32[128,256]{1,0:T(8,128)S(1)} %get-tuple-element.32), channel_id=1, source_target_pairs={{0,30},{1,11},{2,28},{3,9},{4,26},{5,15},{6,24},{7,13},{8,22},{9,3... | collective-permute-start | bytes 393224 | tf_op jit(solution)/shard_map/ppermute | solution.py:213
  39.9 10.7 %collective-permute-start.11 = (f32[128,256]{1,0:T(8,128)S(1)}, f32[128,256]{1,0:T(8,128)S(1)}, u32[]{:S(2)}, u32[]{:S(2)}) collective-permute-start(f32[128,256]{1,0:T(8,128)S(1)} %get-tuple-element.33), channel_id=1, source_target_pairs={{0,96},{1,33},{2,98},{3,35},{4,100},{5,37},{6,102},{7,39},{8,104},... | collective-permute-start | bytes 393224 | tf_op jit(solution)/shard_map/ppermute | solution.py:213
  42.4 8.3 %collective-permute-start.12 = (f32[128,256]{1,0:T(8,128)S(1)}, f32[128,256]{1,0:T(8,128)S(1)}, u32[]{:S(2)}, u32[]{:S(2)}) collective-permute-start(f32[128,256]{1,0:T(8,128)S(1)} %get-tuple-element.34), channel_id=1, source_target_pairs={{0,102},{1,35},{2,100},{3,33},{4,98},{5,39},{6,96},{7,37},{8,110},... | collective-permute-start | bytes 393224 | tf_op jit(solution)/shard_map/ppermute | solution.py:213
  45.2 8.3 %collective-permute-start.13 = (f32[128,256]{1,0:T(8,128)S(1)}, f32[128,256]{1,0:T(8,128)S(1)}, u32[]{:S(2)}, u32[]{:S(2)}) collective-permute-start(f32[128,256]{1,0:T(8,128)S(1)} %get-tuple-element.35), channel_id=1, source_target_pairs={{0,120},{1,41},{2,122},{3,43},{4,124},{5,45},{6,126},{7,47},{8,112... | collective-permute-start | bytes 393224 | tf_op jit(solution)/shard_map/ppermute | solution.py:213
  50.3 10.4 %collective-permute-start.14 = (f32[128,256]{1,0:T(8,128)S(1)}, f32[128,256]{1,0:T(8,128)S(1)}, u32[]{:S(2)}, u32[]{:S(2)}) collective-permute-start(f32[128,256]{1,0:T(8,128)S(1)} %get-tuple-element.36), channel_id=1, source_target_pairs={{0,126},{1,43},{2,124},{3,41},{4,122},{5,47},{6,120},{7,45},{8,118... | collective-permute-start | bytes 393224 | tf_op jit(solution)/shard_map/ppermute | solution.py:213
  60.8 10.9 %collective-permute-start.29 = (f32[64,256]{1,0:T(8,128)S(1)}, f32[64,256]{1,0:T(8,128)S(1)}, u32[]{:S(2)}, u32[]{:S(2)}) collective-permute-start(f32[64,256]{1,0:T(8,128)S(1)} %get-tuple-element.37.refs_0_), channel_id=1, source_target_pairs={{0,126},{1,43},{2,124},{3,41},{4,122},{5,47},{6,120},{7,45},{8,118... | collective-permute-start | bytes 196616 | tf_op jit(solution)/shard_map/ppermute | solution.py:213
  61.2 13.6 %collective-permute-start.28 = (f32[64,256]{1,0:T(8,128)S(1)}, f32[64,256]{1,0:T(8,128)S(1)}, u32[]{:S(2)}, u32[]{:S(2)}) collective-permute-start(f32[64,256]{1,0:T(8,128)S(1)} %get-tuple-element.37.refs_0_), channel_id=1, source_target_pairs={{0,120},{1,41},{2,122},{3,43},{4,124},{5,45},{6,126},{7,47},{8,112... | collective-permute-start | bytes 196616 | tf_op jit(solution)/shard_map/ppermute | solution.py:213
  66.1 11.4 %collective-permute-start.27 = (f32[64,256]{1,0:T(8,128)S(1)}, f32[64,256]{1,0:T(8,128)S(1)}, u32[]{:S(2)}, u32[]{:S(2)}) collective-permute-start(f32[64,256]{1,0:T(8,128)S(1)} %get-tuple-element.37.refs_0_), channel_id=1, source_target_pairs={{0,102},{1,35},{2,100},{3,33},{4,98},{5,39},{6,96},{7,37},{8,110},... | collective-permute-start | bytes 196616 | tf_op jit(solution)/shard_map/ppermute | solution.py:213
  69.0 8.5 %collective-permute-start.26 = (f32[64,256]{1,0:T(8,128)S(1)}, f32[64,256]{1,0:T(8,128)S(1)}, u32[]{:S(2)}, u32[]{:S(2)}) collective-permute-start(f32[64,256]{1,0:T(8,128)S(1)} %get-tuple-element.37.refs_0_), channel_id=1, source_target_pairs={{0,96},{1,33},{2,98},{3,35},{4,100},{5,37},{6,102},{7,39},{8,104},... | collective-permute-start | bytes 196616 | tf_op jit(solution)/shard_map/ppermute | solution.py:213
  71.6 8.0 %collective-permute-start.25 = (f32[64,256]{1,0:T(8,128)S(1)}, f32[64,256]{1,0:T(8,128)S(1)}, u32[]{:S(2)}, u32[]{:S(2)}) collective-permute-start(f32[64,256]{1,0:T(8,128)S(1)} %get-tuple-element.37.refs_0_), channel_id=1, source_target_pairs={{0,30},{1,11},{2,28},{3,9},{4,26},{5,15},{6,24},{7,13},{8,22},{9,3... | collective-permute-start | bytes 196616 | tf_op jit(solution)/shard_map/ppermute | solution.py:213
  71.7 10.2 %collective-permute-start.24 = (f32[64,256]{1,0:T(8,128)S(1)}, f32[64,256]{1,0:T(8,128)S(1)}, u32[]{:S(2)}, u32[]{:S(2)}) collective-permute-start(f32[64,256]{1,0:T(8,128)S(1)} %get-tuple-element.37.refs_0_), channel_id=1, source_target_pairs={{0,24},{1,9},{2,26},{3,11},{4,28},{5,13},{6,30},{7,15},{8,16},{9,1... | collective-permute-start | bytes 196616 | tf_op jit(solution)/shard_map/ppermute | solution.py:213
  74.7 7.2 %collective-permute-start.23 = (f32[64,256]{1,0:T(8,128)S(1)}, f32[64,256]{1,0:T(8,128)S(1)}, u32[]{:S(2)}, u32[]{:S(2)}) collective-permute-start(f32[64,256]{1,0:T(8,128)S(1)} %get-tuple-element.37.refs_0_), channel_id=1, source_target_pairs={{0,6},{1,3},{2,4},{3,1},{4,2},{5,7},{6,0},{7,5},{8,14},{9,11},{10,... | collective-permute-start | bytes 196616 | tf_op jit(solution)/shard_map/ppermute | solution.py:213
  77.5 6.5 %collective-permute-start.15 = (f32[64,256]{1,0:T(8,128)S(1)}, f32[64,256]{1,0:T(8,128)S(1)}, u32[]{:S(2)}, u32[]{:S(2)}) collective-permute-start(f32[64,256]{1,0:T(8,128)S(1)} %get-tuple-element.39), channel_id=1, source_target_pairs={{0,2},{1,7},{2,0},{3,5},{4,6},{5,3},{6,4},{7,1},{8,10},{9,15},{10,... | collective-permute-start | bytes 196616 | tf_op jit(solution)/shard_map/ppermute | solution.py:213
  77.5 20.7 %collective-permute-start.21 = (f32[64,256]{1,0:T(8,128)S(1)}, f32[64,256]{1,0:T(8,128)S(1)}, u32[]{:S(2)}, u32[]{:S(2)}) collective-permute-start(f32[64,256]{1,0:T(8,128)S(1)} %get-tuple-element.39), channel_id=1, source_target_pairs={{0,42},{1,127},{2,40},{3,125},{4,46},{5,123},{6,44},{7,121},{8,34}... | collective-permute-start | bytes 196616 | tf_op jit(solution)/shard_map/ppermute | solution.py:213
  79.5 18.6 %collective-permute-start.20 = (f32[64,256]{1,0:T(8,128)S(1)}, f32[64,256]{1,0:T(8,128)S(1)}, u32[]{:S(2)}, u32[]{:S(2)}) collective-permute-start(f32[64,256]{1,0:T(8,128)S(1)} %get-tuple-element.39), channel_id=1, source_target_pairs={{0,40},{1,121},{2,42},{3,123},{4,44},{5,125},{6,46},{7,127},{8,32}... | collective-permute-start | bytes 196616 | tf_op jit(solution)/shard_map/ppermute | solution.py:213
  81.9 16.2 %collective-permute-start.19 = (f32[64,256]{1,0:T(8,128)S(1)}, f32[64,256]{1,0:T(8,128)S(1)}, u32[]{:S(2)}, u32[]{:S(2)}) collective-permute-start(f32[64,256]{1,0:T(8,128)S(1)} %get-tuple-element.39), channel_id=1, source_target_pairs={{0,34},{1,103},{2,32},{3,101},{4,38},{5,99},{6,36},{7,97},{8,42},{... | collective-permute-start | bytes 196616 | tf_op jit(solution)/shard_map/ppermute | solution.py:213
  81.9 13.6 %collective-permute-start.18 = (f32[64,256]{1,0:T(8,128)S(1)}, f32[64,256]{1,0:T(8,128)S(1)}, u32[]{:S(2)}, u32[]{:S(2)}) collective-permute-start(f32[64,256]{1,0:T(8,128)S(1)} %get-tuple-element.39), channel_id=1, source_target_pairs={{0,32},{1,97},{2,34},{3,99},{4,36},{5,101},{6,38},{7,103},{8,40},{... | collective-permute-start | bytes 196616 | tf_op jit(solution)/shard_map/ppermute | solution.py:213
  84.0 4.3 %collective-permute-start.16 = (f32[64,256]{1,0:T(8,128)S(1)}, f32[64,256]{1,0:T(8,128)S(1)}, u32[]{:S(2)}, u32[]{:S(2)}) collective-permute-start(f32[64,256]{1,0:T(8,128)S(1)} %get-tuple-element.39), channel_id=1, source_target_pairs={{0,8},{1,25},{2,10},{3,27},{4,12},{5,29},{6,14},{7,31},{8,0},{9,17... | collective-permute-start | bytes 196616 | tf_op jit(solution)/shard_map/ppermute | solution.py:213
  88.4 5.2 %collective-permute-start.17 = (f32[64,256]{1,0:T(8,128)S(1)}, f32[64,256]{1,0:T(8,128)S(1)}, u32[]{:S(2)}, u32[]{:S(2)}) collective-permute-start(f32[64,256]{1,0:T(8,128)S(1)} %get-tuple-element.39), channel_id=1, source_target_pairs={{0,10},{1,31},{2,8},{3,29},{4,14},{5,27},{6,12},{7,25},{8,2},{9,23... | collective-permute-start | bytes 196616 | tf_op jit(solution)/shard_map/ppermute | solution.py:213
  93.6 12.1 %collective-permute-start.36 = (f32[512,256]{1,0:T(8,128)S(1)}, f32[512,256]{1,0:T(8,128)S(1)}, u32[]{:S(2)}, u32[]{:S(2)}) collective-permute-start(f32[512,256]{1,0:T(8,128)S(1)} %rows.1.refs_0_), channel_id=1, source_target_pairs={{0,42},{1,127},{2,40},{3,125},{4,46},{5,123},{6,44},{7,121},{8,34}... | collective-permute-start | bytes 1572872 | tf_op jit(solution)/shard_map/ppermute | solution.py:213
  95.5 25.5 %collective-permute-start.35 = (f32[512,256]{1,0:T(8,128)S(1)}, f32[512,256]{1,0:T(8,128)S(1)}, u32[]{:S(2)}, u32[]{:S(2)}) collective-permute-start(f32[512,256]{1,0:T(8,128)S(1)} %rows.1.refs_0_), channel_id=1, source_target_pairs={{0,40},{1,121},{2,42},{3,123},{4,44},{5,125},{6,46},{7,127},{8,32}... | collective-permute-start | bytes 1572872 | tf_op jit(solution)/shard_map/ppermute | solution.py:213
  98.2 22.8 %collective-permute-start.22 = (f32[512,256]{1,0:T(8,128)S(1)}, f32[512,256]{1,0:T(8,128)S(1)}, u32[]{:S(2)}, u32[]{:S(2)}) collective-permute-start(f32[512,256]{1,0:T(8,128)S(1)} %constant_dynamic-update-slice_fusion.own), channel_id=1, source_target_pairs={{0,1},{1,0},{2,3},{3,2},{4,5},{5,4},{6,7},{7,6},{8,9},{9,8},{10,11... | collective-permute-start | bytes 1572872 | tf_op jit(solution)/shard_map/ppermute | solution.py:227
  98.3 45.7 %collective-permute-start.34 = (f32[512,256]{1,0:T(8,128)S(1)}, f32[512,256]{1,0:T(8,128)S(1)}, u32[]{:S(2)}, u32[]{:S(2)}) collective-permute-start(f32[512,256]{1,0:T(8,128)S(1)} %rows.1.refs_0_), channel_id=1, source_target_pairs={{0,34},{1,103},{2,32},{3,101},{4,38},{5,99},{6,36},{7,97},{8,42},{... | collective-permute-start | bytes 1572872 | tf_op jit(solution)/shard_map/ppermute | solution.py:213
  98.5 45.6 %collective-permute-start.33 = (f32[512,256]{1,0:T(8,128)S(1)}, f32[512,256]{1,0:T(8,128)S(1)}, u32[]{:S(2)}, u32[]{:S(2)}) collective-permute-start(f32[512,256]{1,0:T(8,128)S(1)} %rows.1.refs_0_), channel_id=1, source_target_pairs={{0,32},{1,97},{2,34},{3,99},{4,36},{5,101},{6,38},{7,103},{8,40},{... | collective-permute-start | bytes 1572872 | tf_op jit(solution)/shard_map/ppermute | solution.py:213
  105.7 38.3 %collective-permute-start.32 = (f32[512,256]{1,0:T(8,128)S(1)}, f32[512,256]{1,0:T(8,128)S(1)}, u32[]{:S(2)}, u32[]{:S(2)}) collective-permute-start(f32[512,256]{1,0:T(8,128)S(1)} %rows.1.refs_0_), channel_id=1, source_target_pairs={{0,10},{1,31},{2,8},{3,29},{4,14},{5,27},{6,12},{7,25},{8,2},{9,23... | collective-permute-start | bytes 1572872 | tf_op jit(solution)/shard_map/ppermute | solution.py:213
  121.0 23.0 %collective-permute-start.31 = (f32[512,256]{1,0:T(8,128)S(1)}, f32[512,256]{1,0:T(8,128)S(1)}, u32[]{:S(2)}, u32[]{:S(2)}) collective-permute-start(f32[512,256]{1,0:T(8,128)S(1)} %rows.1.refs_0_), channel_id=1, source_target_pairs={{0,8},{1,25},{2,10},{3,27},{4,12},{5,29},{6,14},{7,31},{8,0},{9,17... | collective-permute-start | bytes 1572872 | tf_op jit(solution)/shard_map/ppermute | solution.py:213
  121.1 23.0 %collective-permute-start.30 = (f32[512,256]{1,0:T(8,128)S(1)}, f32[512,256]{1,0:T(8,128)S(1)}, u32[]{:S(2)}, u32[]{:S(2)}) collective-permute-start(f32[512,256]{1,0:T(8,128)S(1)} %rows.1.refs_0_), channel_id=1, source_target_pairs={{0,2},{1,7},{2,0},{3,5},{4,6},{5,3},{6,4},{7,1},{8,10},{9,15},{10,... | collective-permute-start | bytes 1572872 | tf_op jit(solution)/shard_map/ppermute | solution.py:213

commit v4 on v3

--- a/solution.py
+++ b/solution.py
@@ -84,10 +84,6 @@
     return pl.CostEstimate(flops=flops, bytes_accessed=nbytes, transcendentals=0)
 
 
-def indexed(ref):
-    return ref[0], ref[1], ref[2]
-
-
 def aligned(i, n):
     return pl.ds(pl.multiple_of(i * n, n), n)
 
@@ -105,42 +101,24 @@
     )(index, *args)
 
 
-def pack_kernel(index, x_ref, lead_ref, *outs):
-    _, j, _ = indexed(index)
-    for m, out in enumerate(outs):
-        out[:, :LEAD] = lead_ref[...]
-        out[:, LEAD:] = x_ref[:, aligned(j ^ m, 256)]
-
-
-def gram_kernel(index, *refs):
-    ins, outs, (lead, columns, gram) = refs[:8], refs[8:16], refs[16:]
-    core, j, k = indexed(index)
-    for m, ref in enumerate(ins):
-        lead[128 * m : 128 * m + 128, :] = ref[:, :LEAD]
-        columns[128 * m : 128 * m + 128, :] = ref[:, LEAD:]
-    square = mtm(lead[:, aligned(j // 2, 128)], lead[:, aligned(core * 2 + j % 2, 128)])
-    for out in outs:
-        out[64:, :128] = square[:64]
-        out[64:, 128:] = square[64:]
-    gram[...] = mtm(lead[...], columns[...])
-    for m, out in enumerate(outs):
-        out[:64, :] = gram[aligned(k ^ m, 64), :]
-
-
-def rows_kernel(index, *refs):
-    _, _, k = indexed(index)
-    for m in range(8):
-        refs[8][aligned(k ^ m, 64), :] = refs[m][...]
+def pack_kernel(index, x_ref, lead_ref, out):
+    for p in range(8):
+        out[p, :, :LEAD] = lead_ref[...]
+        out[p, :, LEAD:] = x_ref[:, 256 * p : 256 * p + 256]
+
+
+def gram_kernel(index, x_ref, out):
+    lead = x_ref[:, :LEAD]
+    gram = mtm(lead, x_ref[:, LEAD:])
+    square = mtm(lead, x_ref[:, aligned(index[0], 256)])
+    for p in range(8):
+        out[p, :64, :] = gram[64 * p : 64 * p + 64]
+        out[p, 64:, :] = square[64 * p : 64 * p + 64]
 
 
 def inverse_kernel(index, own, other, o_ref, a, d):
-    core, j, k = indexed(index)
-    for side, place, ref in ((core, j, own), (1 - core, k, other)):
-        for m in range(8):
-            at = place ^ m
-            columns = aligned(side * 2 + at % 2, 128)
-            a[aligned(at // 2 * 2, 64), columns] = ref[64 * m : 64 * m + 64, :128]
-            a[aligned(at // 2 * 2 + 1, 64), columns] = ref[64 * m : 64 * m + 64, 128:]
+    a[:, aligned(index[0], 256)] = own[...]
+    a[:, aligned(1 - index[0], 256)] = other[...]
     sub = lax.broadcasted_iota(jnp.int32, S8, 0)
     lane = lax.broadcasted_iota(jnp.int32, S8, 1)
     o_ref[...] = jnp.zeros_like(o_ref)
@@ -174,75 +152,66 @@
     return high, (x - high.astype(F32)).astype(jnp.bfloat16)
 
 
-def product_kernel(index, inverse_ref, *refs):
-    parts, (out_ref, lh_ref, ll_ref, buf, sems) = refs[:8], refs[8:]
-    core, j, _ = indexed(index)
+def product_kernel(index, inverse_ref, parts, out_ref, lh_ref, ll_ref, buf, sems):
     lh_ref[...], ll_ref[...] = two(inverse_ref[...])
     dot = lambda x, y: jnp.dot(x, y, preferred_element_type=F32)
     copies = []
-    for m, part in enumerate(parts):
-        xh, xl = two(part[...])
+    for m in range(8):
+        xh, xl = two(parts[m])
         for r, n in ((0, 256), (256, 512)):
             lh, ll = lh_ref[r : r + 256, :n], ll_ref[r : r + 256, :n]
             y = dot(lh, xh[:n]) + (dot(lh, xl[:n]) + dot(ll, xh[:n]))
-            ids = core * 2048 + (j ^ m) * 256 + lax.broadcasted_iota(jnp.int32, y.shape, 1)
+            ids = index[0] * 2048 + m * 256 + lax.broadcasted_iota(jnp.int32, y.shape, 1)
             y = jnp.where(ids >= r + lax.broadcasted_iota(jnp.int32, y.shape, 0), y, 0.0)
             buf[m, r : r + 256, :] = y
-        copies.append(pltpu.make_async_copy(buf.at[m], out_ref.at[:, aligned(j ^ m, 256)], sems.at[m]))
+        copies.append(pltpu.make_async_copy(buf.at[m], out_ref.at[:, pl.ds(256 * m, 256)], sems.at[m]))
         copies[-1].start()
     for copy in copies:
         copy.wait()
 
 
-def flip(kind, mask):
-    pairs = []
+def cubes(kind):
+    groups = {}
     for chip in range(64):
+        at = (chip % 4, chip // 4 % 4, chip // 16)
+        high = sum(a // 2 << i for i, a in enumerate(at))
+        gray = sum((a // 2 ^ a % 2) << i for i, a in enumerate(at))
         for core in range(2):
-            to = [chip % 4, chip // 4 % 4, chip // 16]
-            for axis in range(3):
-                if mask >> axis & 1:
-                    to[axis] ^= (1, 3)[kind ^ core]
-            pairs.append((chip * 2 + core, (to[0] + 4 * to[1] + 16 * to[2]) * 2 + core))
-    return pairs
-
-
-PLUS, MINUS = 0, 1
-
-
-def exchange(kind, send):
-    return [send(m) if m == 0 else lax.ppermute(send(m), ("row", "col"), flip(kind, m)) for m in range(8)]
+            inside, outside = (gray, high) if core == kind else (high, gray)
+            groups.setdefault((core, outside), {})[inside] = chip * 2 + core
+    return [[group[i] for i in range(8)] for _, group in sorted(groups.items())]
+
+
+PLUS, MINUS = cubes(0), cubes(1)
+
+
+def exchange(x, groups):
+    return lax.all_to_all(x, ("row", "col"), 0, 0, axis_index_groups=groups)
 
 
 def body(contributions, valid_rows):
     blocks, height, width = contributions.shape
     core = lax.axis_index("col")
-    row = lax.axis_index("row")
-    gray, high = 0, 0
-    for axis, at in enumerate((row % 4, row // 4 % 4, row // 16)):
-        high += at // 2 << axis
-        gray += (at // 2 ^ at % 2) << axis
-    index = jnp.stack([core, jnp.where(core == 0, gray, high), jnp.where(core == 0, high, gray)]).astype(jnp.int32)
+    index = core.reshape(1)
 
     def across(x):
         return lax.ppermute(x, "col", [(0, 1), (1, 0)])
+
+    def copies(x):
+        return jnp.broadcast_to(x[None], (8, *x.shape))
 
     live = jnp.arange(height, dtype=jnp.int32)[None, :] < valid_rows[:, None]
     frontal = jnp.where(live[:, :, None], contributions, 0.0).reshape(blocks * height, width)
     own = frontal[:, :LEAD]
     lead = jnp.where(core == 0, own, across(own))
-    packed = call(pack_kernel, (vmem(128, 768),) * 8, index, (frontal, lead), name="pack")
-    packed = exchange(PLUS, lambda m: packed[m])
-    scratch = (pltpu.VMEM((1024, LEAD), F32), pltpu.VMEM((1024, 256), F32), pltpu.VMEM((LEAD, 256), F32))
-    grams = call(gram_kernel, (vmem(128, 256),) * 8, index, packed, 1 << 30, 4 << 20, scratch, name="gram")
-    g = exchange(MINUS, lambda m: grams[m])
-    mine = ((g[0] + g[1]) + (g[2] + g[3])) + ((g[4] + g[5]) + (g[6] + g[7]))
-    rest, square = mine[:64], mine[64:]
-    square = jnp.concatenate(exchange(PLUS, lambda m: square), axis=0)
-    rest = exchange(MINUS, lambda m: rest)
-    rest = call(rows_kernel, vmem(LEAD, 256), index, rest, name="rows")
+    packed = exchange(call(pack_kernel, vmem(8, 128, 768), index, (frontal, lead), name="pack"), PLUS)
+    grams = call(gram_kernel, vmem(8, 128, 256), index, (packed.reshape(1024, 768),), 1 << 30, 4 << 20, name="gram")
+    mine = jnp.sum(exchange(grams, MINUS), axis=0)
+    whole = exchange(copies(mine), MINUS)
+    rest, square = whole[:, :64].reshape(LEAD, 256), whole[:, 64:].reshape(LEAD, 256)
+    parts = exchange(copies(rest), PLUS)
     scratch = (pltpu.VMEM((LEAD, LEAD), F32), pltpu.VMEM((128, 128), F32))
     inverse = call(inverse_kernel, vmem(LEAD, LEAD), index, (square, across(square)), 20 * 10**9, 2 << 20, scratch, name="inverse")
-    parts = exchange(PLUS, lambda m: rest)
     scratch = (
         pltpu.VMEM((LEAD, LEAD), jnp.bfloat16),
         pltpu.VMEM((LEAD, LEAD), jnp.bfloat16),
@@ -250,7 +219,7 @@
         pltpu.SemaphoreType.DMA((8,)),
     )
     spec = pl.BlockSpec(memory_space=pl.ANY)
-    return call(product_kernel, vmem(LEAD, width), index, (inverse, *parts), 3 << 30, 9 << 20, scratch, spec, "product")
+    return call(product_kernel, vmem(LEAD, width), index, (inverse, parts), 3 << 30, 9 << 20, scratch, spec, "product")
 
 
 def solution(mesh):

time: 149 us -> 118 us (0.79)
  blocking collectives: 0 us -> 66.8 us
  starting transfers between devices: 59.8 us -> 4.9 us
  waiting for transfers between devices: 55.8 us -> 10.5 us
  local copies, waits for them, and re-layouts: 0.08 us -> 2.57 us
    all_to_all x0 -> x3, blocking collectives: none -> 66.8 us  [exchange(): return lax.all_to_all(x, ('row', 'col'), 0, 0, axis_index_groups=groups)]
    ppermute x35 -> x0, starting transfers between devices: 59.6 us -> none  [exchange(): lax.ppermute(send(m), ('row', 'col'), flip(kind, m))]
    ppermute x35 -> x0, waiting for transfers between devices: 54.5 us -> none  [exchange(): lax.ppermute(send(m), ('row', 'col'), flip(kind, m))]
    all_to_all x0 -> x1, waiting for transfers between devices: none -> 7.05 us  [exchange(): return lax.all_to_all(x, ('row', 'col'), 0, 0, axis_index_groups=groups)]
    all_to_all x0 -> x1, starting transfers between devices: none -> 4.55 us  [exchange(): return lax.all_to_all(x, ('row', 'col'), 0, 0, axis_index_groups=groups)]
    broadcast_in_dim x0 -> x2, local copies, waits for them, and re-layouts: none -> 2.46 us  [copies(): return jnp.broadcast_to(x[None], (8, *x.shape))]
    ppermute x2, waiting for transfers between devices: 1.31 us -> 3.41 us  [across(): return lax.ppermute(x, 'col', [(0, 1), (1, 0)])]
    pallas_call x5 -> x4, Pallas kernels: 30.4 us -> 30.5 us  [call(): pl.pallas_call(kernel, out_shape=out, in_specs=[pl.BlockSpec(memory_space...]
  transfers between devices with their start and end apart: 37 -> 3, of which waited for: 13 -> 3; matrix products, arithmetic and copies ran while one was open for 0% -> 0% of each run, Pallas kernels for 15% -> 18%
where the time goes in v4:
time: 118 us
  blocking collectives  66.8 us (57%)
  Pallas kernels  30.5 us (26%)
  waiting for transfers between devices  10.5 us (9%)
  starting transfers between devices  4.9 us (4%)
  local copies, waits for them, and re-layouts  2.57 us (2%)
  other arithmetic  1.47 us (1%)
    all_to_all x3, blocking collectives, exchange(): return lax.all_to_all(x, ('row', 'col'), 0, 0, axis_index_groups=groups)  66.8 us
    pallas_call x4, Pallas kernels, call(): pl.pallas_call(kernel, out_shape=out, in_specs=[pl.BlockSpec(memory_space...  30.5 us
    all_to_all x1, waiting for transfers between devices, exchange(): return lax.all_to_all(x, ('row', 'col'), 0, 0, axis_index_groups=groups)  7.05 us
    all_to_all x1, starting transfers between devices, exchange(): return lax.all_to_all(x, ('row', 'col'), 0, 0, axis_index_groups=groups)  4.55 us
    ppermute x2, waiting for transfers between devices, across(): return lax.ppermute(x, 'col', [(0, 1), (1, 0)])  3.41 us
    broadcast_in_dim x2, local copies, waits for them, and re-layouts, copies(): return jnp.broadcast_to(x[None], (8, *x.shape))  2.46 us
  transfers between devices with their start and end apart: 3, of which 3 were waited for; matrix products, arithmetic and copies ran while one was open for 0% of the time, Pallas kernels for 18%

profile of v4, /device:TPU:0, one launch (start us, length us, event | category | flops | bytes accessed | tf_op | source)
XLA Modules:
  0.0 117.6 jit_solution(17089092064860964890)
XLA Ops:
  0.7 1.4 %select_bitcast_fusion.x_ref = f32[128,2048]{1,0:T(8,128)S(1)} fusion(f32[1,128,2048]{2,1,0:T(8,128)} %param.2, pred[128]{0:T(512)(128)(4,1)S(1)} %iota_compare_fusion), kind=kLoop, calls=%fused_computation | loop fusion | flops 262144 | bytes 2097280 | tf_op jit(solution)/shard_map/reshape | solution.py:204
  2.1 0.1 collective-permute-start
  2.2 1.5 %collective-permute-done = f32[128,512]{1,0:T(8,128)S(1)} collective-permute-done((f32[128,512]{1,0:T(8,128)S(1)}, f32[128,512]{1,0:T(8,128)S(1)}, u32[]{:S(2)}, u32[]{:S(2)}) %collective-permute-start) | collective-permute-done | bytes 262176 | tf_op jit(solution)/shard_map/ppermute | solution.py:198
  3.7 0.2 pack.1
  3.9 27.4 %all_to_all.20 = f32[8,128,768]{2,1,0:T(8,128)S(1)} all-to-all(f32[8,128,768]{2,1,0:T(8,128)S(1)} %pack.1), channel_id=1, replica_groups={{0,2,8,10,32,34,40,42},{6,4,14,12,38,36,46,44},{24,26,16,18,56,58,48,50..., dimensions={0} | all-to-all | bytes 6291456 | tf_op jit(solution)/shard_map/all_to_all | solution.py:189
  31.4 3.5 %gram.1 = f32[8,128,256]{2,1,0:T(8,128)S(1)} custom-call(s32[1]{0:T(128)} %bitcast.index, f32[1024,768]{1,0:T(8,128)S(1)} %bitcast.8), custom_call_target="tpu_custom_call" | custom-call | flops 1073741824 | bytes 4194304 | tf_op jit(solution)/shard_map/gram/pallas_call | solution.py:92
  34.8 22.1 %all_to_all.21 = f32[8,128,256]{2,1,0:T(8,128)S(1)} all-to-all(f32[8,128,256]{2,1,0:T(8,128)S(1)} %gram.1), channel_id=1, replica_groups={{0,6,24,30,96,102,120,126},{2,4,26,28,98,100,122,124},{8,14,16,22,104,1..., dimensions={0} | all-to-all | bytes 2097152 | tf_op jit(solution)/shard_map/all_to_all | solution.py:189
  56.9 0.1 reduce_sum.9
  57.0 0.1 broadcast_in_dim.30
  57.1 17.2 %all_to_all.22 = f32[8,128,256]{2,1,0:T(8,128)S(1)} all-to-all(f32[8,128,256]{2,1,0:T(8,128)S(1)} %broadcast_in_dim.30), channel_id=1, replica_groups={{0,6,24,30,96,102,120,126},{2,4,26,28,98,100,122,124},{8,14,16,22,104,1..., dimensions={0} | all-to-all | bytes 2097152 | tf_op jit(solution)/shard_map/all_to_all | solution.py:189
  74.3 0.1 fusion
  74.4 2.4 %broadcast_in_dim.32 = f32[8,512,256]{2,1,0:T(8,128)} broadcast(f32[512,256]{1,0:T(8,128)S(1)} %bitcast.11), dimensions={1,2} | broadcast | bytes 4718592 | tf_op jit(solution)/shard_map/broadcast_in_dim | solution.py:201
  76.8 4.5 %all-to-all-start.3 = ((f32[8,512,256]{2,1,0:T(8,128)}), f32[8,512,256]{2,1,0:T(8,128)}, u32[]{:S(2)}, u32[]{:S(2)}) async-start(f32[8,512,256]{2,1,0:T(8,128)} %broadcast_in_dim.32), calls=%async_computation.3 | async-start | bytes 8388608 | tf_op jit(solution)/shard_map/all_to_all | solution.py:189
  81.4 0.3 collective-permute-start.1
  81.6 1.9 %collective-permute-done.1.other = f32[512,256]{1,0:T(8,128)S(1)} collective-permute-done((f32[512,256]{1,0:T(8,128)S(1)}, f32[512,256]{1,0:T(8,128)S(1)}, u32[]{:S(2)}, u32[]{:S(2)}) %collective-permute-start.1) | collective-permute-done | bytes 524320 | tf_op jit(solution)/shard_map/ppermute | solution.py:198
  83.5 20.7 %inverse.1.inverse_ref = f32[512,512]{1,0:T(8,128)S(1)} custom-call(s32[1]{0:T(128)} %bitcast.index, f32[512,256]{1,0:T(8,128)S(1)} %bitcast.10, f32[512,256]{1,0:T(8,128)S(1)} %collective-permute-done.1.other), custom_call_target="tpu_custom_call" | custom-call | flops 20000000000 | bytes 2097152 | tf_op jit(solution)/shard_map/inverse/pallas_call | solution.py:92
  104.3 7.0 %all-to-all-done.3.parts = f32[8,512,256]{2,1,0:T(8,128)} async-done(((f32[8,512,256]{2,1,0:T(8,128)}), f32[8,512,256]{2,1,0:T(8,128)}, u32[]{:S(2)}, u32[]{:S(2)}) %all-to-all-start.3) | async-done | bytes 4194336 | tf_op jit(solution)/shard_map/all_to_all | solution.py:189
  111.3 6.1 %product.1 = f32[512,2048]{1,0:T(8,128)} custom-call(s32[1]{0:T(128)} %bitcast.index, f32[512,512]{1,0:T(8,128)S(1)} %inverse.1.inverse_ref, f32[8,512,256]{2,1,0:T(8,128)} %all-to-all-done.3.parts), custom_call_target="tpu_custom_call" | custom-call | flops 3221225472 | bytes 9437184 | tf_op jit(solution)/shard_map/product/pallas_call | solution.py:92
  (3 shorter events, 0.1 us)
Async XLA Ops:
  2.1 1.6 %collective-permute-start = (f32[128,512]{1,0:T(8,128)S(1)}, f32[128,512]{1,0:T(8,128)S(1)}, u32[]{:S(2)}, u32[]{:S(2)}) collective-permute-start(f32[128,512]{1,0:T(8,128)S(1)} %slice.12), channel_id=1, source_target_pairs={{0,1},{1,0},{2,3},{3,2},{4,5},{5,4},{6,7},{7,6},{8,9},{9,8},{10,11... | collective-permute-start | bytes 786440 | tf_op jit(solution)/shard_map/ppermute | solution.py:198
  76.8 34.5 %all-to-all-start.3 = ((f32[8,512,256]{2,1,0:T(8,128)}), f32[8,512,256]{2,1,0:T(8,128)}, u32[]{:S(2)}, u32[]{:S(2)}) async-start(f32[8,512,256]{2,1,0:T(8,128)} %broadcast_in_dim.32), calls=%async_computation.3 | async-start | bytes 8388608 | tf_op jit(solution)/shard_map/all_to_all | solution.py:189
  81.4 2.2 %collective-permute-start.1 = (f32[512,256]{1,0:T(8,128)S(1)}, f32[512,256]{1,0:T(8,128)S(1)}, u32[]{:S(2)}, u32[]{:S(2)}) collective-permute-start(f32[512,256]{1,0:T(8,128)S(1)} %bitcast.9), channel_id=1, source_target_pairs={{0,1},{1,0},{2,3},{3,2},{4,5},{5,4},{6,7},{7,6},{8,9},{9,8},{10,11... | collective-permute-start | bytes 1572872 | tf_op jit(solution)/shard_map/ppermute | solution.py:198

commit v5 on v4

--- a/solution.py
+++ b/solution.py
@@ -42,12 +42,25 @@
         F=[sb(E[k],j) for j in range(8)]
         l=[[None]*8 for _ in range(8)]
         inv=[None]*8
+        if k<15:
+            Y1=V[k+1]
+            C=[lb(Y1,8*k+j) for j in range(8)]
+            v1=Y1; e1=E[k+1]
         for j in range(8):
+            if j<7: sq=S[j+1][j]*S[j+1][j]
             inv[j]=1.0/S[j][j]
+            if j<7: S[j+1][j+1]=S[j+1][j+1]-sq*inv[j]
             for i in range(j+1,8):
                 l[i][j]=S[i][j]*inv[j]
                 for m in range(j+1,i+1):
-                    S[i][m]=S[i][m]-l[i][j]*S[m][j]
+                    if not (i==j+1 and m==j+1):
+                        S[i][m]=S[i][m]-l[i][j]*S[m][j]
+            if k<15:
+                c=C[j]*inv[j]
+                v1=v1-c*R[j]
+                e1=e1-c*F[j]
+                for i in range(j+1,8):
+                    C[i]=C[i]-l[i][j]*C[j]
             for i in range(j+1,8):
                 R[i]=R[i]-l[i][j]*R[j]
                 F[i]=F[i]-l[i][j]*F[j]
@@ -56,13 +69,15 @@
             o=jnp.where(sub==j,F[j]*lax.rsqrt(S[j][j]),o)
         out.append(o)
         if k<15:
+            V[k+1]=v1; E[k+1]=e1
+        if k<14:
             W=[R[j]*inv[j] for j in range(8)]
             H=[F[j]*inv[j] for j in range(8)]
             for i in range(7,0,-1):
                 for j in range(i):
                     W[j]=W[j]-l[i][j]*W[i]
                     H[j]=H[j]-l[i][j]*H[i]
-            for m in range(k+1,16):
+            for m in range(k+2,16):
                 Y=V[m]; v=Y; e=E[m]
                 for j in range(7,-1,-1):
                     c=lb(Y,8*k+j)
@@ -77,7 +92,6 @@
 
 
 VMEM = pl.BlockSpec(memory_space=pltpu.VMEM)
-PARAMS = pltpu.CompilerParams(vmem_limit_bytes=40 * 2**20)
 
 
 def cost(flops, nbytes):
@@ -88,23 +102,25 @@
     return pl.ds(pl.multiple_of(i * n, n), n)
 
 
-def call(kernel, out, index, args, flops=0, nbytes=1 << 20, scratch=(), out_specs=None, name=None):
+def call(kernel, out, index, args, flops=0, nbytes=1 << 20, scratch=(), out_specs=None, name=None, limit=12):
     return pl.pallas_call(
         kernel,
         out_shape=out,
         in_specs=[pl.BlockSpec(memory_space=pltpu.SMEM)] + [VMEM] * len(args),
         out_specs=out_specs or jax.tree.map(lambda _: VMEM, out),
         scratch_shapes=list(scratch),
-        compiler_params=PARAMS,
+        compiler_params=pltpu.CompilerParams(vmem_limit_bytes=limit << 20),
         cost_estimate=cost(flops, nbytes),
         name=name,
     )(index, *args)
 
 
-def pack_kernel(index, x_ref, lead_ref, out):
+def pack_kernel(index, x_ref, other_ref, out):
+    live = lax.broadcasted_iota(jnp.int32, (128, LEAD), 0) < index[1]
+    lead = jnp.where(live, jnp.where(index[0] == 0, x_ref[:, :LEAD], other_ref[...]), 0.0)
     for p in range(8):
-        out[p, :, :LEAD] = lead_ref[...]
-        out[p, :, LEAD:] = x_ref[:, 256 * p : 256 * p + 256]
+        out[p, :, :LEAD] = lead
+        out[p, :, LEAD:] = jnp.where(live[:, :256], x_ref[:, 256 * p : 256 * p + 256], 0.0)
 
 
 def gram_kernel(index, x_ref, out):
@@ -173,11 +189,13 @@
 def cubes(kind):
     groups = {}
     for chip in range(64):
-        at = (chip % 4, chip // 4 % 4, chip // 16)
-        high = sum(a // 2 << i for i, a in enumerate(at))
-        gray = sum((a // 2 ^ a % 2) << i for i, a in enumerate(at))
         for core in range(2):
-            inside, outside = (gray, high) if core == kind else (high, gray)
+            inside = outside = 0
+            for axis, at in enumerate((chip % 4, chip // 4 % 4, chip // 16)):
+                bits = (at // 2 ^ at % 2, at // 2)
+                first = kind ^ core ^ (axis == 1)
+                inside += bits[first] << axis
+                outside += bits[1 - first] << axis
             groups.setdefault((core, outside), {})[inside] = chip * 2 + core
     return [[group[i] for i in range(8)] for _, group in sorted(groups.items())]
 
@@ -200,12 +218,11 @@
     def copies(x):
         return jnp.broadcast_to(x[None], (8, *x.shape))
 
-    live = jnp.arange(height, dtype=jnp.int32)[None, :] < valid_rows[:, None]
-    frontal = jnp.where(live[:, :, None], contributions, 0.0).reshape(blocks * height, width)
-    own = frontal[:, :LEAD]
-    lead = jnp.where(core == 0, own, across(own))
-    packed = exchange(call(pack_kernel, vmem(8, 128, 768), index, (frontal, lead), name="pack"), PLUS)
-    grams = call(gram_kernel, vmem(8, 128, 256), index, (packed.reshape(1024, 768),), 1 << 30, 4 << 20, name="gram")
+    raw = contributions.reshape(blocks * height, width)
+    limits = jnp.stack([core, valid_rows[0]])
+    packed = call(pack_kernel, vmem(8, 128, 768), limits, (raw, across(raw[:, :LEAD])), name="pack")
+    packed = exchange(packed, PLUS)
+    grams = call(gram_kernel, vmem(8, 128, 256), index, (packed.reshape(1024, 768),), 1 << 30, 4 << 20, name="gram", limit=24)
     mine = jnp.sum(exchange(grams, MINUS), axis=0)
     whole = exchange(copies(mine), MINUS)
     rest, square = whole[:, :64].reshape(LEAD, 256), whole[:, 64:].reshape(LEAD, 256)
@@ -219,7 +236,7 @@
         pltpu.SemaphoreType.DMA((8,)),
     )
     spec = pl.BlockSpec(memory_space=pl.ANY)
-    return call(product_kernel, vmem(LEAD, width), index, (inverse, parts), 3 << 30, 9 << 20, scratch, spec, "product")
+    return call(product_kernel, vmem(LEAD, width), index, (inverse, parts), 3 << 30, 9 << 20, scratch, spec, "product", 24)
 
 
 def solution(mesh):

time: 118 us -> 118 us (level)
  local copies, waits for them, and re-layouts: 2.57 us -> 4.74 us
  blocking collectives: 66.8 us -> 65 us
  other arithmetic: 1.47 us -> 0.14 us
    all_to_all x3, blocking collectives: 66.8 us -> 65 us  [exchange(): return lax.all_to_all(x, ('row', 'col'), 0, 0, axis_index_groups=groups)]
    all_to_all x1, waiting for transfers between devices: 7.05 us -> 8.78 us  [exchange(): return lax.all_to_all(x, ('row', 'col'), 0, 0, axis_index_groups=groups)]
    reshape x1 -> x0, other arithmetic: 1.36 us -> none  [body(): jnp.where(live[:, :, None], contributions, 0.0)]
    unnamed x0 -> x2, local copies, waits for them, and re-layouts: none -> 1.22 us
  transfers between devices with their start and end apart: 3 -> 3, of which waited for: 3 -> 3; matrix products, arithmetic and copies ran while one was open for 0% -> 0% of each run, Pallas kernels for 18% -> 16%
where the time goes in v5:
time: 118 us; the launch traced here: 117 us
  blocking collectives  65 us (55%)
  Pallas kernels  29.7 us (25%)
  waiting for transfers between devices  11.5 us (10%)
  starting transfers between devices  4.9 us (4%)
  local copies, waits for them, and re-layouts  4.74 us (4%)
    all_to_all x3, blocking collectives, exchange(): return lax.all_to_all(x, ('row', 'col'), 0, 0, axis_index_groups=groups)  65 us
    pallas_call x4, Pallas kernels, call(): pl.pallas_call(kernel, out_shape=out, in_specs=[pl.BlockSpec(memory_space...  29.7 us
    all_to_all x1, waiting for transfers between devices, exchange(): return lax.all_to_all(x, ('row', 'col'), 0, 0, axis_index_groups=groups)  8.78 us
    all_to_all x1, starting transfers between devices, exchange(): return lax.all_to_all(x, ('row', 'col'), 0, 0, axis_index_groups=groups)  4.55 us
    ppermute x2, waiting for transfers between devices, across(): return lax.ppermute(x, 'col', [(0, 1), (1, 0)])  2.69 us
    broadcast_in_dim x2, local copies, waits for them, and re-layouts, copies(): return jnp.broadcast_to(x[None], (8, *x.shape))  2.46 us
  transfers between devices with their start and end apart: 3, of which 3 were waited for; matrix products, arithmetic and copies ran while one was open for 0% of the time, Pallas kernels for 16%

profile of v5, /device:TPU:0, one launch (start us, length us, event | category | flops | bytes accessed | tf_op | source)
XLA Modules:
  0.0 116.8 jit_solution(10068849473480947205)
XLA Ops:
  0.0 1.0 slice.12
  1.0 0.1 collective-permute-start
  1.7 0.1 pad_add_fusion.index
  1.8 0.8 collective-permute-done.other_ref
  2.6 0.0 copy-start
  2.6 1.2 %copy-done = f32[1,128,2048]{2,1,0:T(8,128)S(1)} copy-done((f32[1,128,2048]{2,1,0:T(8,128)S(1)}, f32[1,128,2048]{2,1,0:T(8,128)}, u32[]{:S(2)}) %copy-start) | copy-done | bytes 1048600
  3.8 0.8 pack.1
  4.6 30.1 %all_to_all.20 = f32[8,128,768]{2,1,0:T(8,128)S(1)} all-to-all(f32[8,128,768]{2,1,0:T(8,128)S(1)} %pack.1), channel_id=1, replica_groups={{0,2,24,26,32,34,56,58},{6,4,30,28,38,36,62,60},{8,10,16,18,40,42,48,50..., dimensions={0} | all-to-all | bytes 6291456 | tf_op jit(solution)/shard_map/all_to_all | solution.py:207
  34.7 3.5 %gram.1 = f32[8,128,256]{2,1,0:T(8,128)S(1)} custom-call(s32[1]{0:T(128)} %bitcast.index, f32[1024,768]{1,0:T(8,128)S(1)} %bitcast.5), custom_call_target="tpu_custom_call" | custom-call | flops 1073741824 | bytes 4194304 | tf_op jit(solution)/shard_map/gram/pallas_call | solution.py:106
  38.2 18.9 %all_to_all.21 = f32[8,128,256]{2,1,0:T(8,128)S(1)} all-to-all(f32[8,128,256]{2,1,0:T(8,128)S(1)} %gram.1), channel_id=1, replica_groups={{0,6,8,14,96,102,104,110},{2,4,10,12,98,100,106,108},{24,30,16,22,120,1..., dimensions={0} | all-to-all | bytes 2097152 | tf_op jit(solution)/shard_map/all_to_all | solution.py:207
  57.0 0.1 reduce_sum.9
  57.1 0.1 broadcast_in_dim.6
  57.2 16.0 %all_to_all.22 = f32[8,128,256]{2,1,0:T(8,128)S(1)} all-to-all(f32[8,128,256]{2,1,0:T(8,128)S(1)} %broadcast_in_dim.6), channel_id=1, replica_groups={{0,6,8,14,96,102,104,110},{2,4,10,12,98,100,106,108},{24,30,16,22,120,1..., dimensions={0} | all-to-all | bytes 2097152 | tf_op jit(solution)/shard_map/all_to_all | solution.py:207
  73.2 0.1 fusion
  73.3 2.4 %broadcast_in_dim.15 = f32[8,512,256]{2,1,0:T(8,128)} broadcast(f32[512,256]{1,0:T(8,128)S(1)} %bitcast.10), dimensions={1,2} | broadcast | bytes 4718592 | tf_op jit(solution)/shard_map/broadcast_in_dim | solution.py:219
  75.7 4.5 %all-to-all-start.3 = ((f32[8,512,256]{2,1,0:T(8,128)}), f32[8,512,256]{2,1,0:T(8,128)}, u32[]{:S(2)}, u32[]{:S(2)}) async-start(f32[8,512,256]{2,1,0:T(8,128)} %broadcast_in_dim.15), calls=%async_computation.3 | async-start | bytes 8388608 | tf_op jit(solution)/shard_map/all_to_all | solution.py:207
  80.3 0.3 collective-permute-start.1
  80.5 1.9 %collective-permute-done.1.other = f32[512,256]{1,0:T(8,128)S(1)} collective-permute-done((f32[512,256]{1,0:T(8,128)S(1)}, f32[512,256]{1,0:T(8,128)S(1)}, u32[]{:S(2)}, u32[]{:S(2)}) %collective-permute-start.1) | collective-permute-done | bytes 524320 | tf_op jit(solution)/shard_map/ppermute | solution.py:216
  82.4 19.3 %inverse.1.inverse_ref = f32[512,512]{1,0:T(8,128)S(1)} custom-call(s32[1]{0:T(128)} %bitcast.index, f32[512,256]{1,0:T(8,128)S(1)} %bitcast.9, f32[512,256]{1,0:T(8,128)S(1)} %collective-permute-done.1.other), custom_call_target="tpu_custom_call" | custom-call | flops 20000000000 | bytes 2097152 | tf_op jit(solution)/shard_map/inverse/pallas_call | solution.py:106
  101.7 8.8 %all-to-all-done.3.parts = f32[8,512,256]{2,1,0:T(8,128)} async-done(((f32[8,512,256]{2,1,0:T(8,128)}), f32[8,512,256]{2,1,0:T(8,128)}, u32[]{:S(2)}, u32[]{:S(2)}) %all-to-all-start.3) | async-done | bytes 4194336 | tf_op jit(solution)/shard_map/all_to_all | solution.py:207
  110.5 6.1 %product.1 = f32[512,2048]{1,0:T(8,128)} custom-call(s32[1]{0:T(128)} %bitcast.index, f32[512,512]{1,0:T(8,128)S(1)} %inverse.1.inverse_ref, f32[8,512,256]{2,1,0:T(8,128)} %all-to-all-done.3.parts), custom_call_target="tpu_custom_call" | custom-call | flops 3221225472 | bytes 9437184 | tf_op jit(solution)/shard_map/product/pallas_call | solution.py:106
Async XLA Ops:
  1.0 1.6 %collective-permute-start = (f32[128,512]{1,0:T(8,128)S(1)}, f32[128,512]{1,0:T(8,128)S(1)}, u32[]{:S(2)}, u32[]{:S(2)}) collective-permute-start(f32[128,512]{1,0:T(8,128)S(1)} %slice.12), channel_id=1, source_target_pairs={{0,1},{1,0},{2,3},{3,2},{4,5},{5,4},{6,7},{7,6},{8,9},{9,8},{10,11... | collective-permute-start | bytes 786440 | tf_op jit(solution)/shard_map/ppermute | solution.py:216
  2.6 1.2 %copy-start = (f32[1,128,2048]{2,1,0:T(8,128)S(1)}, f32[1,128,2048]{2,1,0:T(8,128)}, u32[]{:S(2)}) copy-start(f32[1,128,2048]{2,1,0:T(8,128)} %param.2) | copy-start | bytes 3145732
  75.7 34.8 %all-to-all-start.3 = ((f32[8,512,256]{2,1,0:T(8,128)}), f32[8,512,256]{2,1,0:T(8,128)}, u32[]{:S(2)}, u32[]{:S(2)}) async-start(f32[8,512,256]{2,1,0:T(8,128)} %broadcast_in_dim.15), calls=%async_computation.3 | async-start | bytes 8388608 | tf_op jit(solution)/shard_map/all_to_all | solution.py:207
  80.3 2.2 %collective-permute-start.1 = (f32[512,256]{1,0:T(8,128)S(1)}, f32[512,256]{1,0:T(8,128)S(1)}, u32[]{:S(2)}, u32[]{:S(2)}) collective-permute-start(f32[512,256]{1,0:T(8,128)S(1)} %bitcast.8), channel_id=1, source_target_pairs={{0,1},{1,0},{2,3},{3,2},{4,5},{5,4},{6,7},{7,6},{8,9},{9,8},{10,11... | collective-permute-start | bytes 1572872 | tf_op jit(solution)/shard_map/ppermute | solution.py:216

commit v6 on v5

--- a/solution.py
+++ b/solution.py
@@ -132,35 +132,49 @@
         out[p, 64:, :] = square[64 * p : 64 * p + 64]
 
 
-def inverse_kernel(index, own, other, o_ref, a, d):
-    a[:, aligned(index[0], 256)] = own[...]
-    a[:, aligned(1 - index[0], 256)] = other[...]
+def panels(first, d, a, o_ref):
     sub = lax.broadcasted_iota(jnp.int32, S8, 0)
     lane = lax.broadcasted_iota(jnp.int32, S8, 1)
-    o_ref[...] = jnp.zeros_like(o_ref)
+    base = 128 * first
     d[...] = a[0:128, 0:128]
 
-    @pl.loop(0, 4)
+    @pl.loop(0, 2)
     def _(p):
         blocks = chol_inv_128([d[8 * i : 8 * i + 8, :] for i in range(16)], sub, lane)
         for i, block in enumerate(blocks):
             d[8 * i : 8 * i + 8, :] = block
-        for q in range(4):
+        for q in range(2):
 
             @pl.when(p == q)
             def _():
                 lo, hi = 128 * q, 128 * (q + 1)
+                glo, ghi = base + lo, base + hi
                 linv = d[...]
-                if q < 3:
+                if ghi < LEAD:
                     up = mm(linv, a[lo:hi, hi:])
-                    d[...] = a[hi : hi + 128, hi : hi + 128] - mtm(up[:, :128], up[:, :128])
-                    if q < 2:
-                        a[hi:, hi:] = a[hi:, hi:] - mtm(up, up)
-                o_ref[lo:hi, lo:hi] = linv
-                if q > 0:
-                    o_ref[lo:hi, :lo] = mm(linv, o_ref[lo:hi, :lo])
-                if q < 3:
-                    o_ref[hi:, :hi] = o_ref[hi:, :hi] - mtm(up, o_ref[lo:hi, :hi])
+                    left = a[hi:, hi:] - mtm(up, up)
+                    a[hi:, hi:] = left
+                    d[...] = left[:128, :128]
+                o_ref[glo:ghi, glo:ghi] = linv
+                if glo > 0:
+                    o_ref[glo:ghi, :glo] = mm(linv, o_ref[glo:ghi, :glo])
+                if ghi < LEAD:
+                    o_ref[ghi:, :ghi] = o_ref[ghi:, :ghi] - mtm(up, o_ref[glo:ghi, :ghi])
+
+
+def first_kernel(index, own, other, o_ref, left_ref, token, a, d):
+    a[:, aligned(index[0], 256)] = own[...]
+    a[:, aligned(1 - index[0], 256)] = other[...]
+    o_ref[...] = jnp.zeros_like(o_ref)
+    panels(0, d, a, o_ref)
+    left_ref[...] = a[256:, 256:]
+    token[0] = jnp.int32(0)
+
+
+def second_kernel(index, half_ref, left_ref, o_ref, a, d):
+    o_ref[...] = half_ref[...]
+    a[...] = left_ref[...]
+    panels(2, d, a, o_ref)
 
 
 def two(x):
@@ -168,19 +182,20 @@
     return high, (x - high.astype(F32)).astype(jnp.bfloat16)
 
 
-def product_kernel(index, inverse_ref, parts, out_ref, lh_ref, ll_ref, buf, sems):
+def product_kernel(index, inverse_ref, *refs):
+    parts, (out_ref, lh_ref, ll_ref, buf, sems) = refs[:8], refs[8:]
     lh_ref[...], ll_ref[...] = two(inverse_ref[...])
     dot = lambda x, y: jnp.dot(x, y, preferred_element_type=F32)
     copies = []
     for m in range(8):
-        xh, xl = two(parts[m])
+        xh, xl = two(parts[m][...])
         for r, n in ((0, 256), (256, 512)):
             lh, ll = lh_ref[r : r + 256, :n], ll_ref[r : r + 256, :n]
             y = dot(lh, xh[:n]) + (dot(lh, xl[:n]) + dot(ll, xh[:n]))
-            ids = index[0] * 2048 + m * 256 + lax.broadcasted_iota(jnp.int32, y.shape, 1)
+            ids = index[0] * 2048 + (index[1] ^ m) * 256 + lax.broadcasted_iota(jnp.int32, y.shape, 1)
             y = jnp.where(ids >= r + lax.broadcasted_iota(jnp.int32, y.shape, 0), y, 0.0)
             buf[m, r : r + 256, :] = y
-        copies.append(pltpu.make_async_copy(buf.at[m], out_ref.at[:, pl.ds(256 * m, 256)], sems.at[m]))
+        copies.append(pltpu.make_async_copy(buf.at[m], out_ref.at[:, aligned(index[1] ^ m, 256)], sems.at[m]))
         copies[-1].start()
     for copy in copies:
         copy.wait()
@@ -203,6 +218,10 @@
 PLUS, MINUS = cubes(0), cubes(1)
 
 
+def flip(mask):
+    return [(group[i], group[i ^ mask]) for group in PLUS for i in range(8)]
+
+
 def exchange(x, groups):
     return lax.all_to_all(x, ("row", "col"), 0, 0, axis_index_groups=groups)
 
@@ -210,6 +229,7 @@
 def body(contributions, valid_rows):
     blocks, height, width = contributions.shape
     core = lax.axis_index("col")
+    row = lax.axis_index("row")
     index = core.reshape(1)
 
     def across(x):
@@ -226,9 +246,26 @@
     mine = jnp.sum(exchange(grams, MINUS), axis=0)
     whole = exchange(copies(mine), MINUS)
     rest, square = whole[:, :64].reshape(LEAD, 256), whole[:, 64:].reshape(LEAD, 256)
-    parts = exchange(copies(rest), PLUS)
+    def swap(x, mask):
+        return lax.ppermute(x, ("row", "col"), flip(mask))
+
+    near = [swap(rest, mask) for mask in (1, 2, 4)]
+    far = swap(rest, 7)
+    out = (vmem(LEAD, LEAD), vmem(256, 256), jax.ShapeDtypeStruct((1,), jnp.int32))
     scratch = (pltpu.VMEM((LEAD, LEAD), F32), pltpu.VMEM((128, 128), F32))
-    inverse = call(inverse_kernel, vmem(LEAD, LEAD), index, (square, across(square)), 20 * 10**9, 2 << 20, scratch, name="inverse")
+    specs = (VMEM, VMEM, pl.BlockSpec(memory_space=pltpu.SMEM))
+    half, left, token = call(first_kernel, out, index, (square, across(square)), 10**10, 2 << 20, scratch, specs, "first")
+    scratch = (pltpu.VMEM((256, 256), F32), pltpu.VMEM((128, 128), F32))
+    inverse = call(second_kernel, vmem(LEAD, LEAD), index, (half, left), 10**10, 2 << 20, scratch, name="second")
+    zero = token[0].astype(F32)
+    x, y, z = (block + zero for block in near)
+    xy, yz, zx = swap(y, 1), swap(z, 2), swap(x, 4)
+    parts = (rest, near[0], near[1], xy, near[2], zx, yz, far)
+    place = 0
+    for axis, at in enumerate((row % 4, row // 4 % 4, row // 16)):
+        high, gray = at // 2, at // 2 ^ at % 2
+        place += jnp.where((core ^ int(axis == 1)) == 0, gray, high) << axis
+    index = jnp.stack([core, place]).astype(jnp.int32)
     scratch = (
         pltpu.VMEM((LEAD, LEAD), jnp.bfloat16),
         pltpu.VMEM((LEAD, LEAD), jnp.bfloat16),
@@ -236,7 +273,7 @@
         pltpu.SemaphoreType.DMA((8,)),
     )
     spec = pl.BlockSpec(memory_space=pl.ANY)
-    return call(product_kernel, vmem(LEAD, width), index, (inverse, parts), 3 << 30, 9 << 20, scratch, spec, "product", 24)
+    return call(product_kernel, vmem(LEAD, width), index, (inverse, *parts), 3 << 30, 9 << 20, scratch, spec, "product", 24)
 
 
 def solution(mesh):

time: 118 us -> 108 us (0.915)
  waiting for transfers between devices: 11.5 us -> 0.82 us
  starting transfers between devices: 4.9 us -> 8.19 us
  local copies, waits for them, and re-layouts: 4.74 us -> 2.37 us
  Pallas kernels: 29.7 us -> 28.5 us
    all_to_all x1 -> x0, waiting for transfers between devices: 8.78 us -> none  [exchange(): return lax.all_to_all(x, ('row', 'col'), 0, 0, axis_index_groups=groups)]
    ppermute x0 -> x7, starting transfers between devices: none -> 8.02 us  [swap(): return lax.ppermute(x, ('row', 'col'), flip(mask))]
    all_to_all x1 -> x0, starting transfers between devices: 4.55 us -> none  [exchange(): return lax.all_to_all(x, ('row', 'col'), 0, 0, axis_index_groups=groups)]
    broadcast_in_dim x2 -> x1, local copies, waits for them, and re-layouts: 2.46 us -> 0.08 us  [copies(): return jnp.broadcast_to(x[None], (8, *x.shape))]
    ppermute x2, waiting for transfers between devices: 2.69 us -> 0.8 us  [across(): return lax.ppermute(x, 'col', [(0, 1), (1, 0)])]
    pallas_call x4 -> x5, Pallas kernels: 29.7 us -> 28.5 us  [call(): pl.pallas_call(kernel, out_shape=out, in_specs=[pl.BlockSpec(memory_space...]
  transfers between devices with their start and end apart: 3 -> 9, of which waited for: 3 -> 1; matrix products, arithmetic and copies ran while one was open for 0% -> 0% of each run, Pallas kernels for 16% -> 18%
where the time goes in v6:
time: 108 us; the launch traced here: 107 us
  blocking collectives  65 us (60%)
  Pallas kernels  28.5 us (26%)
  starting transfers between devices  8.19 us (8%)
  local copies, waits for them, and re-layouts  2.37 us (2%)
  between operations  1.74 us (2%)
    all_to_all x3, blocking collectives, exchange(): return lax.all_to_all(x, ('row', 'col'), 0, 0, axis_index_groups=groups)  65 us
    pallas_call x5, Pallas kernels, call(): pl.pallas_call(kernel, out_shape=out, in_specs=[pl.BlockSpec(memory_space...  28.5 us
    ppermute x7, starting transfers between devices, swap(): return lax.ppermute(x, ('row', 'col'), flip(mask))  8.02 us
  transfers between devices with their start and end apart: 9, of which 1 were waited for; matrix products, arithmetic and copies ran while one was open for 0% of the time, Pallas kernels for 18%

profile of v6, /device:TPU:0, one launch (start us, length us, event | category | flops | bytes accessed | tf_op | source)
XLA Modules:
  0.0 107.0 jit_solution(12887245304548142339)
XLA Ops:
  0.0 1.0 slice.12
  1.0 0.1 collective-permute-start
  1.7 0.1 pad_add_fusion.1.index
  1.8 0.8 collective-permute-done.other_ref
  2.6 0.0 copy-start
  2.6 1.2 %copy-done = f32[1,128,2048]{2,1,0:T(8,128)S(1)} copy-done((f32[1,128,2048]{2,1,0:T(8,128)S(1)}, f32[1,128,2048]{2,1,0:T(8,128)}, u32[]{:S(2)}) %copy-start) | copy-done | bytes 1048600
  3.8 0.8 pack.1
  4.6 30.1 %all_to_all.15 = f32[8,128,768]{2,1,0:T(8,128)S(1)} all-to-all(f32[8,128,768]{2,1,0:T(8,128)S(1)} %pack.1), channel_id=1, replica_groups={{0,2,24,26,32,34,56,58},{6,4,30,28,38,36,62,60},{8,10,16,18,40,42,48,50..., dimensions={0} | all-to-all | bytes 6291456 | tf_op jit(solution)/shard_map/all_to_all | solution.py:226
  34.7 3.5 %gram.1 = f32[8,128,256]{2,1,0:T(8,128)S(1)} custom-call(s32[1]{0:T(128)} %bitcast.index, f32[1024,768]{1,0:T(8,128)S(1)} %bitcast.7), custom_call_target="tpu_custom_call" | custom-call | flops 1073741824 | bytes 4194304 | tf_op jit(solution)/shard_map/gram/pallas_call | solution.py:106
  38.2 18.9 %all_to_all.16 = f32[8,128,256]{2,1,0:T(8,128)S(1)} all-to-all(f32[8,128,256]{2,1,0:T(8,128)S(1)} %gram.1), channel_id=1, replica_groups={{0,6,8,14,96,102,104,110},{2,4,10,12,98,100,106,108},{24,30,16,22,120,1..., dimensions={0} | all-to-all | bytes 2097152 | tf_op jit(solution)/shard_map/all_to_all | solution.py:226
  57.1 0.1 reduce_sum.9
  57.2 0.1 broadcast_in_dim.2
  57.2 16.0 %all_to_all.17 = f32[8,128,256]{2,1,0:T(8,128)S(1)} all-to-all(f32[8,128,256]{2,1,0:T(8,128)S(1)} %broadcast_in_dim.2), channel_id=1, replica_groups={{0,6,8,14,96,102,104,110},{2,4,10,12,98,100,106,108},{24,30,16,22,120,1..., dimensions={0} | all-to-all | bytes 2097152 | tf_op jit(solution)/shard_map/all_to_all | solution.py:226
  73.3 0.1 fusion
  73.4 0.1 collective-permute-start.1
  73.6 0.1 pad_add_fusion.index
  73.7 0.0 collective-permute-start.8
  73.7 0.1 collective-permute-start.5
  73.8 1.6 %collective-permute-start.3 = (f32[512,256]{1,0:T(8,128)S(1)}, f32[512,256]{1,0:T(8,128)S(1)}, u32[]{:S(2)}, u32[]{:S(2)}) collective-permute-start(f32[512,256]{1,0:T(8,128)S(1)} %bitcast.12), channel_id=1, source_target_pairs={{0,24},{2,26},{24,0},{26,2},{32,56},{34,58},{56,32},{58,34},{6,30}... | collective-permute-start | bytes 1572872 | tf_op jit(solution)/shard_map/ppermute | solution.py:250
  75.4 4.5 %collective-permute-start.2 = (f32[512,256]{1,0:T(8,128)S(1)}, f32[512,256]{1,0:T(8,128)S(1)}, u32[]{:S(2)}, u32[]{:S(2)}) collective-permute-start(f32[512,256]{1,0:T(8,128)S(1)} %bitcast.13), channel_id=1, source_target_pairs={{0,2},{2,0},{24,26},{26,24},{32,34},{34,32},{56,58},{58,56},{6,4},... | collective-permute-start | bytes 1572872 | tf_op jit(solution)/shard_map/ppermute | solution.py:250
  79.9 0.0 collective-permute-done.1.other
  79.9 10.7 %first.1 = (f32[512,512]{1,0:T(8,128)S(1)}, f32[256,256]{1,0:T(8,128)S(1)}, s32[1]{0:T(128)}) custom-call(s32[1]{0:T(128)} %bitcast.index, f32[512,256]{1,0:T(8,128)S(1)} %bitcast.16, f32[512,256]{1,0:T(8,128)S(1)} %collective-permute-done.1.other), custom_call_target="tpu_custom_call" | custom-call | flops 10000000000 | bytes 2097152 | tf_op jit(solution)/shard_map/first/pallas_call | solution.py:106
  91.2 0.0 collective-permute-done.5.refs_4_
  91.2 0.3 collective-permute-start.7
  91.5 0.0 collective-permute-done.3.refs_2_
  91.6 0.1 collective-permute-start.4
  91.7 0.0 collective-permute-done.2.refs_1_
  91.7 1.5 %collective-permute-start.6 = (f32[512,256]{1,0:T(8,128)S(1)}, f32[512,256]{1,0:T(8,128)S(1)}, u32[]{:S(2)}, u32[]{:S(2)}) collective-permute-start(f32[512,256]{1,0:T(8,128)S(1)} %broadcast_add_fusion.1), channel_id=1, source_target_pairs={{0,32},{2,34},{24,56},{26,58},{32,0},{34,2},{56,24},{58,26},{6,38}... | collective-permute-start | bytes 1572872 | tf_op jit(solution)/shard_map/ppermute | solution.py:250
  93.2 9.1 %second.1.inverse_ref = f32[512,512]{1,0:T(8,128)S(1)} custom-call(s32[1]{0:T(128)} %bitcast.index, f32[512,512]{1,0:T(8,128)S(1)} %get-tuple-element.8.half_ref, f32[256,256]{1,0:T(8,128)S(1)} %get-tuple-element.9.left_ref), custom_call_target="tpu_custom_call" | custom-call | flops 10000000000 | bytes 2097152 | tf_op jit(solution)/shard_map/second/pallas_call | solution.py:106
  102.3 0.0 collective-permute-done.8.refs_7_
  102.3 0.0 collective-permute-done.7.refs_6_
  102.3 0.0 collective-permute-done.4.refs_3_
  102.3 0.0 collective-permute-done.6.refs_5_
  102.3 4.5 %product.1 = f32[512,2048]{1,0:T(8,128)} custom-call(s32[2]{0:T(128)S(1)} %pad_add_fusion.index, f32[512,512]{1,0:T(8,128)S(1)} %second.1.inverse_ref, f32[512,256]{1,0:T(8,128)S(1)} %bitcast.14, f32[512,256]{1,0:T(8,128)S(1)} %collective-permute-done.2.refs_1_, f32[512,256]{1,0:T(8,128)S(1)} %collective-permute-done.3.refs_2_, ...), custom_call_target="tpu_custom_call" | custom-call | flops 3221225472 | bytes 9437184 | tf_op jit(solution)/shard_map/product/pallas_call | solution.py:106
  (3 shorter events, 0.1 us)
Async XLA Ops:
  1.0 1.6 %collective-permute-start = (f32[128,512]{1,0:T(8,128)S(1)}, f32[128,512]{1,0:T(8,128)S(1)}, u32[]{:S(2)}, u32[]{:S(2)}) collective-permute-start(f32[128,512]{1,0:T(8,128)S(1)} %slice.12), channel_id=1, source_target_pairs={{0,1},{1,0},{2,3},{3,2},{4,5},{5,4},{6,7},{7,6},{8,9},{9,8},{10,11... | collective-permute-start | bytes 786440 | tf_op jit(solution)/shard_map/ppermute | solution.py:236
  2.6 1.2 %copy-start = (f32[1,128,2048]{2,1,0:T(8,128)S(1)}, f32[1,128,2048]{2,1,0:T(8,128)}, u32[]{:S(2)}) copy-start(f32[1,128,2048]{2,1,0:T(8,128)} %param.2) | copy-start | bytes 3145732
  73.4 6.5 %collective-permute-start.1 = (f32[512,256]{1,0:T(8,128)S(1)}, f32[512,256]{1,0:T(8,128)S(1)}, u32[]{:S(2)}, u32[]{:S(2)}) collective-permute-start(f32[512,256]{1,0:T(8,128)S(1)} %bitcast.15), channel_id=1, source_target_pairs={{0,1},{1,0},{2,3},{3,2},{4,5},{5,4},{6,7},{7,6},{8,9},{9,8},{10,11... | collective-permute-start | bytes 1572872 | tf_op jit(solution)/shard_map/ppermute | solution.py:236
  73.7 28.6 %collective-permute-start.8 = (f32[512,256]{1,0:T(8,128)S(1)}, f32[512,256]{1,0:T(8,128)S(1)}, u32[]{:S(2)}, u32[]{:S(2)}) collective-permute-start(f32[512,256]{1,0:T(8,128)S(1)} %bitcast.10), channel_id=1, source_target_pairs={{0,58},{2,56},{24,34},{26,32},{32,26},{34,24},{56,2},{58,0},{6,60}... | collective-permute-start | bytes 1572872 | tf_op jit(solution)/shard_map/ppermute | solution.py:250
  73.7 17.5 %collective-permute-start.5 = (f32[512,256]{1,0:T(8,128)S(1)}, f32[512,256]{1,0:T(8,128)S(1)}, u32[]{:S(2)}, u32[]{:S(2)}) collective-permute-start(f32[512,256]{1,0:T(8,128)S(1)} %bitcast.11), channel_id=1, source_target_pairs={{0,32},{2,34},{24,56},{26,58},{32,0},{34,2},{56,24},{58,26},{6,38}... | collective-permute-start | bytes 1572872 | tf_op jit(solution)/shard_map/ppermute | solution.py:250
  73.8 17.7 %collective-permute-start.3 = (f32[512,256]{1,0:T(8,128)S(1)}, f32[512,256]{1,0:T(8,128)S(1)}, u32[]{:S(2)}, u32[]{:S(2)}) collective-permute-start(f32[512,256]{1,0:T(8,128)S(1)} %bitcast.12), channel_id=1, source_target_pairs={{0,24},{2,26},{24,0},{26,2},{32,56},{34,58},{56,32},{58,34},{6,30}... | collective-permute-start | bytes 1572872 | tf_op jit(solution)/shard_map/ppermute | solution.py:250
  75.4 16.3 %collective-permute-start.2 = (f32[512,256]{1,0:T(8,128)S(1)}, f32[512,256]{1,0:T(8,128)S(1)}, u32[]{:S(2)}, u32[]{:S(2)}) collective-permute-start(f32[512,256]{1,0:T(8,128)S(1)} %bitcast.13), channel_id=1, source_target_pairs={{0,2},{2,0},{24,26},{26,24},{32,34},{34,32},{56,58},{58,56},{6,4},... | collective-permute-start | bytes 1572872 | tf_op jit(solution)/shard_map/ppermute | solution.py:250
  91.2 11.1 %collective-permute-start.7 = (f32[512,256]{1,0:T(8,128)S(1)}, f32[512,256]{1,0:T(8,128)S(1)}, u32[]{:S(2)}, u32[]{:S(2)}) collective-permute-start(f32[512,256]{1,0:T(8,128)S(1)} %broadcast_add_fusion), channel_id=1, source_target_pairs={{0,24},{2,26},{24,0},{26,2},{32,56},{34,58},{56,32},{58,34},{6,30}... | collective-permute-start | bytes 1572872 | tf_op jit(solution)/shard_map/ppermute | solution.py:250
  91.6 10.7 %collective-permute-start.4 = (f32[512,256]{1,0:T(8,128)S(1)}, f32[512,256]{1,0:T(8,128)S(1)}, u32[]{:S(2)}, u32[]{:S(2)}) collective-permute-start(f32[512,256]{1,0:T(8,128)S(1)} %broadcast_add_fusion.2), channel_id=1, source_target_pairs={{0,2},{2,0},{24,26},{26,24},{32,34},{34,32},{56,58},{58,56},{6,4},... | collective-permute-start | bytes 1572872 | tf_op jit(solution)/shard_map/ppermute | solution.py:250
  91.7 10.6 %collective-permute-start.6 = (f32[512,256]{1,0:T(8,128)S(1)}, f32[512,256]{1,0:T(8,128)S(1)}, u32[]{:S(2)}, u32[]{:S(2)}) collective-permute-start(f32[512,256]{1,0:T(8,128)S(1)} %broadcast_add_fusion.1), channel_id=1, source_target_pairs={{0,32},{2,34},{24,56},{26,58},{32,0},{34,2},{56,24},{58,26},{6,38}... | collective-permute-start | bytes 1572872 | tf_op jit(solution)/shard_map/ppermute | solution.py:250

commit v7 on v6

--- a/solution.py
+++ b/solution.py
@@ -46,24 +46,38 @@
             Y1=V[k+1]
             C=[lb(Y1,8*k+j) for j in range(8)]
             v1=Y1; e1=E[k+1]
-        for j in range(8):
-            if j<7: sq=S[j+1][j]*S[j+1][j]
-            inv[j]=1.0/S[j][j]
-            if j<7: S[j+1][j+1]=S[j+1][j+1]-sq*inv[j]
-            for i in range(j+1,8):
-                l[i][j]=S[i][j]*inv[j]
-                for m in range(j+1,i+1):
-                    if not (i==j+1 and m==j+1):
-                        S[i][m]=S[i][m]-l[i][j]*S[m][j]
-            if k<15:
-                c=C[j]*inv[j]
-                v1=v1-c*R[j]
-                e1=e1-c*F[j]
-                for i in range(j+1,8):
-                    C[i]=C[i]-l[i][j]*C[j]
-            for i in range(j+1,8):
-                R[i]=R[i]-l[i][j]*R[j]
-                F[i]=F[i]-l[i][j]*F[j]
+        for j in range(0,8,2):
+            a,b,c=S[j][j],S[j+1][j],S[j+1][j+1]
+            det=a*c-b*b
+            both=1.0/det
+            inv[j]=1.0/a
+            inv[j+1]=a*both
+            l[j+1][j]=b*inv[j]
+            S[j+1][j+1]=det*inv[j]
+            p={i:S[i][j] for i in range(j+2,8)}
+            q={i:S[i][j+1] for i in range(j+2,8)}
+            r={}
+            near={}
+            for i in range(j+2,min(j+4,8)):
+                for m in range(j+2,i+1):
+                    n=(c*p[i])*p[m]-b*(p[i]*q[m]+q[i]*p[m])+(a*q[i])*q[m] if i!=m else (c*p[i])*p[i]-(b+b)*(p[i]*q[i])+(a*q[i])*q[i]
+                    near[i,m]=S[i][m]-n*both
+            for i in range(j+2,8):
+                l[i][j]=p[i]*inv[j]
+                r[i]=q[i]-l[i][j]*b
+                l[i][j+1]=r[i]*inv[j+1]
+                for m in range(j+2,i+1):
+                    S[i][m]=near[i,m] if (i,m) in near else S[i][m]-l[i][j]*p[m]-l[i][j+1]*r[m]
+            for t in (j,j+1):
+                if k<15:
+                    cc=C[t]*inv[t]
+                    v1=v1-cc*R[t]
+                    e1=e1-cc*F[t]
+                    for i in range(t+1,8):
+                        C[i]=C[i]-l[i][t]*C[t]
+                for i in range(t+1,8):
+                    R[i]=R[i]-l[i][t]*R[t]
+                    F[i]=F[i]-l[i][t]*F[t]
         o=F[0]*lax.rsqrt(S[0][0])
         for j in range(1,8):
             o=jnp.where(sub==j,F[j]*lax.rsqrt(S[j][j]),o)
@@ -115,21 +129,26 @@
     )(index, *args)
 
 
-def pack_kernel(index, x_ref, other_ref, out):
-    live = lax.broadcasted_iota(jnp.int32, (128, LEAD), 0) < index[1]
-    lead = jnp.where(live, jnp.where(index[0] == 0, x_ref[:, :LEAD], other_ref[...]), 0.0)
+def mask_kernel(limits, x_ref, out):
+    live = lax.broadcasted_iota(jnp.int32, out.shape, 0) < limits[1]
+    out[...] = jnp.where(live, x_ref[...], 0.0)
+
+
+def pack_kernel(limits, x_ref, other_ref, out):
+    live = lax.broadcasted_iota(jnp.int32, other_ref.shape, 0) < limits[1]
+    lead = jnp.where(limits[0] == 0, x_ref[:, :LEAD], jnp.where(live, other_ref[...], 0.0))
     for p in range(8):
         out[p, :, :LEAD] = lead
-        out[p, :, LEAD:] = jnp.where(live[:, :256], x_ref[:, 256 * p : 256 * p + 256], 0.0)
-
-
-def gram_kernel(index, x_ref, out):
-    lead = x_ref[:, :LEAD]
-    gram = mtm(lead, x_ref[:, LEAD:])
-    square = mtm(lead, x_ref[:, aligned(index[0], 256)])
+        out[p, :, LEAD:] = x_ref[:, 256 * p : 256 * p + 256]
+
+
+def gram_kernel(index, x_ref, out, right):
+    right[:, :256] = x_ref[:, LEAD:]
+    right[:, 256:] = x_ref[:, aligned(index[0], 256)]
+    gram = mtm(x_ref[:, :LEAD], right[...])
     for p in range(8):
-        out[p, :64, :] = gram[64 * p : 64 * p + 64]
-        out[p, 64:, :] = square[64 * p : 64 * p + 64]
+        out[p, :64, :] = gram[64 * p : 64 * p + 64, :256]
+        out[p, 64:, :] = gram[64 * p : 64 * p + 64, 256:]
 
 
 def panels(first, d, a, o_ref):
@@ -168,13 +187,7 @@
     o_ref[...] = jnp.zeros_like(o_ref)
     panels(0, d, a, o_ref)
     left_ref[...] = a[256:, 256:]
-    token[0] = jnp.int32(0)
-
-
-def second_kernel(index, half_ref, left_ref, o_ref, a, d):
-    o_ref[...] = half_ref[...]
-    a[...] = left_ref[...]
-    panels(2, d, a, o_ref)
+    token[...] = jnp.zeros_like(token)
 
 
 def two(x):
@@ -182,9 +195,15 @@
     return high, (x - high.astype(F32)).astype(jnp.bfloat16)
 
 
-def product_kernel(index, inverse_ref, *refs):
-    parts, (out_ref, lh_ref, ll_ref, buf, sems) = refs[:8], refs[8:]
-    lh_ref[...], ll_ref[...] = two(inverse_ref[...])
+def second_kernel(index, half_ref, left_ref, high_ref, low_ref, o, a, d):
+    o[...] = half_ref[...]
+    a[...] = left_ref[...]
+    panels(2, d, a, o)
+    high_ref[...], low_ref[...] = two(o[...])
+
+
+def product_kernel(index, lh_ref, ll_ref, *refs):
+    parts, (out_ref, buf, sems) = refs[:8], refs[8:]
     dot = lambda x, y: jnp.dot(x, y, preferred_element_type=F32)
     copies = []
     for m in range(8):
@@ -240,9 +259,11 @@
 
     raw = contributions.reshape(blocks * height, width)
     limits = jnp.stack([core, valid_rows[0]])
-    packed = call(pack_kernel, vmem(8, 128, 768), limits, (raw, across(raw[:, :LEAD])), name="pack")
+    other = across(raw[:, :LEAD])
+    masked = call(mask_kernel, vmem(height, width), limits, (raw,), name="mask")
+    packed = call(pack_kernel, vmem(8, 128, 768), limits, (masked, other), name="pack")
     packed = exchange(packed, PLUS)
-    grams = call(gram_kernel, vmem(8, 128, 256), index, (packed.reshape(1024, 768),), 1 << 30, 4 << 20, name="gram", limit=24)
+    grams = call(gram_kernel, vmem(8, 128, 256), index, (packed.reshape(1024, 768),), 1 << 30, 4 << 20, (pltpu.VMEM((1024, LEAD), F32),), name="gram", limit=24)
     mine = jnp.sum(exchange(grams, MINUS), axis=0)
     whole = exchange(copies(mine), MINUS)
     rest, square = whole[:, :64].reshape(LEAD, 256), whole[:, 64:].reshape(LEAD, 256)
@@ -251,13 +272,12 @@
 
     near = [swap(rest, mask) for mask in (1, 2, 4)]
     far = swap(rest, 7)
-    out = (vmem(LEAD, LEAD), vmem(256, 256), jax.ShapeDtypeStruct((1,), jnp.int32))
+    out = (vmem(LEAD, LEAD), vmem(256, 256), vmem(1, 256))
     scratch = (pltpu.VMEM((LEAD, LEAD), F32), pltpu.VMEM((128, 128), F32))
-    specs = (VMEM, VMEM, pl.BlockSpec(memory_space=pltpu.SMEM))
-    half, left, token = call(first_kernel, out, index, (square, across(square)), 10**10, 2 << 20, scratch, specs, "first")
-    scratch = (pltpu.VMEM((256, 256), F32), pltpu.VMEM((128, 128), F32))
-    inverse = call(second_kernel, vmem(LEAD, LEAD), index, (half, left), 10**10, 2 << 20, scratch, name="second")
-    zero = token[0].astype(F32)
+    half, left, zero = call(first_kernel, out, index, (square, across(square)), 10**10, 2 << 20, scratch, name="first")
+    scratch = (pltpu.VMEM((LEAD, LEAD), F32), pltpu.VMEM((256, 256), F32), pltpu.VMEM((128, 128), F32))
+    out = (jax.ShapeDtypeStruct((LEAD, LEAD), jnp.bfloat16),) * 2
+    inverse = call(second_kernel, out, index, (half, left), 10**10, 2 << 20, scratch, name="second")
     x, y, z = (block + zero for block in near)
     xy, yz, zx = swap(y, 1), swap(z, 2), swap(x, 4)
     parts = (rest, near[0], near[1], xy, near[2], zx, yz, far)
@@ -267,13 +287,11 @@
         place += jnp.where((core ^ int(axis == 1)) == 0, gray, high) << axis
     index = jnp.stack([core, place]).astype(jnp.int32)
     scratch = (
-        pltpu.VMEM((LEAD, LEAD), jnp.bfloat16),
-        pltpu.VMEM((LEAD, LEAD), jnp.bfloat16),
         pltpu.VMEM((8, LEAD, 256), F32),
         pltpu.SemaphoreType.DMA((8,)),
     )
     spec = pl.BlockSpec(memory_space=pl.ANY)
-    return call(product_kernel, vmem(LEAD, width), index, (inverse, *parts), 3 << 30, 9 << 20, scratch, spec, "product", 24)
+    return call(product_kernel, vmem(LEAD, width), index, (*inverse, *parts), 3 << 30, 9 << 20, scratch, spec, "product", 24)
 
 
 def solution(mesh):

time: 108 us -> 108 us (level)
  starting transfers between devices: 8.19 us -> 9.7 us
  Pallas kernels: 28.5 us -> 27.4 us
    ppermute x7, starting transfers between devices: 8.02 us -> 9.53 us  [swap(): return lax.ppermute(x, ('row', 'col'), flip(mask))]
    pallas_call x5 -> x6, Pallas kernels: 28.5 us -> 27.4 us  [call(): pl.pallas_call(kernel, out_shape=out, in_specs=[pl.BlockSpec(memory_space...]
where the time goes in v7:
time: 108 us; the launch traced here: 106 us
  blocking collectives  65 us (60%)
  Pallas kernels  27.4 us (25%)
  starting transfers between devices  9.7 us (9%)
  local copies, waits for them, and re-layouts  2.37 us (2%)
  between operations  1.11 us (1%)
    all_to_all x3, blocking collectives, exchange(): return lax.all_to_all(x, ('row', 'col'), 0, 0, axis_index_groups=groups)  65 us
    pallas_call x6, Pallas kernels, call(): pl.pallas_call(kernel, out_shape=out, in_specs=[pl.BlockSpec(memory_space...  27.4 us
    ppermute x7, starting transfers between devices, swap(): return lax.ppermute(x, ('row', 'col'), flip(mask))  9.53 us
  transfers between devices with their start and end apart: 9, of which 1 were waited for; matrix products, arithmetic and copies ran while one was open for 0% of the time, Pallas kernels for 18%

profile of v7, /device:TPU:0, one launch (start us, length us, event | category | flops | bytes accessed | tf_op | source)
XLA Modules:
  0.0 106.5 jit_solution(398417938827453387)
XLA Ops:
  0.0 1.0 slice.12
  1.0 0.1 collective-permute-start
  1.7 0.1 pad_add_fusion.1.limits
  1.8 0.0 copy-start
  1.8 1.2 %copy-done = f32[1,128,2048]{2,1,0:T(8,128)S(1)} copy-done((f32[1,128,2048]{2,1,0:T(8,128)S(1)}, f32[1,128,2048]{2,1,0:T(8,128)}, u32[]{:S(2)}) %copy-start) | copy-done | bytes 1048600
  3.0 0.6 mask.1.x_ref
  3.6 0.0 collective-permute-done.other_ref
  3.6 0.8 pack.1
  4.4 30.1 %all_to_all.15 = f32[8,128,768]{2,1,0:T(8,128)S(1)} all-to-all(f32[8,128,768]{2,1,0:T(8,128)S(1)} %pack.1), channel_id=1, replica_groups={{0,2,24,26,32,34,56,58},{6,4,30,28,38,36,62,60},{8,10,16,18,40,42,48,50..., dimensions={0} | all-to-all | bytes 6291456 | tf_op jit(solution)/shard_map/all_to_all | solution.py:245
  34.5 3.5 %gram.1 = f32[8,128,256]{2,1,0:T(8,128)S(1)} custom-call(s32[1]{0:T(128)} %bitcast.index, f32[1024,768]{1,0:T(8,128)S(1)} %bitcast.7), custom_call_target="tpu_custom_call" | custom-call | flops 1073741824 | bytes 4194304 | tf_op jit(solution)/shard_map/gram/pallas_call | solution.py:120
  38.0 18.9 %all_to_all.16 = f32[8,128,256]{2,1,0:T(8,128)S(1)} all-to-all(f32[8,128,256]{2,1,0:T(8,128)S(1)} %gram.1), channel_id=1, replica_groups={{0,6,8,14,96,102,104,110},{2,4,10,12,98,100,106,108},{24,30,16,22,120,1..., dimensions={0} | all-to-all | bytes 2097152 | tf_op jit(solution)/shard_map/all_to_all | solution.py:245
  56.9 0.1 reduce_sum.9
  57.0 0.1 broadcast_in_dim.2
  57.1 16.0 %all_to_all.17 = f32[8,128,256]{2,1,0:T(8,128)S(1)} all-to-all(f32[8,128,256]{2,1,0:T(8,128)S(1)} %broadcast_in_dim.2), channel_id=1, replica_groups={{0,6,8,14,96,102,104,110},{2,4,10,12,98,100,106,108},{24,30,16,22,120,1..., dimensions={0} | all-to-all | bytes 2097152 | tf_op jit(solution)/shard_map/all_to_all | solution.py:245
  73.1 0.1 fusion
  73.2 0.1 collective-permute-start.1
  73.5 0.1 pad_add_fusion.index
  73.5 0.0 collective-permute-start.8
  73.6 0.1 collective-permute-start.5
  73.7 1.6 %collective-permute-start.3 = (f32[512,256]{1,0:T(8,128)S(1)}, f32[512,256]{1,0:T(8,128)S(1)}, u32[]{:S(2)}, u32[]{:S(2)}) collective-permute-start(f32[512,256]{1,0:T(8,128)S(1)} %bitcast.12), channel_id=1, source_target_pairs={{0,24},{2,26},{24,0},{26,2},{32,56},{34,58},{56,32},{58,34},{6,30}... | collective-permute-start | bytes 1572872 | tf_op jit(solution)/shard_map/ppermute | solution.py:271
  75.2 4.5 %collective-permute-start.2 = (f32[512,256]{1,0:T(8,128)S(1)}, f32[512,256]{1,0:T(8,128)S(1)}, u32[]{:S(2)}, u32[]{:S(2)}) collective-permute-start(f32[512,256]{1,0:T(8,128)S(1)} %bitcast.13), channel_id=1, source_target_pairs={{0,2},{2,0},{24,26},{26,24},{32,34},{34,32},{56,58},{58,56},{6,4},... | collective-permute-start | bytes 1572872 | tf_op jit(solution)/shard_map/ppermute | solution.py:271
  79.7 0.0 collective-permute-done.1.other
  79.7 9.5 %first.1 = (f32[512,512]{1,0:T(8,128)S(1)}, f32[256,256]{1,0:T(8,128)S(1)}, f32[1,256]{1,0:T(1,128)S(1)}) custom-call(s32[1]{0:T(128)} %bitcast.index, f32[512,256]{1,0:T(8,128)S(1)} %bitcast.16, f32[512,256]{1,0:T(8,128)S(1)} %collective-permute-done.1.other), custom_call_target="tpu_custom_call" | custom-call | flops 10000000000 | bytes 2097152 | tf_op jit(solution)/shard_map/first/pallas_call | solution.py:120
  89.2 0.0 collective-permute-done.5.refs_4_
  89.2 0.0 collective-permute-done.3.refs_2_
  89.2 0.0 collective-permute-done.2.refs_1_
  89.3 0.1 broadcast_add_fusion
  89.4 0.3 collective-permute-start.7
  89.7 3.1 %collective-permute-start.6 = (f32[512,256]{1,0:T(8,128)S(1)}, f32[512,256]{1,0:T(8,128)S(1)}, u32[]{:S(2)}, u32[]{:S(2)}) collective-permute-start(f32[512,256]{1,0:T(8,128)S(1)} %get-tuple-element.18), channel_id=1, source_target_pairs={{0,32},{2,34},{24,56},{26,58},{32,0},{34,2},{56,24},{58,26},{6,38}... | collective-permute-start | bytes 1572872 | tf_op jit(solution)/shard_map/ppermute | solution.py:271
  92.7 0.0 collective-permute-start.4
  92.7 8.5 %second.1 = (bf16[512,512]{1,0:T(8,128)(2,1)S(1)}, bf16[512,512]{1,0:T(8,128)(2,1)S(1)}) custom-call(s32[1]{0:T(128)} %bitcast.index, f32[512,512]{1,0:T(8,128)S(1)} %get-tuple-element.10.half_ref, f32[256,256]{1,0:T(8,128)S(1)} %get-tuple-element.11.left_ref), custom_call_target="tpu_custom_call" | custom-call | flops 10000000000 | bytes 2097152 | tf_op jit(solution)/shard_map/second/pallas_call | solution.py:120
  101.3 0.0 collective-permute-done.8.refs_7_
  101.3 0.0 collective-permute-done.7.refs_6_
  101.3 0.0 collective-permute-done.6.refs_5_
  101.3 0.6 collective-permute-done.4.refs_3_
  101.9 4.4 %product.1 = f32[512,2048]{1,0:T(8,128)} custom-call(s32[2]{0:T(128)S(1)} %pad_add_fusion.index, bf16[512,512]{1,0:T(8,128)(2,1)S(1)} %get-tuple-element.12.lh_ref, bf16[512,512]{1,0:T(8,128)(2,1)S(1)} %get-tuple-element.13.ll_ref, f32[512,256]{1,0:T(8,128)S(1)} %bitcast.14, f32[512,256]{1,0:T(8,128)S(1)} %collective-permute-done.2.refs_1_, ...), custom_call_target="tpu_custom_call" | custom-call | flops 3221225472 | bytes 9437184 | tf_op jit(solution)/shard_map/product/pallas_call | solution.py:120
Async XLA Ops:
  1.0 2.7 %collective-permute-start = (f32[128,512]{1,0:T(8,128)S(1)}, f32[128,512]{1,0:T(8,128)S(1)}, u32[]{:S(2)}, u32[]{:S(2)}) collective-permute-start(f32[128,512]{1,0:T(8,128)S(1)} %slice.12), channel_id=1, source_target_pairs={{0,1},{1,0},{2,3},{3,2},{4,5},{5,4},{6,7},{7,6},{8,9},{9,8},{10,11... | collective-permute-start | bytes 786440 | tf_op jit(solution)/shard_map/ppermute | solution.py:255
  1.8 1.2 %copy-start = (f32[1,128,2048]{2,1,0:T(8,128)S(1)}, f32[1,128,2048]{2,1,0:T(8,128)}, u32[]{:S(2)}) copy-start(f32[1,128,2048]{2,1,0:T(8,128)} %param.2) | copy-start | bytes 3145732
  73.2 6.5 %collective-permute-start.1 = (f32[512,256]{1,0:T(8,128)S(1)}, f32[512,256]{1,0:T(8,128)S(1)}, u32[]{:S(2)}, u32[]{:S(2)}) collective-permute-start(f32[512,256]{1,0:T(8,128)S(1)} %bitcast.15), channel_id=1, source_target_pairs={{0,1},{1,0},{2,3},{3,2},{4,5},{5,4},{6,7},{7,6},{8,9},{9,8},{10,11... | collective-permute-start | bytes 1572872 | tf_op jit(solution)/shard_map/ppermute | solution.py:255
  73.5 27.8 %collective-permute-start.8 = (f32[512,256]{1,0:T(8,128)S(1)}, f32[512,256]{1,0:T(8,128)S(1)}, u32[]{:S(2)}, u32[]{:S(2)}) collective-permute-start(f32[512,256]{1,0:T(8,128)S(1)} %bitcast.10), channel_id=1, source_target_pairs={{0,58},{2,56},{24,34},{26,32},{32,26},{34,24},{56,2},{58,0},{6,60}... | collective-permute-start | bytes 1572872 | tf_op jit(solution)/shard_map/ppermute | solution.py:271
  73.6 15.7 %collective-permute-start.5 = (f32[512,256]{1,0:T(8,128)S(1)}, f32[512,256]{1,0:T(8,128)S(1)}, u32[]{:S(2)}, u32[]{:S(2)}) collective-permute-start(f32[512,256]{1,0:T(8,128)S(1)} %bitcast.11), channel_id=1, source_target_pairs={{0,32},{2,34},{24,56},{26,58},{32,0},{34,2},{56,24},{58,26},{6,38}... | collective-permute-start | bytes 1572872 | tf_op jit(solution)/shard_map/ppermute | solution.py:271
  73.7 15.6 %collective-permute-start.3 = (f32[512,256]{1,0:T(8,128)S(1)}, f32[512,256]{1,0:T(8,128)S(1)}, u32[]{:S(2)}, u32[]{:S(2)}) collective-permute-start(f32[512,256]{1,0:T(8,128)S(1)} %bitcast.12), channel_id=1, source_target_pairs={{0,24},{2,26},{24,0},{26,2},{32,56},{34,58},{56,32},{58,34},{6,30}... | collective-permute-start | bytes 1572872 | tf_op jit(solution)/shard_map/ppermute | solution.py:271
  75.2 14.0 %collective-permute-start.2 = (f32[512,256]{1,0:T(8,128)S(1)}, f32[512,256]{1,0:T(8,128)S(1)}, u32[]{:S(2)}, u32[]{:S(2)}) collective-permute-start(f32[512,256]{1,0:T(8,128)S(1)} %bitcast.13), channel_id=1, source_target_pairs={{0,2},{2,0},{24,26},{26,24},{32,34},{34,32},{56,58},{58,56},{6,4},... | collective-permute-start | bytes 1572872 | tf_op jit(solution)/shard_map/ppermute | solution.py:271
  89.4 11.9 %collective-permute-start.7 = (f32[512,256]{1,0:T(8,128)S(1)}, f32[512,256]{1,0:T(8,128)S(1)}, u32[]{:S(2)}, u32[]{:S(2)}) collective-permute-start(f32[512,256]{1,0:T(8,128)S(1)} %get-tuple-element.17), channel_id=1, source_target_pairs={{0,24},{2,26},{24,0},{26,2},{32,56},{34,58},{56,32},{58,34},{6,30}... | collective-permute-start | bytes 1572872 | tf_op jit(solution)/shard_map/ppermute | solution.py:271
  89.7 11.7 %collective-permute-start.6 = (f32[512,256]{1,0:T(8,128)S(1)}, f32[512,256]{1,0:T(8,128)S(1)}, u32[]{:S(2)}, u32[]{:S(2)}) collective-permute-start(f32[512,256]{1,0:T(8,128)S(1)} %get-tuple-element.18), channel_id=1, source_target_pairs={{0,32},{2,34},{24,56},{26,58},{32,0},{34,2},{56,24},{58,26},{6,38}... | collective-permute-start | bytes 1572872 | tf_op jit(solution)/shard_map/ppermute | solution.py:271
  92.7 9.2 %collective-permute-start.4 = (f32[512,256]{1,0:T(8,128)S(1)}, f32[512,256]{1,0:T(8,128)S(1)}, u32[]{:S(2)}, u32[]{:S(2)}) collective-permute-start(f32[512,256]{1,0:T(8,128)S(1)} %get-tuple-element.19), channel_id=1, source_target_pairs={{0,2},{2,0},{24,26},{26,24},{32,34},{34,32},{56,58},{58,56},{6,4},... | collective-permute-start | bytes 1572872 | tf_op jit(solution)/shard_map/ppermute | solution.py:271

commit v8 on v7

--- a/solution.py
+++ b/solution.py
@@ -116,36 +116,37 @@
     return pl.ds(pl.multiple_of(i * n, n), n)
 
 
-def call(kernel, out, index, args, flops=0, nbytes=1 << 20, scratch=(), out_specs=None, name=None, limit=12):
+def call(kernel, out, args, flops=0, nbytes=1 << 20, scratch=(), out_specs=None, name=None, limit=12):
     return pl.pallas_call(
         kernel,
         out_shape=out,
-        in_specs=[pl.BlockSpec(memory_space=pltpu.SMEM)] + [VMEM] * len(args),
+        in_specs=[VMEM] * len(args),
         out_specs=out_specs or jax.tree.map(lambda _: VMEM, out),
         scratch_shapes=list(scratch),
         compiler_params=pltpu.CompilerParams(vmem_limit_bytes=limit << 20),
         cost_estimate=cost(flops, nbytes),
         name=name,
-    )(index, *args)
-
-
-def mask_kernel(limits, x_ref, out):
-    live = lax.broadcasted_iota(jnp.int32, out.shape, 0) < limits[1]
-    out[...] = jnp.where(live, x_ref[...], 0.0)
-
-
-def pack_kernel(limits, x_ref, other_ref, out):
-    live = lax.broadcasted_iota(jnp.int32, other_ref.shape, 0) < limits[1]
-    lead = jnp.where(limits[0] == 0, x_ref[:, :LEAD], jnp.where(live, other_ref[...], 0.0))
+    )(*args)
+
+
+def two(x):
+    high = x.astype(jnp.bfloat16)
+    return high, (x - high.astype(F32)).astype(jnp.bfloat16)
+
+
+def pack_kernel(x_ref, lead_ref, out):
     for p in range(8):
-        out[p, :, :LEAD] = lead
+        out[p, :, :LEAD] = lead_ref[...]
         out[p, :, LEAD:] = x_ref[:, 256 * p : 256 * p + 256]
 
 
-def gram_kernel(index, x_ref, out, right):
+def gram_kernel(x_ref, out, right):
     right[:, :256] = x_ref[:, LEAD:]
-    right[:, 256:] = x_ref[:, aligned(index[0], 256)]
-    gram = mtm(x_ref[:, :LEAD], right[...])
+    right[:, 256:] = x_ref[:, aligned(lax.axis_index("col"), 256)]
+    dot = lambda x, y: lax.dot_general(x, y, LEFT, preferred_element_type=F32)
+    xh, xl = two(x_ref[:, :LEAD])
+    yh, yl = two(right[...])
+    gram = dot(xh, yh) + ((dot(xl, yh) + dot(xh, yl)) + dot(xl, yl))
     for p in range(8):
         out[p, :64, :] = gram[64 * p : 64 * p + 64, :256]
         out[p, 64:, :] = gram[64 * p : 64 * p + 64, 256:]
@@ -181,40 +182,51 @@
                     o_ref[ghi:, :ghi] = o_ref[ghi:, :ghi] - mtm(up, o_ref[glo:ghi, :ghi])
 
 
-def first_kernel(index, own, other, o_ref, left_ref, token, a, d):
-    a[:, aligned(index[0], 256)] = own[...]
-    a[:, aligned(1 - index[0], 256)] = other[...]
+def first_kernel(own, other, o_ref, left_ref, token, a, d):
+    core = lax.axis_index("col")
+    a[:, aligned(core, 256)] = own[...]
+    a[:, aligned(1 - core, 256)] = other[...]
     o_ref[...] = jnp.zeros_like(o_ref)
     panels(0, d, a, o_ref)
     left_ref[...] = a[256:, 256:]
     token[...] = jnp.zeros_like(token)
 
 
-def two(x):
-    high = x.astype(jnp.bfloat16)
-    return high, (x - high.astype(F32)).astype(jnp.bfloat16)
-
-
-def second_kernel(index, half_ref, left_ref, high_ref, low_ref, o, a, d):
+def second_kernel(half_ref, left_ref, head_ref, tail_ref, o, a, d):
     o[...] = half_ref[...]
     a[...] = left_ref[...]
     panels(2, d, a, o)
-    high_ref[...], low_ref[...] = two(o[...])
-
-
-def product_kernel(index, lh_ref, ll_ref, *refs):
+    head_ref[:LEAD, :], head_ref[LEAD:, :] = two(o[:, :256])
+    tail_ref[:256, :], tail_ref[256:, :] = two(o[256:, 256:])
+
+
+def place():
+    core, row = lax.axis_index("col"), lax.axis_index("row")
+    x, y, z = row & 3, (row >> 2) & 3, row >> 4
+    gray = lambda at: (at >> 1) ^ (at & 1)
+    first = gray(x) | ((y >> 1) << 1) | (gray(z) << 2)
+    second = (x >> 1) | (gray(y) << 1) | ((z >> 1) << 2)
+    return jnp.where(core == 0, first, second)
+
+
+def product_kernel(head_ref, tail_ref, *refs):
     parts, (out_ref, buf, sems) = refs[:8], refs[8:]
+    mine = place()
+    offset = lax.axis_index("col") * 2048
     dot = lambda x, y: jnp.dot(x, y, preferred_element_type=F32)
     copies = []
-    for m in range(8):
-        xh, xl = two(parts[m][...])
-        for r, n in ((0, 256), (256, 512)):
-            lh, ll = lh_ref[r : r + 256, :n], ll_ref[r : r + 256, :n]
-            y = dot(lh, xh[:n]) + (dot(lh, xl[:n]) + dot(ll, xh[:n]))
-            ids = index[0] * 2048 + (index[1] ^ m) * 256 + lax.broadcasted_iota(jnp.int32, y.shape, 1)
-            y = jnp.where(ids >= r + lax.broadcasted_iota(jnp.int32, y.shape, 0), y, 0.0)
-            buf[m, r : r + 256, :] = y
-        copies.append(pltpu.make_async_copy(buf.at[m], out_ref.at[:, aligned(index[1] ^ m, 256)], sems.at[m]))
+    for m, part in enumerate(parts):
+        xh, xl = two(part[:256])
+        both = dot(head_ref[...], xh)
+        y = both[:LEAD] + (both[LEAD:] + dot(head_ref[:LEAD], xl))
+        xh, xl = two(part[256:])
+        both = dot(tail_ref[...], xh)
+        low = y[256:] + (both[:256] + (both[256:] + dot(tail_ref[:256], xl)))
+        column = offset + (mine ^ m) * 256
+        for r, block in ((0, y[:256]), (256, low)):
+            ids = column + lax.broadcasted_iota(jnp.int32, block.shape, 1)
+            buf[m, r : r + 256, :] = jnp.where(ids >= r + lax.broadcasted_iota(jnp.int32, block.shape, 0), block, 0.0)
+        copies.append(pltpu.make_async_copy(buf.at[m], out_ref.at[:, aligned(mine ^ m, 256)], sems.at[m]))
         copies[-1].start()
     for copy in copies:
         copy.wait()
@@ -248,8 +260,6 @@
 def body(contributions, valid_rows):
     blocks, height, width = contributions.shape
     core = lax.axis_index("col")
-    row = lax.axis_index("row")
-    index = core.reshape(1)
 
     def across(x):
         return lax.ppermute(x, "col", [(0, 1), (1, 0)])
@@ -257,41 +267,35 @@
     def copies(x):
         return jnp.broadcast_to(x[None], (8, *x.shape))
 
+    def swap(x, mask):
+        return lax.ppermute(x, ("row", "col"), flip(mask))
+
     raw = contributions.reshape(blocks * height, width)
-    limits = jnp.stack([core, valid_rows[0]])
     other = across(raw[:, :LEAD])
-    masked = call(mask_kernel, vmem(height, width), limits, (raw,), name="mask")
-    packed = call(pack_kernel, vmem(8, 128, 768), limits, (masked, other), name="pack")
-    packed = exchange(packed, PLUS)
-    grams = call(gram_kernel, vmem(8, 128, 256), index, (packed.reshape(1024, 768),), 1 << 30, 4 << 20, (pltpu.VMEM((1024, LEAD), F32),), name="gram", limit=24)
+    live = jnp.arange(height, dtype=jnp.int32)[:, None] < valid_rows[0]
+    masked = jnp.where(live, raw, 0.0)
+    lead = jnp.where(live, jnp.where(core == 0, raw[:, :LEAD], other), 0.0)
+    packed = exchange(call(pack_kernel, vmem(8, 128, 768), (masked, lead), name="pack"), PLUS)
+    scratch = (pltpu.VMEM((1024, LEAD), F32),)
+    grams = call(gram_kernel, vmem(8, 128, 256), (packed.reshape(1024, 768),), 1 << 30, 4 << 20, scratch, name="gram", limit=24)
     mine = jnp.sum(exchange(grams, MINUS), axis=0)
     whole = exchange(copies(mine), MINUS)
     rest, square = whole[:, :64].reshape(LEAD, 256), whole[:, 64:].reshape(LEAD, 256)
-    def swap(x, mask):
-        return lax.ppermute(x, ("row", "col"), flip(mask))
 
     near = [swap(rest, mask) for mask in (1, 2, 4)]
     far = swap(rest, 7)
     out = (vmem(LEAD, LEAD), vmem(256, 256), vmem(1, 256))
     scratch = (pltpu.VMEM((LEAD, LEAD), F32), pltpu.VMEM((128, 128), F32))
-    half, left, zero = call(first_kernel, out, index, (square, across(square)), 10**10, 2 << 20, scratch, name="first")
+    half, left, zero = call(first_kernel, out, (square, across(square)), 10**10, 2 << 20, scratch, name="first")
     scratch = (pltpu.VMEM((LEAD, LEAD), F32), pltpu.VMEM((256, 256), F32), pltpu.VMEM((128, 128), F32))
-    out = (jax.ShapeDtypeStruct((LEAD, LEAD), jnp.bfloat16),) * 2
-    inverse = call(second_kernel, out, index, (half, left), 10**10, 2 << 20, scratch, name="second")
+    out = (jax.ShapeDtypeStruct((2 * LEAD, 256), jnp.bfloat16), jax.ShapeDtypeStruct((LEAD, 256), jnp.bfloat16))
+    inverse = call(second_kernel, out, (half, left), 10**10, 2 << 20, scratch, name="second")
     x, y, z = (block + zero for block in near)
     xy, yz, zx = swap(y, 1), swap(z, 2), swap(x, 4)
     parts = (rest, near[0], near[1], xy, near[2], zx, yz, far)
-    place = 0
-    for axis, at in enumerate((row % 4, row // 4 % 4, row // 16)):
-        high, gray = at // 2, at // 2 ^ at % 2
-        place += jnp.where((core ^ int(axis == 1)) == 0, gray, high) << axis
-    index = jnp.stack([core, place]).astype(jnp.int32)
-    scratch = (
-        pltpu.VMEM((8, LEAD, 256), F32),
-        pltpu.SemaphoreType.DMA((8,)),
-    )
+    scratch = (pltpu.VMEM((8, LEAD, 256), F32), pltpu.SemaphoreType.DMA((8,)))
     spec = pl.BlockSpec(memory_space=pl.ANY)
-    return call(product_kernel, vmem(LEAD, width), index, (*inverse, *parts), 3 << 30, 9 << 20, scratch, spec, "product", 24)
+    return call(product_kernel, vmem(LEAD, width), (*inverse, *parts), 3 << 30, 9 << 20, scratch, spec, "product", 24)
 
 
 def solution(mesh):

time: 108 us -> 106 us (0.981)
  Pallas kernels: 27.4 us -> 24.5 us
  other arithmetic: 0.32 us -> 2.59 us
  local copies, waits for them, and re-layouts: 2.37 us -> 1.14 us
    pallas_call x6 -> x5, Pallas kernels: 27.4 us -> 24.5 us  [call(): pl.pallas_call(kernel, out_shape=out, in_specs=[VMEM] * len(args), out_sp...]
    select_n x0 -> x2, other arithmetic: none -> 2.4 us  [the longest x1 1.36 us: body(): masked = jnp.where(live, raw, 0.0)]
    unnamed x2 -> x0, local copies, waits for them, and re-layouts: 1.22 us -> none
  transfers between devices with their start and end apart: 9 -> 9, of which waited for: 1 -> 1; matrix products, arithmetic and copies ran while one was open for 0% -> 1% of each run, Pallas kernels for 18% -> 17%
where the time goes in v8:
time: 106 us; the launch traced here: 105 us
  blocking collectives  65 us (61%)
  Pallas kernels  24.5 us (23%)
  starting transfers between devices  9.77 us (9%)
  other arithmetic  2.59 us (2%)
  local copies, waits for them, and re-layouts  1.14 us (1%)
    all_to_all x3, blocking collectives, exchange(): return lax.all_to_all(x, ('row', 'col'), 0, 0, axis_index_groups=groups)  65 us
    pallas_call x5, Pallas kernels, call(): pl.pallas_call(kernel, out_shape=out, in_specs=[VMEM] * len(args), out_sp...  24.5 us
    ppermute x7, starting transfers between devices, swap(): return lax.ppermute(x, ('row', 'col'), flip(mask))  9.6 us
  transfers between devices with their start and end apart: 9, of which 1 were waited for; matrix products, arithmetic and copies ran while one was open for 1% of the time, Pallas kernels for 17%

profile of v8, /device:TPU:0, one launch (start us, length us, event | category | flops | bytes accessed | tf_op | source)
XLA Modules:
  0.0 104.7 jit_solution(13023819855445759521)
XLA Ops:
  0.0 1.0 slice.13
  1.0 0.1 collective-permute-start
  1.7 1.4 %broadcast_select_fusion.x_ref = f32[128,2048]{1,0:T(8,128)S(1)} fusion(pred[128]{0:T(512)(128)(4,1)S(1)} %iota_compare_fusion, f32[1,128,2048]{2,1,0:T(8,128)} %param.2), kind=kLoop, calls=%fused_computation | loop fusion | flops 262144 | bytes 2097280 | tf_op jit(solution)/shard_map/jit(_where)/select_n | solution.py:276
  3.1 0.0 collective-permute-done
  3.1 1.0 select_select_fusion.lead_ref
  4.2 0.2 pack.1
  4.4 30.1 %all_to_all.15 = f32[8,128,768]{2,1,0:T(8,128)S(1)} all-to-all(f32[8,128,768]{2,1,0:T(8,128)S(1)} %pack.1), channel_id=1, replica_groups={{0,2,24,26,32,34,56,58},{6,4,30,28,38,36,62,60},{8,10,16,18,40,42,48,50..., dimensions={0} | all-to-all | bytes 6291456 | tf_op jit(solution)/shard_map/all_to_all | solution.py:257
  34.5 2.4 %gram.1 = f32[8,128,256]{2,1,0:T(8,128)S(1)} custom-call(f32[1024,768]{1,0:T(8,128)S(1)} %bitcast.8), custom_call_target="tpu_custom_call" | custom-call | flops 1073741824 | bytes 4194304 | tf_op jit(solution)/shard_map/gram/pallas_call | solution.py:120
  36.8 18.9 %all_to_all.16 = f32[8,128,256]{2,1,0:T(8,128)S(1)} all-to-all(f32[8,128,256]{2,1,0:T(8,128)S(1)} %gram.1), channel_id=1, replica_groups={{0,6,8,14,96,102,104,110},{2,4,10,12,98,100,106,108},{24,30,16,22,120,1..., dimensions={0} | all-to-all | bytes 2097152 | tf_op jit(solution)/shard_map/all_to_all | solution.py:257
  55.7 0.1 reduce_sum.9
  55.8 0.1 broadcast_in_dim.35
  55.9 16.0 %all_to_all.17 = f32[8,128,256]{2,1,0:T(8,128)S(1)} all-to-all(f32[8,128,256]{2,1,0:T(8,128)S(1)} %broadcast_in_dim.35), channel_id=1, replica_groups={{0,6,8,14,96,102,104,110},{2,4,10,12,98,100,106,108},{24,30,16,22,120,1..., dimensions={0} | all-to-all | bytes 2097152 | tf_op jit(solution)/shard_map/all_to_all | solution.py:257
  71.9 0.1 fusion
  72.0 0.1 collective-permute-start.1
  72.1 0.1 collective-permute-start.8
  72.2 0.1 collective-permute-start.5
  72.3 1.6 %collective-permute-start.3 = (f32[512,256]{1,0:T(8,128)S(1)}, f32[512,256]{1,0:T(8,128)S(1)}, u32[]{:S(2)}, u32[]{:S(2)}) collective-permute-start(f32[512,256]{1,0:T(8,128)S(1)} %bitcast.11), channel_id=1, source_target_pairs={{0,24},{2,26},{24,0},{26,2},{32,56},{34,58},{56,32},{58,34},{6,30}... | collective-permute-start | bytes 1572872 | tf_op jit(solution)/shard_map/ppermute | solution.py:271
  73.9 4.5 %collective-permute-start.2 = (f32[512,256]{1,0:T(8,128)S(1)}, f32[512,256]{1,0:T(8,128)S(1)}, u32[]{:S(2)}, u32[]{:S(2)}) collective-permute-start(f32[512,256]{1,0:T(8,128)S(1)} %bitcast.12), channel_id=1, source_target_pairs={{0,2},{2,0},{24,26},{26,24},{32,34},{34,32},{56,58},{58,56},{6,4},... | collective-permute-start | bytes 1572872 | tf_op jit(solution)/shard_map/ppermute | solution.py:271
  78.4 0.0 collective-permute-done.1.other
  78.4 9.5 %first.1 = (f32[512,512]{1,0:T(8,128)S(1)}, f32[256,256]{1,0:T(8,128)S(1)}, f32[1,256]{1,0:T(1,128)S(1)}) custom-call(f32[512,256]{1,0:T(8,128)S(1)} %bitcast.15, f32[512,256]{1,0:T(8,128)S(1)} %collective-permute-done.1.other), custom_call_target="tpu_custom_call" | custom-call | flops 10000000000 | bytes 2097152 | tf_op jit(solution)/shard_map/first/pallas_call | solution.py:120
  87.8 0.0 collective-permute-done.5.refs_4_
  87.9 0.0 collective-permute-done.3.refs_2_
  87.9 0.0 collective-permute-done.2.refs_1_
  87.9 0.1 broadcast_add_fusion
  88.0 0.3 collective-permute-start.7
  88.3 3.1 %collective-permute-start.6 = (f32[512,256]{1,0:T(8,128)S(1)}, f32[512,256]{1,0:T(8,128)S(1)}, u32[]{:S(2)}, u32[]{:S(2)}) collective-permute-start(f32[512,256]{1,0:T(8,128)S(1)} %get-tuple-element.18), channel_id=1, source_target_pairs={{0,32},{2,34},{24,56},{26,58},{32,0},{34,2},{56,24},{58,26},{6,38}... | collective-permute-start | bytes 1572872 | tf_op jit(solution)/shard_map/ppermute | solution.py:271
  91.4 0.0 collective-permute-start.4
  91.4 8.5 %second.1 = (bf16[1024,256]{1,0:T(8,128)(2,1)S(1)}, bf16[512,256]{1,0:T(8,128)(2,1)S(1)}) custom-call(f32[512,512]{1,0:T(8,128)S(1)} %get-tuple-element.10.half_ref, f32[256,256]{1,0:T(8,128)S(1)} %get-tuple-element.11.left_ref), custom_call_target="tpu_custom_call" | custom-call | flops 10000000000 | bytes 2097152 | tf_op jit(solution)/shard_map/second/pallas_call | solution.py:120
  99.9 0.0 collective-permute-done.8.refs_7_
  99.9 0.0 collective-permute-done.7.refs_6_
  99.9 0.0 collective-permute-done.6.refs_5_
  99.9 0.6 collective-permute-done.4.refs_3_
  100.6 3.9 %product.1 = f32[512,2048]{1,0:T(8,128)} custom-call(bf16[1024,256]{1,0:T(8,128)(2,1)S(1)} %get-tuple-element.12.head_ref, bf16[512,256]{1,0:T(8,128)(2,1)S(1)} %get-tuple-element.13.tail_ref, f32[512,256]{1,0:T(8,128)S(1)} %bitcast.13, f32[512,256]{1,0:T(8,128)S(1)} %collective-permute-done.2.refs_1_, f32[512,256]{1,0:T(8,128)S(1)} %collective-permute-done.3.refs_2_, ...), custom_call_target="tpu_custom_call" | custom-call | flops 3221225472 | bytes 9437184 | tf_op jit(solution)/shard_map/product/pallas_call | solution.py:120
  (1 shorter events, 0.0 us)
Async XLA Ops:
  1.0 2.1 %collective-permute-start = (f32[128,512]{1,0:T(8,128)S(1)}, f32[128,512]{1,0:T(8,128)S(1)}, u32[]{:S(2)}, u32[]{:S(2)}) collective-permute-start(f32[128,512]{1,0:T(8,128)S(1)} %slice.13), channel_id=1, source_target_pairs={{0,1},{1,0},{2,3},{3,2},{4,5},{5,4},{6,7},{7,6},{8,9},{9,8},{10,11... | collective-permute-start | bytes 786440 | tf_op jit(solution)/shard_map/ppermute | solution.py:265
  72.0 6.3 %collective-permute-start.1 = (f32[512,256]{1,0:T(8,128)S(1)}, f32[512,256]{1,0:T(8,128)S(1)}, u32[]{:S(2)}, u32[]{:S(2)}) collective-permute-start(f32[512,256]{1,0:T(8,128)S(1)} %bitcast.14), channel_id=1, source_target_pairs={{0,1},{1,0},{2,3},{3,2},{4,5},{5,4},{6,7},{7,6},{8,9},{9,8},{10,11... | collective-permute-start | bytes 1572872 | tf_op jit(solution)/shard_map/ppermute | solution.py:265
  72.1 27.8 %collective-permute-start.8 = (f32[512,256]{1,0:T(8,128)S(1)}, f32[512,256]{1,0:T(8,128)S(1)}, u32[]{:S(2)}, u32[]{:S(2)}) collective-permute-start(f32[512,256]{1,0:T(8,128)S(1)} %bitcast.9), channel_id=1, source_target_pairs={{0,58},{2,56},{24,34},{26,32},{32,26},{34,24},{56,2},{58,0},{6,60}... | collective-permute-start | bytes 1572872 | tf_op jit(solution)/shard_map/ppermute | solution.py:271
  72.2 15.6 %collective-permute-start.5 = (f32[512,256]{1,0:T(8,128)S(1)}, f32[512,256]{1,0:T(8,128)S(1)}, u32[]{:S(2)}, u32[]{:S(2)}) collective-permute-start(f32[512,256]{1,0:T(8,128)S(1)} %bitcast.10), channel_id=1, source_target_pairs={{0,32},{2,34},{24,56},{26,58},{32,0},{34,2},{56,24},{58,26},{6,38}... | collective-permute-start | bytes 1572872 | tf_op jit(solution)/shard_map/ppermute | solution.py:271
  72.3 15.6 %collective-permute-start.3 = (f32[512,256]{1,0:T(8,128)S(1)}, f32[512,256]{1,0:T(8,128)S(1)}, u32[]{:S(2)}, u32[]{:S(2)}) collective-permute-start(f32[512,256]{1,0:T(8,128)S(1)} %bitcast.11), channel_id=1, source_target_pairs={{0,24},{2,26},{24,0},{26,2},{32,56},{34,58},{56,32},{58,34},{6,30}... | collective-permute-start | bytes 1572872 | tf_op jit(solution)/shard_map/ppermute | solution.py:271
  73.9 14.0 %collective-permute-start.2 = (f32[512,256]{1,0:T(8,128)S(1)}, f32[512,256]{1,0:T(8,128)S(1)}, u32[]{:S(2)}, u32[]{:S(2)}) collective-permute-start(f32[512,256]{1,0:T(8,128)S(1)} %bitcast.12), channel_id=1, source_target_pairs={{0,2},{2,0},{24,26},{26,24},{32,34},{34,32},{56,58},{58,56},{6,4},... | collective-permute-start | bytes 1572872 | tf_op jit(solution)/shard_map/ppermute | solution.py:271
  88.0 11.9 %collective-permute-start.7 = (f32[512,256]{1,0:T(8,128)S(1)}, f32[512,256]{1,0:T(8,128)S(1)}, u32[]{:S(2)}, u32[]{:S(2)}) collective-permute-start(f32[512,256]{1,0:T(8,128)S(1)} %get-tuple-element.17), channel_id=1, source_target_pairs={{0,24},{2,26},{24,0},{26,2},{32,56},{34,58},{56,32},{58,34},{6,30}... | collective-permute-start | bytes 1572872 | tf_op jit(solution)/shard_map/ppermute | solution.py:271
  88.3 11.6 %collective-permute-start.6 = (f32[512,256]{1,0:T(8,128)S(1)}, f32[512,256]{1,0:T(8,128)S(1)}, u32[]{:S(2)}, u32[]{:S(2)}) collective-permute-start(f32[512,256]{1,0:T(8,128)S(1)} %get-tuple-element.18), channel_id=1, source_target_pairs={{0,32},{2,34},{24,56},{26,58},{32,0},{34,2},{56,24},{58,26},{6,38}... | collective-permute-start | bytes 1572872 | tf_op jit(solution)/shard_map/ppermute | solution.py:271
  91.4 9.2 %collective-permute-start.4 = (f32[512,256]{1,0:T(8,128)S(1)}, f32[512,256]{1,0:T(8,128)S(1)}, u32[]{:S(2)}, u32[]{:S(2)}) collective-permute-start(f32[512,256]{1,0:T(8,128)S(1)} %get-tuple-element.19), channel_id=1, source_target_pairs={{0,2},{2,0},{24,26},{26,24},{32,34},{34,32},{56,58},{58,56},{6,4},... | collective-permute-start | bytes 1572872 | tf_op jit(solution)/shard_map/ppermute | solution.py:271

commit v9 on v8

--- a/solution.py
+++ b/solution.py
@@ -30,16 +30,17 @@
     return lax.dot_general(x, y, LEFT, precision=HI, preferred_element_type=F32)
 
 
-def chol_inv_128(V, sub, lane):
+def chol_inv_128(V, sub, lane, u):
     V=list(V)
     E=[jnp.where(lane==sub+8*k,1.0,0.0) for k in range(16)]
     out=[]
     for k in range(16):
         X=V[k]
-        LB=[lb(X,8*k+j) for j in range(8)]
-        S=[[sb(LB[j],i) if i>=j else None for j in range(8)] for i in range(8)]
-        R=[sb(X,j) for j in range(8)]
-        F=[sb(E[k],j) for j in range(8)]
+        u[8*k:8*k+8,:]=X
+        R=[u[pl.ds(8*k+j,8,stride=0),:] for j in range(8)]
+        S=[[lb(R[i],8*k+j) if i>=j else None for j in range(8)] for i in range(8)]
+        u[128+8*k:136+8*k,:]=E[k]
+        F=[u[pl.ds(128+8*k+j,8,stride=0),:] for j in range(8)]
         l=[[None]*8 for _ in range(8)]
         inv=[None]*8
         if k<15:
@@ -152,7 +153,7 @@
         out[p, 64:, :] = gram[64 * p : 64 * p + 64, 256:]
 
 
-def panels(first, d, a, o_ref):
+def panels(first, d, a, o_ref, rows):
     sub = lax.broadcasted_iota(jnp.int32, S8, 0)
     lane = lax.broadcasted_iota(jnp.int32, S8, 1)
     base = 128 * first
@@ -160,7 +161,7 @@
 
     @pl.loop(0, 2)
     def _(p):
-        blocks = chol_inv_128([d[8 * i : 8 * i + 8, :] for i in range(16)], sub, lane)
+        blocks = chol_inv_128([d[8 * i : 8 * i + 8, :] for i in range(16)], sub, lane, rows)
         for i, block in enumerate(blocks):
             d[8 * i : 8 * i + 8, :] = block
         for q in range(2):
@@ -182,20 +183,20 @@
                     o_ref[ghi:, :ghi] = o_ref[ghi:, :ghi] - mtm(up, o_ref[glo:ghi, :ghi])
 
 
-def first_kernel(own, other, o_ref, left_ref, token, a, d):
+def first_kernel(own, other, o_ref, left_ref, token, a, d, rows):
     core = lax.axis_index("col")
     a[:, aligned(core, 256)] = own[...]
     a[:, aligned(1 - core, 256)] = other[...]
     o_ref[...] = jnp.zeros_like(o_ref)
-    panels(0, d, a, o_ref)
+    panels(0, d, a, o_ref, rows)
     left_ref[...] = a[256:, 256:]
     token[...] = jnp.zeros_like(token)
 
 
-def second_kernel(half_ref, left_ref, head_ref, tail_ref, o, a, d):
+def second_kernel(half_ref, left_ref, head_ref, tail_ref, o, a, d, rows):
     o[...] = half_ref[...]
     a[...] = left_ref[...]
-    panels(2, d, a, o)
+    panels(2, d, a, o, rows)
     head_ref[:LEAD, :], head_ref[LEAD:, :] = two(o[:, :256])
     tail_ref[:256, :], tail_ref[256:, :] = two(o[256:, 256:])
 
@@ -274,7 +275,7 @@
     other = across(raw[:, :LEAD])
     live = jnp.arange(height, dtype=jnp.int32)[:, None] < valid_rows[0]
     masked = jnp.where(live, raw, 0.0)
-    lead = jnp.where(live, jnp.where(core == 0, raw[:, :LEAD], other), 0.0)
+    lead = jnp.where(core == 0, masked[:, :LEAD], jnp.where(live, other, 0.0))
     packed = exchange(call(pack_kernel, vmem(8, 128, 768), (masked, lead), name="pack"), PLUS)
     scratch = (pltpu.VMEM((1024, LEAD), F32),)
     grams = call(gram_kernel, vmem(8, 128, 256), (packed.reshape(1024, 768),), 1 << 30, 4 << 20, scratch, name="gram", limit=24)
@@ -285,9 +286,9 @@
     near = [swap(rest, mask) for mask in (1, 2, 4)]
     far = swap(rest, 7)
     out = (vmem(LEAD, LEAD), vmem(256, 256), vmem(1, 256))
-    scratch = (pltpu.VMEM((LEAD, LEAD), F32), pltpu.VMEM((128, 128), F32))
+    scratch = (pltpu.VMEM((LEAD, LEAD), F32), pltpu.VMEM((128, 128), F32), pltpu.VMEM((272, 128), F32))
     half, left, zero = call(first_kernel, out, (square, across(square)), 10**10, 2 << 20, scratch, name="first")
-    scratch = (pltpu.VMEM((LEAD, LEAD), F32), pltpu.VMEM((256, 256), F32), pltpu.VMEM((128, 128), F32))
+    scratch = (pltpu.VMEM((LEAD, LEAD), F32), pltpu.VMEM((256, 256), F32), pltpu.VMEM((128, 128), F32), pltpu.VMEM((272, 128), F32))
     out = (jax.ShapeDtypeStruct((2 * LEAD, 256), jnp.bfloat16), jax.ShapeDtypeStruct((LEAD, 256), jnp.bfloat16))
     inverse = call(second_kernel, out, (half, left), 10**10, 2 << 20, scratch, name="second")
     x, y, z = (block + zero for block in near)

time: 106 us -> 105 us (level)
    pallas_call x5, Pallas kernels: 24.5 us -> 23.5 us  [call(): pl.pallas_call(kernel, out_shape=out, in_specs=[VMEM] * len(args), out_sp...]
  transfers between devices with their start and end apart: 9 -> 9, of which waited for: 1 -> 1; matrix products, arithmetic and copies ran while one was open for 1% -> 1% of each run, Pallas kernels for 17% -> 16%
where the time goes in v9:
time: 105 us; the launch traced here: 104 us
  blocking collectives  65 us (62%)
  Pallas kernels  23.5 us (22%)
  starting transfers between devices  10.3 us (10%)
  other arithmetic  1.64 us (2%)
  waiting for transfers between devices  1.16 us (1%)
  local copies, waits for them, and re-layouts  1.14 us (1%)
    all_to_all x3, blocking collectives, exchange(): return lax.all_to_all(x, ('row', 'col'), 0, 0, axis_index_groups=groups)  65 us
    pallas_call x5, Pallas kernels, call(): pl.pallas_call(kernel, out_shape=out, in_specs=[VMEM] * len(args), out_sp...  23.5 us
    ppermute x7, starting transfers between devices, swap(): return lax.ppermute(x, ('row', 'col'), flip(mask))  10.1 us
  transfers between devices with their start and end apart: 9, of which 1 were waited for; matrix products, arithmetic and copies ran while one was open for 1% of the time, Pallas kernels for 16%

profile of v9, /device:TPU:0, one launch (start us, length us, event | category | flops | bytes accessed | tf_op | source)
XLA Modules:
  0.0 103.7 jit_solution(14727702872086771161)
XLA Ops:
  0.0 1.0 slice.17
  1.0 0.1 collective-permute-start
  1.7 1.4 %broadcast_select_fusion.x_ref = f32[128,2048]{1,0:T(8,128)S(1)} fusion(pred[128]{0:T(512)(128)(4,1)S(1)} %iota_compare_fusion, f32[1,128,2048]{2,1,0:T(8,128)} %param.2), kind=kLoop, calls=%fused_computation | loop fusion | flops 262144 | bytes 2097280 | tf_op jit(solution)/shard_map/jit(_where)/select_n | solution.py:277
  3.1 0.0 collective-permute-done
  3.1 0.1 slice_select_fusion.lead_ref
  3.2 0.2 pack.1
  3.4 30.1 %all_to_all.15 = f32[8,128,768]{2,1,0:T(8,128)S(1)} all-to-all(f32[8,128,768]{2,1,0:T(8,128)S(1)} %pack.1), channel_id=1, replica_groups={{0,2,24,26,32,34,56,58},{6,4,30,28,38,36,62,60},{8,10,16,18,40,42,48,50..., dimensions={0} | all-to-all | bytes 6291456 | tf_op jit(solution)/shard_map/all_to_all | solution.py:258
  33.5 2.4 %gram.1 = f32[8,128,256]{2,1,0:T(8,128)S(1)} custom-call(f32[1024,768]{1,0:T(8,128)S(1)} %bitcast.8), custom_call_target="tpu_custom_call" | custom-call | flops 1073741824 | bytes 4194304 | tf_op jit(solution)/shard_map/gram/pallas_call | solution.py:121
  35.9 18.9 %all_to_all.16 = f32[8,128,256]{2,1,0:T(8,128)S(1)} all-to-all(f32[8,128,256]{2,1,0:T(8,128)S(1)} %gram.1), channel_id=1, replica_groups={{0,6,8,14,96,102,104,110},{2,4,10,12,98,100,106,108},{24,30,16,22,120,1..., dimensions={0} | all-to-all | bytes 2097152 | tf_op jit(solution)/shard_map/all_to_all | solution.py:258
  54.8 0.1 reduce_sum.9
  54.8 0.1 broadcast_in_dim.35
  54.9 16.0 %all_to_all.17 = f32[8,128,256]{2,1,0:T(8,128)S(1)} all-to-all(f32[8,128,256]{2,1,0:T(8,128)S(1)} %broadcast_in_dim.35), channel_id=1, replica_groups={{0,6,8,14,96,102,104,110},{2,4,10,12,98,100,106,108},{24,30,16,22,120,1..., dimensions={0} | all-to-all | bytes 2097152 | tf_op jit(solution)/shard_map/all_to_all | solution.py:258
  71.0 0.1 fusion
  71.1 0.1 collective-permute-start.1
  71.2 0.1 collective-permute-start.8
  71.3 0.1 collective-permute-start.5
  71.3 1.6 %collective-permute-start.3 = (f32[512,256]{1,0:T(8,128)S(1)}, f32[512,256]{1,0:T(8,128)S(1)}, u32[]{:S(2)}, u32[]{:S(2)}) collective-permute-start(f32[512,256]{1,0:T(8,128)S(1)} %bitcast.11), channel_id=1, source_target_pairs={{0,24},{2,26},{24,0},{26,2},{32,56},{34,58},{56,32},{58,34},{6,30}... | collective-permute-start | bytes 1572872 | tf_op jit(solution)/shard_map/ppermute | solution.py:272
  72.9 4.5 %collective-permute-start.2 = (f32[512,256]{1,0:T(8,128)S(1)}, f32[512,256]{1,0:T(8,128)S(1)}, u32[]{:S(2)}, u32[]{:S(2)}) collective-permute-start(f32[512,256]{1,0:T(8,128)S(1)} %bitcast.12), channel_id=1, source_target_pairs={{0,2},{2,0},{24,26},{26,24},{32,34},{34,32},{56,58},{58,56},{6,4},... | collective-permute-start | bytes 1572872 | tf_op jit(solution)/shard_map/ppermute | solution.py:272
  77.4 0.0 collective-permute-done.1.other
  77.4 9.0 %first.1 = (f32[512,512]{1,0:T(8,128)S(1)}, f32[256,256]{1,0:T(8,128)S(1)}, f32[1,256]{1,0:T(1,128)S(1)}) custom-call(f32[512,256]{1,0:T(8,128)S(1)} %bitcast.15, f32[512,256]{1,0:T(8,128)S(1)} %collective-permute-done.1.other), custom_call_target="tpu_custom_call" | custom-call | flops 10000000000 | bytes 2097152 | tf_op jit(solution)/shard_map/first/pallas_call | solution.py:121
  86.4 0.0 collective-permute-done.5.refs_4_
  86.4 0.0 collective-permute-done.3.refs_2_
  86.4 0.0 collective-permute-done.2.refs_1_
  86.4 0.1 broadcast_add_fusion
  86.5 0.3 collective-permute-start.7
  86.8 3.6 %collective-permute-start.6 = (f32[512,256]{1,0:T(8,128)S(1)}, f32[512,256]{1,0:T(8,128)S(1)}, u32[]{:S(2)}, u32[]{:S(2)}) collective-permute-start(f32[512,256]{1,0:T(8,128)S(1)} %get-tuple-element.18), channel_id=1, source_target_pairs={{0,32},{2,34},{24,56},{26,58},{32,0},{34,2},{56,24},{58,26},{6,38}... | collective-permute-start | bytes 1572872 | tf_op jit(solution)/shard_map/ppermute | solution.py:272
  90.4 0.0 collective-permute-start.4
  90.4 8.0 %second.1 = (bf16[1024,256]{1,0:T(8,128)(2,1)S(1)}, bf16[512,256]{1,0:T(8,128)(2,1)S(1)}) custom-call(f32[512,512]{1,0:T(8,128)S(1)} %get-tuple-element.10.half_ref, f32[256,256]{1,0:T(8,128)S(1)} %get-tuple-element.11.left_ref), custom_call_target="tpu_custom_call" | custom-call | flops 10000000000 | bytes 2097152 | tf_op jit(solution)/shard_map/second/pallas_call | solution.py:121
  98.4 0.0 collective-permute-done.8.refs_7_
  98.4 0.0 collective-permute-done.7.refs_6_
  98.5 0.0 collective-permute-done.6.refs_5_
  98.5 1.1 %collective-permute-done.4.refs_3_ = f32[512,256]{1,0:T(8,128)S(1)} collective-permute-done((f32[512,256]{1,0:T(8,128)S(1)}, f32[512,256]{1,0:T(8,128)S(1)}, u32[]{:S(2)}, u32[]{:S(2)}) %collective-permute-start.4) | collective-permute-done | bytes 524320 | tf_op jit(solution)/shard_map/ppermute | solution.py:272
  99.6 3.9 %product.1 = f32[512,2048]{1,0:T(8,128)} custom-call(bf16[1024,256]{1,0:T(8,128)(2,1)S(1)} %get-tuple-element.12.head_ref, bf16[512,256]{1,0:T(8,128)(2,1)S(1)} %get-tuple-element.13.tail_ref, f32[512,256]{1,0:T(8,128)S(1)} %bitcast.13, f32[512,256]{1,0:T(8,128)S(1)} %collective-permute-done.2.refs_1_, f32[512,256]{1,0:T(8,128)S(1)} %collective-permute-done.3.refs_2_, ...), custom_call_target="tpu_custom_call" | custom-call | flops 3221225472 | bytes 9437184 | tf_op jit(solution)/shard_map/product/pallas_call | solution.py:121
  (1 shorter events, 0.0 us)
Async XLA Ops:
  1.0 2.1 %collective-permute-start = (f32[128,512]{1,0:T(8,128)S(1)}, f32[128,512]{1,0:T(8,128)S(1)}, u32[]{:S(2)}, u32[]{:S(2)}) collective-permute-start(f32[128,512]{1,0:T(8,128)S(1)} %slice.17), channel_id=1, source_target_pairs={{0,1},{1,0},{2,3},{3,2},{4,5},{5,4},{6,7},{7,6},{8,9},{9,8},{10,11... | collective-permute-start | bytes 786440 | tf_op jit(solution)/shard_map/ppermute | solution.py:266
  71.1 6.3 %collective-permute-start.1 = (f32[512,256]{1,0:T(8,128)S(1)}, f32[512,256]{1,0:T(8,128)S(1)}, u32[]{:S(2)}, u32[]{:S(2)}) collective-permute-start(f32[512,256]{1,0:T(8,128)S(1)} %bitcast.14), channel_id=1, source_target_pairs={{0,1},{1,0},{2,3},{3,2},{4,5},{5,4},{6,7},{7,6},{8,9},{9,8},{10,11... | collective-permute-start | bytes 1572872 | tf_op jit(solution)/shard_map/ppermute | solution.py:266
  71.2 27.3 %collective-permute-start.8 = (f32[512,256]{1,0:T(8,128)S(1)}, f32[512,256]{1,0:T(8,128)S(1)}, u32[]{:S(2)}, u32[]{:S(2)}) collective-permute-start(f32[512,256]{1,0:T(8,128)S(1)} %bitcast.9), channel_id=1, source_target_pairs={{0,58},{2,56},{24,34},{26,32},{32,26},{34,24},{56,2},{58,0},{6,60}... | collective-permute-start | bytes 1572872 | tf_op jit(solution)/shard_map/ppermute | solution.py:272
  71.3 15.1 %collective-permute-start.5 = (f32[512,256]{1,0:T(8,128)S(1)}, f32[512,256]{1,0:T(8,128)S(1)}, u32[]{:S(2)}, u32[]{:S(2)}) collective-permute-start(f32[512,256]{1,0:T(8,128)S(1)} %bitcast.10), channel_id=1, source_target_pairs={{0,32},{2,34},{24,56},{26,58},{32,0},{34,2},{56,24},{58,26},{6,38}... | collective-permute-start | bytes 1572872 | tf_op jit(solution)/shard_map/ppermute | solution.py:272
  71.3 15.0 %collective-permute-start.3 = (f32[512,256]{1,0:T(8,128)S(1)}, f32[512,256]{1,0:T(8,128)S(1)}, u32[]{:S(2)}, u32[]{:S(2)}) collective-permute-start(f32[512,256]{1,0:T(8,128)S(1)} %bitcast.11), channel_id=1, source_target_pairs={{0,24},{2,26},{24,0},{26,2},{32,56},{34,58},{56,32},{58,34},{6,30}... | collective-permute-start | bytes 1572872 | tf_op jit(solution)/shard_map/ppermute | solution.py:272
  72.9 13.5 %collective-permute-start.2 = (f32[512,256]{1,0:T(8,128)S(1)}, f32[512,256]{1,0:T(8,128)S(1)}, u32[]{:S(2)}, u32[]{:S(2)}) collective-permute-start(f32[512,256]{1,0:T(8,128)S(1)} %bitcast.12), channel_id=1, source_target_pairs={{0,2},{2,0},{24,26},{26,24},{32,34},{34,32},{56,58},{58,56},{6,4},... | collective-permute-start | bytes 1572872 | tf_op jit(solution)/shard_map/ppermute | solution.py:272
  86.5 11.9 %collective-permute-start.7 = (f32[512,256]{1,0:T(8,128)S(1)}, f32[512,256]{1,0:T(8,128)S(1)}, u32[]{:S(2)}, u32[]{:S(2)}) collective-permute-start(f32[512,256]{1,0:T(8,128)S(1)} %get-tuple-element.17), channel_id=1, source_target_pairs={{0,24},{2,26},{24,0},{26,2},{32,56},{34,58},{56,32},{58,34},{6,30}... | collective-permute-start | bytes 1572872 | tf_op jit(solution)/shard_map/ppermute | solution.py:272
  86.8 11.6 %collective-permute-start.6 = (f32[512,256]{1,0:T(8,128)S(1)}, f32[512,256]{1,0:T(8,128)S(1)}, u32[]{:S(2)}, u32[]{:S(2)}) collective-permute-start(f32[512,256]{1,0:T(8,128)S(1)} %get-tuple-element.18), channel_id=1, source_target_pairs={{0,32},{2,34},{24,56},{26,58},{32,0},{34,2},{56,24},{58,26},{6,38}... | collective-permute-start | bytes 1572872 | tf_op jit(solution)/shard_map/ppermute | solution.py:272
  90.4 9.2 %collective-permute-start.4 = (f32[512,256]{1,0:T(8,128)S(1)}, f32[512,256]{1,0:T(8,128)S(1)}, u32[]{:S(2)}, u32[]{:S(2)}) collective-permute-start(f32[512,256]{1,0:T(8,128)S(1)} %get-tuple-element.19), channel_id=1, source_target_pairs={{0,2},{2,0},{24,26},{26,24},{32,34},{34,32},{56,58},{58,56},{6,4},... | collective-permute-start | bytes 1572872 | tf_op jit(solution)/shard_map/ppermute | solution.py:272

commit v10 on v9

--- a/solution.py
+++ b/solution.py
@@ -135,10 +135,13 @@
     return high, (x - high.astype(F32)).astype(jnp.bfloat16)
 
 
-def pack_kernel(x_ref, lead_ref, out):
+def pack_kernel(x_ref, other_ref, valid_ref, out):
+    live = lax.broadcasted_iota(jnp.int32, (128, 128), 0) < valid_ref[...]
+    clear = lambda x: jnp.concatenate([jnp.where(live, x[:, i : i + 128], 0.0) for i in range(0, x.shape[1], 128)], axis=1)
+    lead = clear(jnp.where(lax.axis_index("col") == 0, x_ref[:, :LEAD], other_ref[...]))
     for p in range(8):
-        out[p, :, :LEAD] = lead_ref[...]
-        out[p, :, LEAD:] = x_ref[:, 256 * p : 256 * p + 256]
+        out[p, :, :LEAD] = lead
+        out[p, :, LEAD:] = clear(x_ref[:, 256 * p : 256 * p + 256])
 
 
 def gram_kernel(x_ref, out, right):
@@ -207,7 +210,7 @@
     gray = lambda at: (at >> 1) ^ (at & 1)
     first = gray(x) | ((y >> 1) << 1) | (gray(z) << 2)
     second = (x >> 1) | (gray(y) << 1) | ((z >> 1) << 2)
-    return jnp.where(core == 0, first, second)
+    return jnp.where(core == 1, first, second)
 
 
 def product_kernel(head_ref, tail_ref, *refs):
@@ -240,7 +243,7 @@
             inside = outside = 0
             for axis, at in enumerate((chip % 4, chip // 4 % 4, chip // 16)):
                 bits = (at // 2 ^ at % 2, at // 2)
-                first = kind ^ core ^ (axis == 1)
+                first = kind ^ core ^ (axis != 1)
                 inside += bits[first] << axis
                 outside += bits[1 - first] << axis
             groups.setdefault((core, outside), {})[inside] = chip * 2 + core
@@ -273,10 +276,8 @@
 
     raw = contributions.reshape(blocks * height, width)
     other = across(raw[:, :LEAD])
-    live = jnp.arange(height, dtype=jnp.int32)[:, None] < valid_rows[0]
-    masked = jnp.where(live, raw, 0.0)
-    lead = jnp.where(core == 0, masked[:, :LEAD], jnp.where(live, other, 0.0))
-    packed = exchange(call(pack_kernel, vmem(8, 128, 768), (masked, lead), name="pack"), PLUS)
+    packed = call(pack_kernel, vmem(8, 128, 768), (raw, other, valid_rows.reshape(1, 1)), name="pack")
+    packed = exchange(packed, PLUS)
     scratch = (pltpu.VMEM((1024, LEAD), F32),)
     grams = call(gram_kernel, vmem(8, 128, 256), (packed.reshape(1024, 768),), 1 << 30, 4 << 20, scratch, name="gram", limit=24)
     mine = jnp.sum(exchange(grams, MINUS), axis=0)

time: 105 us -> 106 us (level)
  waiting for transfers between devices: 1.16 us -> 3.23 us
  other arithmetic: 1.64 us -> 0.18 us
  blocking collectives: 65 us -> 63.7 us
  local copies, waits for them, and re-layouts: 1.14 us -> 2.37 us
  starting transfers between devices: 10.3 us -> 11.5 us
    select_n x2 -> x0, other arithmetic: 1.45 us -> none  [the longest x1 1.36 us: body(): masked = jnp.where(live, raw, 0.0)]
    all_to_all x3, blocking collectives: 65 us -> 63.7 us  [exchange(): return lax.all_to_all(x, ('row', 'col'), 0, 0, axis_index_groups=groups)]
    ppermute x7, starting transfers between devices: 10.1 us -> 11.4 us  [swap(): return lax.ppermute(x, ('row', 'col'), flip(mask))]
    unnamed x0 -> x2, local copies, waits for them, and re-layouts: none -> 1.22 us
    ppermute x7, waiting for transfers between devices: 1.16 us -> 2.36 us  [swap(): return lax.ppermute(x, ('row', 'col'), flip(mask))]
  transfers between devices with their start and end apart: 9 -> 9, of which waited for: 1 -> 3; matrix products, arithmetic and copies ran while one was open for 1% -> 0% of each run, Pallas kernels for 16% -> 16%
where the time goes in v10:
time: 106 us
  blocking collectives  63.7 us (60%)
  Pallas kernels  23.6 us (22%)
  starting transfers between devices  11.5 us (11%)
  waiting for transfers between devices  3.23 us (3%)
  local copies, waits for them, and re-layouts  2.37 us (2%)
    all_to_all x3, blocking collectives, exchange(): return lax.all_to_all(x, ('row', 'col'), 0, 0, axis_index_groups=groups)  63.7 us
    pallas_call x5, Pallas kernels, call(): pl.pallas_call(kernel, out_shape=out, in_specs=[VMEM] * len(args), out_sp...  23.6 us
    ppermute x7, starting transfers between devices, swap(): return lax.ppermute(x, ('row', 'col'), flip(mask))  11.4 us
    ppermute x7, waiting for transfers between devices, swap(): return lax.ppermute(x, ('row', 'col'), flip(mask))  2.36 us
  transfers between devices with their start and end apart: 9, of which 3 were waited for; matrix products, arithmetic and copies ran while one was open for 0% of the time, Pallas kernels for 16%

profile of v10, /device:TPU:0, one launch (start us, length us, event | category | flops | bytes accessed | tf_op | source)
XLA Modules:
  0.0 105.5 jit_solution(17302195413519148109)
XLA Ops:
  0.0 1.0 slice.12
  1.0 0.1 collective-permute-start
  1.7 0.9 collective-permute-done.other_ref
  2.6 0.0 copy-start
  2.6 1.2 %copy-done = f32[1,128,2048]{2,1,0:T(8,128)S(1)} copy-done((f32[1,128,2048]{2,1,0:T(8,128)S(1)}, f32[1,128,2048]{2,1,0:T(8,128)}, u32[]{:S(2)}) %copy-start) | copy-done | bytes 1048600
  3.8 0.3 pack.1
  4.1 33.2 %all_to_all.15 = f32[8,128,768]{2,1,0:T(8,128)S(1)} all-to-all(f32[8,128,768]{2,1,0:T(8,128)S(1)} %pack.1), channel_id=1, replica_groups={{0,6,8,14,96,102,104,110},{2,4,10,12,98,100,106,108},{24,30,16,22,120,1..., dimensions={0} | all-to-all | bytes 6291456 | tf_op jit(solution)/shard_map/all_to_all | solution.py:261
  37.3 2.4 %gram.1 = f32[8,128,256]{2,1,0:T(8,128)S(1)} custom-call(f32[1024,768]{1,0:T(8,128)S(1)} %bitcast.7), custom_call_target="tpu_custom_call" | custom-call | flops 1073741824 | bytes 4194304 | tf_op jit(solution)/shard_map/gram/pallas_call | solution.py:121
  39.7 15.7 %all_to_all.16 = f32[8,128,256]{2,1,0:T(8,128)S(1)} all-to-all(f32[8,128,256]{2,1,0:T(8,128)S(1)} %gram.1), channel_id=1, replica_groups={{0,2,24,26,32,34,56,58},{6,4,30,28,38,36,62,60},{8,10,16,18,40,42,48,50..., dimensions={0} | all-to-all | bytes 2097152 | tf_op jit(solution)/shard_map/all_to_all | solution.py:261
  55.4 0.1 reduce_sum.9
  55.4 0.1 broadcast_in_dim.2
  55.5 14.8 %all_to_all.17 = f32[8,128,256]{2,1,0:T(8,128)S(1)} all-to-all(f32[8,128,256]{2,1,0:T(8,128)S(1)} %broadcast_in_dim.2), channel_id=1, replica_groups={{0,2,24,26,32,34,56,58},{6,4,30,28,38,36,62,60},{8,10,16,18,40,42,48,50..., dimensions={0} | all-to-all | bytes 2097152 | tf_op jit(solution)/shard_map/all_to_all | solution.py:261
  70.4 0.1 fusion
  70.5 0.1 collective-permute-start.1
  70.5 0.1 collective-permute-start.8
  70.6 0.8 collective-permute-start.5
  71.4 3.9 %collective-permute-start.3 = (f32[512,256]{1,0:T(8,128)S(1)}, f32[512,256]{1,0:T(8,128)S(1)}, u32[]{:S(2)}, u32[]{:S(2)}) collective-permute-start(f32[512,256]{1,0:T(8,128)S(1)} %bitcast.12), channel_id=1, source_target_pairs={{0,8},{6,14},{8,0},{14,6},{96,104},{102,110},{104,96},{110,102},{2... | collective-permute-start | bytes 1572872 | tf_op jit(solution)/shard_map/ppermute | solution.py:275
  75.3 2.7 %collective-permute-start.2 = (f32[512,256]{1,0:T(8,128)S(1)}, f32[512,256]{1,0:T(8,128)S(1)}, u32[]{:S(2)}, u32[]{:S(2)}) collective-permute-start(f32[512,256]{1,0:T(8,128)S(1)} %bitcast.13), channel_id=1, source_target_pairs={{0,6},{6,0},{8,14},{14,8},{96,102},{102,96},{104,110},{110,104},{2... | collective-permute-start | bytes 1572872 | tf_op jit(solution)/shard_map/ppermute | solution.py:275
  78.0 0.0 collective-permute-done.1.other
  78.0 9.0 %first.1 = (f32[512,512]{1,0:T(8,128)S(1)}, f32[256,256]{1,0:T(8,128)S(1)}, f32[1,256]{1,0:T(1,128)S(1)}) custom-call(f32[512,256]{1,0:T(8,128)S(1)} %bitcast.16, f32[512,256]{1,0:T(8,128)S(1)} %collective-permute-done.1.other), custom_call_target="tpu_custom_call" | custom-call | flops 10000000000 | bytes 2097152 | tf_op jit(solution)/shard_map/first/pallas_call | solution.py:121
  87.0 0.0 collective-permute-done.5.refs_4_
  87.0 0.6 collective-permute-done.3.refs_2_
  87.5 0.0 collective-permute-done.2.refs_1_
  87.5 0.1 broadcast_add_fusion
  87.7 0.7 collective-permute-start.7
  88.3 2.7 %collective-permute-start.6 = (f32[512,256]{1,0:T(8,128)S(1)}, f32[512,256]{1,0:T(8,128)S(1)}, u32[]{:S(2)}, u32[]{:S(2)}) collective-permute-start(f32[512,256]{1,0:T(8,128)S(1)} %get-tuple-element.18), channel_id=1, source_target_pairs={{0,96},{6,102},{8,104},{14,110},{96,0},{102,6},{104,8},{110,14},{2... | collective-permute-start | bytes 1572872 | tf_op jit(solution)/shard_map/ppermute | solution.py:275
  91.0 0.6 collective-permute-start.4
  91.6 8.0 %second.1 = (bf16[1024,256]{1,0:T(8,128)(2,1)S(1)}, bf16[512,256]{1,0:T(8,128)(2,1)S(1)}) custom-call(f32[512,512]{1,0:T(8,128)S(1)} %get-tuple-element.10.half_ref, f32[256,256]{1,0:T(8,128)S(1)} %get-tuple-element.11.left_ref), custom_call_target="tpu_custom_call" | custom-call | flops 10000000000 | bytes 2097152 | tf_op jit(solution)/shard_map/second/pallas_call | solution.py:121
  99.6 0.0 collective-permute-done.8.refs_7_
  99.6 0.0 collective-permute-done.7.refs_6_
  99.6 0.0 collective-permute-done.6.refs_5_
  99.6 1.8 %collective-permute-done.4.refs_3_ = f32[512,256]{1,0:T(8,128)S(1)} collective-permute-done((f32[512,256]{1,0:T(8,128)S(1)}, f32[512,256]{1,0:T(8,128)S(1)}, u32[]{:S(2)}, u32[]{:S(2)}) %collective-permute-start.4) | collective-permute-done | bytes 524320 | tf_op jit(solution)/shard_map/ppermute | solution.py:275
  101.4 3.9 %product.1 = f32[512,2048]{1,0:T(8,128)} custom-call(bf16[1024,256]{1,0:T(8,128)(2,1)S(1)} %get-tuple-element.12.head_ref, bf16[512,256]{1,0:T(8,128)(2,1)S(1)} %get-tuple-element.13.tail_ref, f32[512,256]{1,0:T(8,128)S(1)} %bitcast.14, f32[512,256]{1,0:T(8,128)S(1)} %collective-permute-done.2.refs_1_, f32[512,256]{1,0:T(8,128)S(1)} %collective-permute-done.3.refs_2_, ...), custom_call_target="tpu_custom_call" | custom-call | flops 3221225472 | bytes 9437184 | tf_op jit(solution)/shard_map/product/pallas_call | solution.py:121
Async XLA Ops:
  1.0 1.6 %collective-permute-start = (f32[128,512]{1,0:T(8,128)S(1)}, f32[128,512]{1,0:T(8,128)S(1)}, u32[]{:S(2)}, u32[]{:S(2)}) collective-permute-start(f32[128,512]{1,0:T(8,128)S(1)} %slice.12), channel_id=1, source_target_pairs={{0,1},{1,0},{2,3},{3,2},{4,5},{5,4},{6,7},{7,6},{8,9},{9,8},{10,11... | collective-permute-start | bytes 786440 | tf_op jit(solution)/shard_map/ppermute | solution.py:269
  2.6 1.2 %copy-start = (f32[1,128,2048]{2,1,0:T(8,128)S(1)}, f32[1,128,2048]{2,1,0:T(8,128)}, u32[]{:S(2)}) copy-start(f32[1,128,2048]{2,1,0:T(8,128)} %param.2) | copy-start | bytes 3145732
  70.5 7.5 %collective-permute-start.1 = (f32[512,256]{1,0:T(8,128)S(1)}, f32[512,256]{1,0:T(8,128)S(1)}, u32[]{:S(2)}, u32[]{:S(2)}) collective-permute-start(f32[512,256]{1,0:T(8,128)S(1)} %bitcast.15), channel_id=1, source_target_pairs={{0,1},{1,0},{2,3},{3,2},{4,5},{5,4},{6,7},{7,6},{8,9},{9,8},{10,11... | collective-permute-start | bytes 1572872 | tf_op jit(solution)/shard_map/ppermute | solution.py:269
  70.5 29.0 %collective-permute-start.8 = (f32[512,256]{1,0:T(8,128)S(1)}, f32[512,256]{1,0:T(8,128)S(1)}, u32[]{:S(2)}, u32[]{:S(2)}) collective-permute-start(f32[512,256]{1,0:T(8,128)S(1)} %bitcast.10), channel_id=1, source_target_pairs={{0,110},{6,104},{8,102},{14,96},{96,14},{102,8},{104,6},{110,0},{2... | collective-permute-start | bytes 1572872 | tf_op jit(solution)/shard_map/ppermute | solution.py:275
  70.6 16.3 %collective-permute-start.5 = (f32[512,256]{1,0:T(8,128)S(1)}, f32[512,256]{1,0:T(8,128)S(1)}, u32[]{:S(2)}, u32[]{:S(2)}) collective-permute-start(f32[512,256]{1,0:T(8,128)S(1)} %bitcast.11), channel_id=1, source_target_pairs={{0,96},{6,102},{8,104},{14,110},{96,0},{102,6},{104,8},{110,14},{2... | collective-permute-start | bytes 1572872 | tf_op jit(solution)/shard_map/ppermute | solution.py:275
  71.4 16.1 %collective-permute-start.3 = (f32[512,256]{1,0:T(8,128)S(1)}, f32[512,256]{1,0:T(8,128)S(1)}, u32[]{:S(2)}, u32[]{:S(2)}) collective-permute-start(f32[512,256]{1,0:T(8,128)S(1)} %bitcast.12), channel_id=1, source_target_pairs={{0,8},{6,14},{8,0},{14,6},{96,104},{102,110},{104,96},{110,102},{2... | collective-permute-start | bytes 1572872 | tf_op jit(solution)/shard_map/ppermute | solution.py:275
  75.3 12.2 %collective-permute-start.2 = (f32[512,256]{1,0:T(8,128)S(1)}, f32[512,256]{1,0:T(8,128)S(1)}, u32[]{:S(2)}, u32[]{:S(2)}) collective-permute-start(f32[512,256]{1,0:T(8,128)S(1)} %bitcast.13), channel_id=1, source_target_pairs={{0,6},{6,0},{8,14},{14,8},{96,102},{102,96},{104,110},{110,104},{2... | collective-permute-start | bytes 1572872 | tf_op jit(solution)/shard_map/ppermute | solution.py:275
  87.7 11.9 %collective-permute-start.7 = (f32[512,256]{1,0:T(8,128)S(1)}, f32[512,256]{1,0:T(8,128)S(1)}, u32[]{:S(2)}, u32[]{:S(2)}) collective-permute-start(f32[512,256]{1,0:T(8,128)S(1)} %get-tuple-element.17), channel_id=1, source_target_pairs={{0,8},{6,14},{8,0},{14,6},{96,104},{102,110},{104,96},{110,102},{2... | collective-permute-start | bytes 1572872 | tf_op jit(solution)/shard_map/ppermute | solution.py:275
  88.3 11.3 %collective-permute-start.6 = (f32[512,256]{1,0:T(8,128)S(1)}, f32[512,256]{1,0:T(8,128)S(1)}, u32[]{:S(2)}, u32[]{:S(2)}) collective-permute-start(f32[512,256]{1,0:T(8,128)S(1)} %get-tuple-element.18), channel_id=1, source_target_pairs={{0,96},{6,102},{8,104},{14,110},{96,0},{102,6},{104,8},{110,14},{2... | collective-permute-start | bytes 1572872 | tf_op jit(solution)/shard_map/ppermute | solution.py:275
  91.0 10.4 %collective-permute-start.4 = (f32[512,256]{1,0:T(8,128)S(1)}, f32[512,256]{1,0:T(8,128)S(1)}, u32[]{:S(2)}, u32[]{:S(2)}) collective-permute-start(f32[512,256]{1,0:T(8,128)S(1)} %get-tuple-element.19), channel_id=1, source_target_pairs={{0,6},{6,0},{8,14},{14,8},{96,102},{102,96},{104,110},{110,104},{2... | collective-permute-start | bytes 1572872 | tf_op jit(solution)/shard_map/ppermute | solution.py:275

commit v11 on v9

--- a/solution.py
+++ b/solution.py
@@ -1,3 +1,5 @@
+import functools
+
 import jax
 import jax.numpy as jnp
 from jax import lax
@@ -207,16 +209,16 @@
     gray = lambda at: (at >> 1) ^ (at & 1)
     first = gray(x) | ((y >> 1) << 1) | (gray(z) << 2)
     second = (x >> 1) | (gray(y) << 1) | ((z >> 1) << 2)
-    return jnp.where(core == 0, first, second)
-
-
-def product_kernel(head_ref, tail_ref, *refs):
-    parts, (out_ref, buf, sems) = refs[:8], refs[8:]
+    return jnp.where(core == 1, first, second)
+
+
+def product_kernel(masks, head_ref, tail_ref, *refs):
+    parts, (out_ref, buf, sems) = refs[: len(masks)], refs[-3:]
     mine = place()
     offset = lax.axis_index("col") * 2048
     dot = lambda x, y: jnp.dot(x, y, preferred_element_type=F32)
     copies = []
-    for m, part in enumerate(parts):
+    for i, (m, part) in enumerate(zip(masks, parts)):
         xh, xl = two(part[:256])
         both = dot(head_ref[...], xh)
         y = both[:LEAD] + (both[LEAD:] + dot(head_ref[:LEAD], xl))
@@ -226,11 +228,28 @@
         column = offset + (mine ^ m) * 256
         for r, block in ((0, y[:256]), (256, low)):
             ids = column + lax.broadcasted_iota(jnp.int32, block.shape, 1)
-            buf[m, r : r + 256, :] = jnp.where(ids >= r + lax.broadcasted_iota(jnp.int32, block.shape, 0), block, 0.0)
-        copies.append(pltpu.make_async_copy(buf.at[m], out_ref.at[:, aligned(mine ^ m, 256)], sems.at[m]))
+            buf[i, r : r + 256, :] = jnp.where(ids >= r + lax.broadcasted_iota(jnp.int32, block.shape, 0), block, 0.0)
+        copies.append(pltpu.make_async_copy(buf.at[i], out_ref.at[:, aligned(mine ^ m, 256)], sems.at[i]))
         copies[-1].start()
     for copy in copies:
         copy.wait()
+
+
+def product(masks, inverse, parts, out=None):
+    n = len(parts)
+    hbm = pl.BlockSpec(memory_space=pl.ANY)
+    more = () if out is None else (out,)
+    return pl.pallas_call(
+        functools.partial(product_kernel, masks),
+        out_shape=vmem(LEAD, 2048),
+        in_specs=[VMEM] * (2 + n) + [hbm] * len(more),
+        out_specs=hbm,
+        scratch_shapes=[pltpu.VMEM((n, LEAD, 256), F32), pltpu.SemaphoreType.DMA((n,))],
+        input_output_aliases={2 + n: 0} if more else {},
+        compiler_params=pltpu.CompilerParams(vmem_limit_bytes=24 << 20),
+        cost_estimate=cost(n * 400_000_000, n << 20),
+        name="product",
+    )(*inverse, *parts, *more)
 
 
 def cubes(kind):
@@ -240,7 +259,7 @@
             inside = outside = 0
             for axis, at in enumerate((chip % 4, chip // 4 % 4, chip // 16)):
                 bits = (at // 2 ^ at % 2, at // 2)
-                first = kind ^ core ^ (axis == 1)
+                first = kind ^ core ^ (axis != 1)
                 inside += bits[first] << axis
                 outside += bits[1 - first] << axis
             groups.setdefault((core, outside), {})[inside] = chip * 2 + core
@@ -293,10 +312,8 @@
     inverse = call(second_kernel, out, (half, left), 10**10, 2 << 20, scratch, name="second")
     x, y, z = (block + zero for block in near)
     xy, yz, zx = swap(y, 1), swap(z, 2), swap(x, 4)
-    parts = (rest, near[0], near[1], xy, near[2], zx, yz, far)
-    scratch = (pltpu.VMEM((8, LEAD, 256), F32), pltpu.SemaphoreType.DMA((8,)))
-    spec = pl.BlockSpec(memory_space=pl.ANY)
-    return call(product_kernel, vmem(LEAD, width), (*inverse, *parts), 3 << 30, 9 << 20, scratch, spec, "product", 24)
+    done = product((0, 1, 2, 4, 7), inverse, (rest, *near, far))
+    return product((3, 6, 5), inverse, (xy, yz, zx), done)
 
 
 def solution(mesh):

time: 105 us -> 104 us (level); the launches traced: 104 us -> 104 us
  blocking collectives: 65 us -> 63.7 us
  starting transfers between devices: 10.3 us -> 11.5 us
    pallas_call x0 -> x2, Pallas kernels: none -> 4.91 us  [product(): pl.pallas_call(functools.partial(product_kernel, masks), out_shape=vmem(L...]
    pallas_call x5 -> x4, Pallas kernels: 23.5 us -> 19.5 us  [call(): pl.pallas_call(kernel, out_shape=out, in_specs=[VMEM] * len(args), out_sp...]
    all_to_all x3, blocking collectives: 65 us -> 63.7 us  [exchange(): return lax.all_to_all(x, ('row', 'col'), 0, 0, axis_index_groups=groups)]
    ppermute x7, starting transfers between devices: 10.1 us -> 11.4 us  [swap(): return lax.ppermute(x, ('row', 'col'), flip(mask))]
  transfers between devices with their start and end apart: 9 -> 9, of which waited for: 1 -> 1; matrix products, arithmetic and copies ran while one was open for 1% -> 1% of each run, Pallas kernels for 16% -> 19%
where the time goes in v11:
time: 104 us
  blocking collectives  63.7 us (61%)
  Pallas kernels  24.5 us (24%)
  starting transfers between devices  11.5 us (11%)
  other arithmetic  1.67 us (2%)
  local copies, waits for them, and re-layouts  1.14 us (1%)
    all_to_all x3, blocking collectives, exchange(): return lax.all_to_all(x, ('row', 'col'), 0, 0, axis_index_groups=groups)  63.7 us
    pallas_call x4, Pallas kernels, call(): pl.pallas_call(kernel, out_shape=out, in_specs=[VMEM] * len(args), out_sp...  19.5 us
    ppermute x7, starting transfers between devices, swap(): return lax.ppermute(x, ('row', 'col'), flip(mask))  11.4 us
    pallas_call x2, Pallas kernels, product(): pl.pallas_call(functools.partial(product_kernel, masks), out_shape=vmem(L...  4.91 us
  transfers between devices with their start and end apart: 9, of which 1 were waited for; matrix products, arithmetic and copies ran while one was open for 1% of the time, Pallas kernels for 19%

profile of v11, /device:TPU:0, one launch (start us, length us, event | category | flops | bytes accessed | tf_op | source)
XLA Modules:
  0.0 104.1 jit_solution(10151196481612157905)
XLA Ops:
  0.0 1.0 slice.17
  1.0 0.1 collective-permute-start
  1.7 1.4 %broadcast_select_fusion.x_ref = f32[128,2048]{1,0:T(8,128)S(1)} fusion(pred[128]{0:T(512)(128)(4,1)S(1)} %iota_compare_fusion, f32[1,128,2048]{2,1,0:T(8,128)} %param.2), kind=kLoop, calls=%fused_computation | loop fusion | flops 262144 | bytes 2097280 | tf_op jit(solution)/shard_map/jit(_where)/select_n | solution.py:296
  3.1 0.0 collective-permute-done
  3.1 0.1 slice_select_fusion.lead_ref
  3.2 0.2 pack.1
  3.4 33.2 %all_to_all.15 = f32[8,128,768]{2,1,0:T(8,128)S(1)} all-to-all(f32[8,128,768]{2,1,0:T(8,128)S(1)} %pack.1), channel_id=1, replica_groups={{0,6,8,14,96,102,104,110},{2,4,10,12,98,100,106,108},{24,30,16,22,120,1..., dimensions={0} | all-to-all | bytes 6291456 | tf_op jit(solution)/shard_map/all_to_all | solution.py:277
  36.7 2.4 %gram.1 = f32[8,128,256]{2,1,0:T(8,128)S(1)} custom-call(f32[1024,768]{1,0:T(8,128)S(1)} %bitcast.8), custom_call_target="tpu_custom_call" | custom-call | flops 1073741824 | bytes 4194304 | tf_op jit(solution)/shard_map/gram/pallas_call | solution.py:123
  39.0 15.7 %all_to_all.16 = f32[8,128,256]{2,1,0:T(8,128)S(1)} all-to-all(f32[8,128,256]{2,1,0:T(8,128)S(1)} %gram.1), channel_id=1, replica_groups={{0,2,24,26,32,34,56,58},{6,4,30,28,38,36,62,60},{8,10,16,18,40,42,48,50..., dimensions={0} | all-to-all | bytes 2097152 | tf_op jit(solution)/shard_map/all_to_all | solution.py:277
  54.7 0.1 reduce_sum.9
  54.8 0.1 broadcast_in_dim.35
  54.9 14.8 %all_to_all.17 = f32[8,128,256]{2,1,0:T(8,128)S(1)} all-to-all(f32[8,128,256]{2,1,0:T(8,128)S(1)} %broadcast_in_dim.35), channel_id=1, replica_groups={{0,2,24,26,32,34,56,58},{6,4,30,28,38,36,62,60},{8,10,16,18,40,42,48,50..., dimensions={0} | all-to-all | bytes 2097152 | tf_op jit(solution)/shard_map/all_to_all | solution.py:277
  69.7 0.1 fusion
  69.8 0.1 collective-permute-start.1
  69.9 0.1 collective-permute-start.8
  70.0 0.9 collective-permute-start.6
  70.9 2.3 %collective-permute-start.4 = (f32[512,256]{1,0:T(8,128)S(1)}, f32[512,256]{1,0:T(8,128)S(1)}, u32[]{:S(2)}, u32[]{:S(2)}) collective-permute-start(f32[512,256]{1,0:T(8,128)S(1)} %bitcast.11), channel_id=1, source_target_pairs={{0,96},{6,102},{8,104},{14,110},{96,0},{102,6},{104,8},{110,14},{2... | collective-permute-start | bytes 1572872 | tf_op jit(solution)/shard_map/ppermute | solution.py:291
  73.2 4.1 %collective-permute-start.2 = (f32[512,256]{1,0:T(8,128)S(1)}, f32[512,256]{1,0:T(8,128)S(1)}, u32[]{:S(2)}, u32[]{:S(2)}) collective-permute-start(f32[512,256]{1,0:T(8,128)S(1)} %bitcast.12), channel_id=1, source_target_pairs={{0,8},{6,14},{8,0},{14,6},{96,104},{102,110},{104,96},{110,102},{2... | collective-permute-start | bytes 1572872 | tf_op jit(solution)/shard_map/ppermute | solution.py:291
  77.3 0.0 collective-permute-done.1.other
  77.3 9.0 %first.1 = (f32[512,512]{1,0:T(8,128)S(1)}, f32[256,256]{1,0:T(8,128)S(1)}, f32[1,256]{1,0:T(1,128)S(1)}) custom-call(f32[512,256]{1,0:T(8,128)S(1)} %bitcast.15, f32[512,256]{1,0:T(8,128)S(1)} %collective-permute-done.1.other), custom_call_target="tpu_custom_call" | custom-call | flops 10000000000 | bytes 2097152 | tf_op jit(solution)/shard_map/first/pallas_call | solution.py:123
  86.3 0.0 collective-permute-done.6.refs_1_
  86.3 0.6 collective-permute-done.4.refs_3_
  86.9 0.0 collective-permute-done.2.refs_2_
  86.9 0.1 broadcast_add_fusion
  87.0 2.8 %collective-permute-start.7 = (f32[512,256]{1,0:T(8,128)S(1)}, f32[512,256]{1,0:T(8,128)S(1)}, u32[]{:S(2)}, u32[]{:S(2)}) collective-permute-start(f32[512,256]{1,0:T(8,128)S(1)} %get-tuple-element.17), channel_id=1, source_target_pairs={{0,96},{6,102},{8,104},{14,110},{96,0},{102,6},{104,8},{110,14},{2... | collective-permute-start | bytes 1572872 | tf_op jit(solution)/shard_map/ppermute | solution.py:291
  89.8 0.6 collective-permute-start.5
  90.4 0.6 collective-permute-start.3
  91.0 8.0 %second.1 = (bf16[1024,256]{1,0:T(8,128)(2,1)S(1)}, bf16[512,256]{1,0:T(8,128)(2,1)S(1)}) custom-call(f32[512,512]{1,0:T(8,128)S(1)} %get-tuple-element.10.half_ref, f32[256,256]{1,0:T(8,128)S(1)} %get-tuple-element.11.left_ref), custom_call_target="tpu_custom_call" | custom-call | flops 10000000000 | bytes 2097152 | tf_op jit(solution)/shard_map/second/pallas_call | solution.py:123
  99.0 0.0 collective-permute-done.8.refs_4_
  99.0 2.8 %product.2.refs_3_ = f32[512,2048]{1,0:T(8,128)} custom-call(bf16[1024,256]{1,0:T(8,128)(2,1)S(1)} %get-tuple-element.12.head_ref, bf16[512,256]{1,0:T(8,128)(2,1)S(1)} %get-tuple-element.13.tail_ref, f32[512,256]{1,0:T(8,128)S(1)} %bitcast.13, f32[512,256]{1,0:T(8,128)S(1)} %collective-permute-done.6.refs_1_, ...), custom_call_target="tpu_custom_call" | custom-call | flops 2000000000 | bytes 5242880 | tf_op jit(solution)/shard_map/product/pallas_call | solution.py:242
  101.8 0.0 collective-permute-done.7.refs_2_
  101.8 0.0 collective-permute-done.5.refs_1_
  101.8 0.0 collective-permute-done.3.refs_0_
  101.9 2.1 %product.3 = f32[512,2048]{1,0:T(8,128)} custom-call(bf16[1024,256]{1,0:T(8,128)(2,1)S(1)} %get-tuple-element.12.head_ref, bf16[512,256]{1,0:T(8,128)(2,1)S(1)} %get-tuple-element.13.tail_ref, f32[512,256]{1,0:T(8,128)S(1)} %collective-permute-done.3.refs_0_, f32[512,256]{1,0:T(8,128)S(1)} %collective-permute-done.5.refs_1_, ...), custom_call_target="tpu_custom_call", output_to_operand_aliasing={{}: (5, {})} | custom-call | flops 1200000000 | bytes 3145728 | tf_op jit(solution)/shard_map/product/pallas_call | solution.py:242
  (1 shorter events, 0.0 us)
Async XLA Ops:
  1.0 2.1 %collective-permute-start = (f32[128,512]{1,0:T(8,128)S(1)}, f32[128,512]{1,0:T(8,128)S(1)}, u32[]{:S(2)}, u32[]{:S(2)}) collective-permute-start(f32[128,512]{1,0:T(8,128)S(1)} %slice.17), channel_id=1, source_target_pairs={{0,1},{1,0},{2,3},{3,2},{4,5},{5,4},{6,7},{7,6},{8,9},{9,8},{10,11... | collective-permute-start | bytes 786440 | tf_op jit(solution)/shard_map/ppermute | solution.py:285
  69.8 7.5 %collective-permute-start.1 = (f32[512,256]{1,0:T(8,128)S(1)}, f32[512,256]{1,0:T(8,128)S(1)}, u32[]{:S(2)}, u32[]{:S(2)}) collective-permute-start(f32[512,256]{1,0:T(8,128)S(1)} %bitcast.14), channel_id=1, source_target_pairs={{0,1},{1,0},{2,3},{3,2},{4,5},{5,4},{6,7},{7,6},{8,9},{9,8},{10,11... | collective-permute-start | bytes 1572872 | tf_op jit(solution)/shard_map/ppermute | solution.py:285
  69.9 29.1 %collective-permute-start.8 = (f32[512,256]{1,0:T(8,128)S(1)}, f32[512,256]{1,0:T(8,128)S(1)}, u32[]{:S(2)}, u32[]{:S(2)}) collective-permute-start(f32[512,256]{1,0:T(8,128)S(1)} %bitcast.9), channel_id=1, source_target_pairs={{0,110},{6,104},{8,102},{14,96},{96,14},{102,8},{104,6},{110,0},{2... | collective-permute-start | bytes 1572872 | tf_op jit(solution)/shard_map/ppermute | solution.py:291
  70.0 16.3 %collective-permute-start.6 = (f32[512,256]{1,0:T(8,128)S(1)}, f32[512,256]{1,0:T(8,128)S(1)}, u32[]{:S(2)}, u32[]{:S(2)}) collective-permute-start(f32[512,256]{1,0:T(8,128)S(1)} %bitcast.10), channel_id=1, source_target_pairs={{0,6},{6,0},{8,14},{14,8},{96,102},{102,96},{104,110},{110,104},{2... | collective-permute-start | bytes 1572872 | tf_op jit(solution)/shard_map/ppermute | solution.py:291
  70.9 16.0 %collective-permute-start.4 = (f32[512,256]{1,0:T(8,128)S(1)}, f32[512,256]{1,0:T(8,128)S(1)}, u32[]{:S(2)}, u32[]{:S(2)}) collective-permute-start(f32[512,256]{1,0:T(8,128)S(1)} %bitcast.11), channel_id=1, source_target_pairs={{0,96},{6,102},{8,104},{14,110},{96,0},{102,6},{104,8},{110,14},{2... | collective-permute-start | bytes 1572872 | tf_op jit(solution)/shard_map/ppermute | solution.py:291
  73.2 13.7 %collective-permute-start.2 = (f32[512,256]{1,0:T(8,128)S(1)}, f32[512,256]{1,0:T(8,128)S(1)}, u32[]{:S(2)}, u32[]{:S(2)}) collective-permute-start(f32[512,256]{1,0:T(8,128)S(1)} %bitcast.12), channel_id=1, source_target_pairs={{0,8},{6,14},{8,0},{14,6},{96,104},{102,110},{104,96},{110,102},{2... | collective-permute-start | bytes 1572872 | tf_op jit(solution)/shard_map/ppermute | solution.py:291
  87.0 14.8 %collective-permute-start.7 = (f32[512,256]{1,0:T(8,128)S(1)}, f32[512,256]{1,0:T(8,128)S(1)}, u32[]{:S(2)}, u32[]{:S(2)}) collective-permute-start(f32[512,256]{1,0:T(8,128)S(1)} %get-tuple-element.17), channel_id=1, source_target_pairs={{0,96},{6,102},{8,104},{14,110},{96,0},{102,6},{104,8},{110,14},{2... | collective-permute-start | bytes 1572872 | tf_op jit(solution)/shard_map/ppermute | solution.py:291
  89.8 12.0 %collective-permute-start.5 = (f32[512,256]{1,0:T(8,128)S(1)}, f32[512,256]{1,0:T(8,128)S(1)}, u32[]{:S(2)}, u32[]{:S(2)}) collective-permute-start(f32[512,256]{1,0:T(8,128)S(1)} %get-tuple-element.18), channel_id=1, source_target_pairs={{0,8},{6,14},{8,0},{14,6},{96,104},{102,110},{104,96},{110,102},{2... | collective-permute-start | bytes 1572872 | tf_op jit(solution)/shard_map/ppermute | solution.py:291
  90.4 11.4 %collective-permute-start.3 = (f32[512,256]{1,0:T(8,128)S(1)}, f32[512,256]{1,0:T(8,128)S(1)}, u32[]{:S(2)}, u32[]{:S(2)}) collective-permute-start(f32[512,256]{1,0:T(8,128)S(1)} %get-tuple-element.19), channel_id=1, source_target_pairs={{0,6},{6,0},{8,14},{14,8},{96,102},{102,96},{104,110},{110,104},{2... | collective-permute-start | bytes 1572872 | tf_op jit(solution)/shard_map/ppermute | solution.py:291

commit v12 on v11

--- a/solution.py
+++ b/solution.py
@@ -40,7 +40,8 @@
         X=V[k]
         u[8*k:8*k+8,:]=X
         R=[u[pl.ds(8*k+j,8,stride=0),:] for j in range(8)]
-        S=[[lb(R[i],8*k+j) if i>=j else None for j in range(8)] for i in range(8)]
+        for j in range(8): u[256+8*j:264+8*j,:]=lb(X,8*k+j)
+        S=[[u[pl.ds(256+8*j+i,8,stride=0),:] if i>=j else None for j in range(8)] for i in range(8)]
         u[128+8*k:136+8*k,:]=E[k]
         F=[u[pl.ds(128+8*k+j,8,stride=0),:] for j in range(8)]
         l=[[None]*8 for _ in range(8)]
@@ -305,9 +306,9 @@
     near = [swap(rest, mask) for mask in (1, 2, 4)]
     far = swap(rest, 7)
     out = (vmem(LEAD, LEAD), vmem(256, 256), vmem(1, 256))
-    scratch = (pltpu.VMEM((LEAD, LEAD), F32), pltpu.VMEM((128, 128), F32), pltpu.VMEM((272, 128), F32))
+    scratch = (pltpu.VMEM((LEAD, LEAD), F32), pltpu.VMEM((128, 128), F32), pltpu.VMEM((336, 128), F32))
     half, left, zero = call(first_kernel, out, (square, across(square)), 10**10, 2 << 20, scratch, name="first")
-    scratch = (pltpu.VMEM((LEAD, LEAD), F32), pltpu.VMEM((256, 256), F32), pltpu.VMEM((128, 128), F32), pltpu.VMEM((272, 128), F32))
+    scratch = (pltpu.VMEM((LEAD, LEAD), F32), pltpu.VMEM((256, 256), F32), pltpu.VMEM((128, 128), F32), pltpu.VMEM((336, 128), F32))
     out = (jax.ShapeDtypeStruct((2 * LEAD, 256), jnp.bfloat16), jax.ShapeDtypeStruct((LEAD, 256), jnp.bfloat16))
     inverse = call(second_kernel, out, (half, left), 10**10, 2 << 20, scratch, name="second")
     x, y, z = (block + zero for block in near)

time: 104 us -> 104 us (level)
  Pallas kernels: 24.5 us -> 22.8 us
    pallas_call x4, Pallas kernels: 19.5 us -> 17.8 us  [call(): pl.pallas_call(kernel, out_shape=out, in_specs=[VMEM] * len(args), out_sp...]
  transfers between devices with their start and end apart: 9 -> 9, of which waited for: 1 -> 1; matrix products, arithmetic and copies ran while one was open for 1% -> 1% of each run, Pallas kernels for 19% -> 17%
where the time goes in v12:
time: 104 us; the launch traced here: 103 us
  blocking collectives  63.7 us (61%)
  Pallas kernels  22.8 us (22%)
  starting transfers between devices  11.5 us (11%)
  other arithmetic  1.67 us (2%)
  waiting for transfers between devices  1.47 us (1%)
  local copies, waits for them, and re-layouts  1.14 us (1%)
    all_to_all x3, blocking collectives, exchange(): return lax.all_to_all(x, ('row', 'col'), 0, 0, axis_index_groups=groups)  63.7 us
    pallas_call x4, Pallas kernels, call(): pl.pallas_call(kernel, out_shape=out, in_specs=[VMEM] * len(args), out_sp...  17.8 us
    ppermute x7, starting transfers between devices, swap(): return lax.ppermute(x, ('row', 'col'), flip(mask))  11.4 us
    pallas_call x2, Pallas kernels, product(): pl.pallas_call(functools.partial(product_kernel, masks), out_shape=vmem(L...  4.93 us
  transfers between devices with their start and end apart: 9, of which 1 were waited for; matrix products, arithmetic and copies ran while one was open for 1% of the time, Pallas kernels for 17%

profile of v12, /device:TPU:0, one launch (start us, length us, event | category | flops | bytes accessed | tf_op | source)
XLA Modules:
  0.0 103.3 jit_solution(7315138723480689996)
XLA Ops:
  0.0 1.0 slice.17
  1.0 0.1 collective-permute-start
  1.7 1.4 %broadcast_select_fusion.x_ref = f32[128,2048]{1,0:T(8,128)S(1)} fusion(pred[128]{0:T(512)(128)(4,1)S(1)} %iota_compare_fusion, f32[1,128,2048]{2,1,0:T(8,128)} %param.2), kind=kLoop, calls=%fused_computation | loop fusion | flops 262144 | bytes 2097280 | tf_op jit(solution)/shard_map/jit(_where)/select_n | solution.py:297
  3.1 0.0 collective-permute-done
  3.1 0.1 slice_select_fusion.lead_ref
  3.2 0.2 pack.1
  3.4 33.2 %all_to_all.15 = f32[8,128,768]{2,1,0:T(8,128)S(1)} all-to-all(f32[8,128,768]{2,1,0:T(8,128)S(1)} %pack.1), channel_id=1, replica_groups={{0,6,8,14,96,102,104,110},{2,4,10,12,98,100,106,108},{24,30,16,22,120,1..., dimensions={0} | all-to-all | bytes 6291456 | tf_op jit(solution)/shard_map/all_to_all | solution.py:278
  36.7 2.4 %gram.1 = f32[8,128,256]{2,1,0:T(8,128)S(1)} custom-call(f32[1024,768]{1,0:T(8,128)S(1)} %bitcast.8), custom_call_target="tpu_custom_call" | custom-call | flops 1073741824 | bytes 4194304 | tf_op jit(solution)/shard_map/gram/pallas_call | solution.py:124
  39.0 15.7 %all_to_all.16 = f32[8,128,256]{2,1,0:T(8,128)S(1)} all-to-all(f32[8,128,256]{2,1,0:T(8,128)S(1)} %gram.1), channel_id=1, replica_groups={{0,2,24,26,32,34,56,58},{6,4,30,28,38,36,62,60},{8,10,16,18,40,42,48,50..., dimensions={0} | all-to-all | bytes 2097152 | tf_op jit(solution)/shard_map/all_to_all | solution.py:278
  54.7 0.1 reduce_sum.9
  54.8 0.1 broadcast_in_dim.35
  54.9 14.8 %all_to_all.17 = f32[8,128,256]{2,1,0:T(8,128)S(1)} all-to-all(f32[8,128,256]{2,1,0:T(8,128)S(1)} %broadcast_in_dim.35), channel_id=1, replica_groups={{0,2,24,26,32,34,56,58},{6,4,30,28,38,36,62,60},{8,10,16,18,40,42,48,50..., dimensions={0} | all-to-all | bytes 2097152 | tf_op jit(solution)/shard_map/all_to_all | solution.py:278
  69.7 0.1 fusion
  69.8 0.1 collective-permute-start.1
  69.9 0.1 collective-permute-start.8
  70.0 0.9 collective-permute-start.6
  70.9 2.3 %collective-permute-start.4 = (f32[512,256]{1,0:T(8,128)S(1)}, f32[512,256]{1,0:T(8,128)S(1)}, u32[]{:S(2)}, u32[]{:S(2)}) collective-permute-start(f32[512,256]{1,0:T(8,128)S(1)} %bitcast.11), channel_id=1, source_target_pairs={{0,96},{6,102},{8,104},{14,110},{96,0},{102,6},{104,8},{110,14},{2... | collective-permute-start | bytes 1572872 | tf_op jit(solution)/shard_map/ppermute | solution.py:292
  73.2 4.1 %collective-permute-start.2 = (f32[512,256]{1,0:T(8,128)S(1)}, f32[512,256]{1,0:T(8,128)S(1)}, u32[]{:S(2)}, u32[]{:S(2)}) collective-permute-start(f32[512,256]{1,0:T(8,128)S(1)} %bitcast.12), channel_id=1, source_target_pairs={{0,8},{6,14},{8,0},{14,6},{96,104},{102,110},{104,96},{110,102},{2... | collective-permute-start | bytes 1572872 | tf_op jit(solution)/shard_map/ppermute | solution.py:292
  77.3 0.0 collective-permute-done.1.other
  77.3 8.1 %first.1 = (f32[512,512]{1,0:T(8,128)S(1)}, f32[256,256]{1,0:T(8,128)S(1)}, f32[1,256]{1,0:T(1,128)S(1)}) custom-call(f32[512,256]{1,0:T(8,128)S(1)} %bitcast.15, f32[512,256]{1,0:T(8,128)S(1)} %collective-permute-done.1.other), custom_call_target="tpu_custom_call" | custom-call | flops 10000000000 | bytes 2097152 | tf_op jit(solution)/shard_map/first/pallas_call | solution.py:124
  85.4 0.0 collective-permute-done.6.refs_1_
  85.4 1.4 %collective-permute-done.4.refs_3_ = f32[512,256]{1,0:T(8,128)S(1)} collective-permute-done((f32[512,256]{1,0:T(8,128)S(1)}, f32[512,256]{1,0:T(8,128)S(1)}, u32[]{:S(2)}, u32[]{:S(2)}) %collective-permute-start.4) | collective-permute-done | bytes 524320 | tf_op jit(solution)/shard_map/ppermute | solution.py:292
  86.9 0.0 collective-permute-done.2.refs_2_
  86.9 0.1 broadcast_add_fusion
  87.0 2.8 %collective-permute-start.7 = (f32[512,256]{1,0:T(8,128)S(1)}, f32[512,256]{1,0:T(8,128)S(1)}, u32[]{:S(2)}, u32[]{:S(2)}) collective-permute-start(f32[512,256]{1,0:T(8,128)S(1)} %get-tuple-element.17), channel_id=1, source_target_pairs={{0,96},{6,102},{8,104},{14,110},{96,0},{102,6},{104,8},{110,14},{2... | collective-permute-start | bytes 1572872 | tf_op jit(solution)/shard_map/ppermute | solution.py:292
  89.8 0.6 collective-permute-start.5
  90.4 0.6 collective-permute-start.3
  91.0 7.1 %second.1 = (bf16[1024,256]{1,0:T(8,128)(2,1)S(1)}, bf16[512,256]{1,0:T(8,128)(2,1)S(1)}) custom-call(f32[512,512]{1,0:T(8,128)S(1)} %get-tuple-element.10.half_ref, f32[256,256]{1,0:T(8,128)S(1)} %get-tuple-element.11.left_ref), custom_call_target="tpu_custom_call" | custom-call | flops 10000000000 | bytes 2097152 | tf_op jit(solution)/shard_map/second/pallas_call | solution.py:124
  98.1 0.0 collective-permute-done.8.refs_4_
  98.1 2.8 %product.2.refs_3_ = f32[512,2048]{1,0:T(8,128)} custom-call(bf16[1024,256]{1,0:T(8,128)(2,1)S(1)} %get-tuple-element.12.head_ref, bf16[512,256]{1,0:T(8,128)(2,1)S(1)} %get-tuple-element.13.tail_ref, f32[512,256]{1,0:T(8,128)S(1)} %bitcast.13, f32[512,256]{1,0:T(8,128)S(1)} %collective-permute-done.6.refs_1_, ...), custom_call_target="tpu_custom_call" | custom-call | flops 2000000000 | bytes 5242880 | tf_op jit(solution)/shard_map/product/pallas_call | solution.py:243
  101.0 0.0 collective-permute-done.7.refs_2_
  101.0 0.0 collective-permute-done.5.refs_1_
  101.0 0.0 collective-permute-done.3.refs_0_
  101.0 2.1 %product.3 = f32[512,2048]{1,0:T(8,128)} custom-call(bf16[1024,256]{1,0:T(8,128)(2,1)S(1)} %get-tuple-element.12.head_ref, bf16[512,256]{1,0:T(8,128)(2,1)S(1)} %get-tuple-element.13.tail_ref, f32[512,256]{1,0:T(8,128)S(1)} %collective-permute-done.3.refs_0_, f32[512,256]{1,0:T(8,128)S(1)} %collective-permute-done.5.refs_1_, ...), custom_call_target="tpu_custom_call", output_to_operand_aliasing={{}: (5, {})} | custom-call | flops 1200000000 | bytes 3145728 | tf_op jit(solution)/shard_map/product/pallas_call | solution.py:243
  (1 shorter events, 0.0 us)
Async XLA Ops:
  1.0 2.1 %collective-permute-start = (f32[128,512]{1,0:T(8,128)S(1)}, f32[128,512]{1,0:T(8,128)S(1)}, u32[]{:S(2)}, u32[]{:S(2)}) collective-permute-start(f32[128,512]{1,0:T(8,128)S(1)} %slice.17), channel_id=1, source_target_pairs={{0,1},{1,0},{2,3},{3,2},{4,5},{5,4},{6,7},{7,6},{8,9},{9,8},{10,11... | collective-permute-start | bytes 786440 | tf_op jit(solution)/shard_map/ppermute | solution.py:286
  69.8 7.5 %collective-permute-start.1 = (f32[512,256]{1,0:T(8,128)S(1)}, f32[512,256]{1,0:T(8,128)S(1)}, u32[]{:S(2)}, u32[]{:S(2)}) collective-permute-start(f32[512,256]{1,0:T(8,128)S(1)} %bitcast.14), channel_id=1, source_target_pairs={{0,1},{1,0},{2,3},{3,2},{4,5},{5,4},{6,7},{7,6},{8,9},{9,8},{10,11... | collective-permute-start | bytes 1572872 | tf_op jit(solution)/shard_map/ppermute | solution.py:286
  69.9 28.3 %collective-permute-start.8 = (f32[512,256]{1,0:T(8,128)S(1)}, f32[512,256]{1,0:T(8,128)S(1)}, u32[]{:S(2)}, u32[]{:S(2)}) collective-permute-start(f32[512,256]{1,0:T(8,128)S(1)} %bitcast.9), channel_id=1, source_target_pairs={{0,110},{6,104},{8,102},{14,96},{96,14},{102,8},{104,6},{110,0},{2... | collective-permute-start | bytes 1572872 | tf_op jit(solution)/shard_map/ppermute | solution.py:292
  70.0 15.5 %collective-permute-start.6 = (f32[512,256]{1,0:T(8,128)S(1)}, f32[512,256]{1,0:T(8,128)S(1)}, u32[]{:S(2)}, u32[]{:S(2)}) collective-permute-start(f32[512,256]{1,0:T(8,128)S(1)} %bitcast.10), channel_id=1, source_target_pairs={{0,6},{6,0},{8,14},{14,8},{96,102},{102,96},{104,110},{110,104},{2... | collective-permute-start | bytes 1572872 | tf_op jit(solution)/shard_map/ppermute | solution.py:292
  70.9 16.0 %collective-permute-start.4 = (f32[512,256]{1,0:T(8,128)S(1)}, f32[512,256]{1,0:T(8,128)S(1)}, u32[]{:S(2)}, u32[]{:S(2)}) collective-permute-start(f32[512,256]{1,0:T(8,128)S(1)} %bitcast.11), channel_id=1, source_target_pairs={{0,96},{6,102},{8,104},{14,110},{96,0},{102,6},{104,8},{110,14},{2... | collective-permute-start | bytes 1572872 | tf_op jit(solution)/shard_map/ppermute | solution.py:292
  73.2 13.7 %collective-permute-start.2 = (f32[512,256]{1,0:T(8,128)S(1)}, f32[512,256]{1,0:T(8,128)S(1)}, u32[]{:S(2)}, u32[]{:S(2)}) collective-permute-start(f32[512,256]{1,0:T(8,128)S(1)} %bitcast.12), channel_id=1, source_target_pairs={{0,8},{6,14},{8,0},{14,6},{96,104},{102,110},{104,96},{110,102},{2... | collective-permute-start | bytes 1572872 | tf_op jit(solution)/shard_map/ppermute | solution.py:292
  87.0 13.9 %collective-permute-start.7 = (f32[512,256]{1,0:T(8,128)S(1)}, f32[512,256]{1,0:T(8,128)S(1)}, u32[]{:S(2)}, u32[]{:S(2)}) collective-permute-start(f32[512,256]{1,0:T(8,128)S(1)} %get-tuple-element.17), channel_id=1, source_target_pairs={{0,96},{6,102},{8,104},{14,110},{96,0},{102,6},{104,8},{110,14},{2... | collective-permute-start | bytes 1572872 | tf_op jit(solution)/shard_map/ppermute | solution.py:292
  89.8 11.2 %collective-permute-start.5 = (f32[512,256]{1,0:T(8,128)S(1)}, f32[512,256]{1,0:T(8,128)S(1)}, u32[]{:S(2)}, u32[]{:S(2)}) collective-permute-start(f32[512,256]{1,0:T(8,128)S(1)} %get-tuple-element.18), channel_id=1, source_target_pairs={{0,8},{6,14},{8,0},{14,6},{96,104},{102,110},{104,96},{110,102},{2... | collective-permute-start | bytes 1572872 | tf_op jit(solution)/shard_map/ppermute | solution.py:292
  90.4 10.6 %collective-permute-start.3 = (f32[512,256]{1,0:T(8,128)S(1)}, f32[512,256]{1,0:T(8,128)S(1)}, u32[]{:S(2)}, u32[]{:S(2)}) collective-permute-start(f32[512,256]{1,0:T(8,128)S(1)} %get-tuple-element.19), channel_id=1, source_target_pairs={{0,6},{6,0},{8,14},{14,8},{96,102},{102,96},{104,110},{110,104},{2... | collective-permute-start | bytes 1572872 | tf_op jit(solution)/shard_map/ppermute | solution.py:292

commit v13 on v12

--- a/solution.py
+++ b/solution.py
@@ -204,6 +204,10 @@
     tail_ref[:256, :], tail_ref[256:, :] = two(o[256:, 256:])
 
 
+def later_kernel(x_ref, after_ref, out):
+    out[...] = x_ref[...]
+
+
 def place():
     core, row = lax.axis_index("col"), lax.axis_index("row")
     x, y, z = row & 3, (row >> 2) & 3, row >> 4
@@ -303,11 +307,12 @@
     whole = exchange(copies(mine), MINUS)
     rest, square = whole[:, :64].reshape(LEAD, 256), whole[:, 64:].reshape(LEAD, 256)
 
+    other = across(square)
     near = [swap(rest, mask) for mask in (1, 2, 4)]
-    far = swap(rest, 7)
+    far = swap(call(later_kernel, vmem(LEAD, 256), (rest, other), name="later"), 7)
     out = (vmem(LEAD, LEAD), vmem(256, 256), vmem(1, 256))
     scratch = (pltpu.VMEM((LEAD, LEAD), F32), pltpu.VMEM((128, 128), F32), pltpu.VMEM((336, 128), F32))
-    half, left, zero = call(first_kernel, out, (square, across(square)), 10**10, 2 << 20, scratch, name="first")
+    half, left, zero = call(first_kernel, out, (square, other), 10**10, 2 << 20, scratch, name="first")
     scratch = (pltpu.VMEM((LEAD, LEAD), F32), pltpu.VMEM((256, 256), F32), pltpu.VMEM((128, 128), F32), pltpu.VMEM((336, 128), F32))
     out = (jax.ShapeDtypeStruct((2 * LEAD, 256), jnp.bfloat16), jax.ShapeDtypeStruct((LEAD, 256), jnp.bfloat16))
     inverse = call(second_kernel, out, (half, left), 10**10, 2 << 20, scratch, name="second")

time: 104 us -> 104 us (level)
    pallas_call x4 -> x5, Pallas kernels: 17.8 us -> 17.9 us  [call(): pl.pallas_call(kernel, out_shape=out, in_specs=[VMEM] * len(args), out_sp...]
  transfers between devices with their start and end apart: 9 -> 9, of which waited for: 1 -> 2; matrix products, arithmetic and copies ran while one was open for 1% -> 1% of each run, Pallas kernels for 17% -> 17%
where the time goes in v13:
time: 104 us
  blocking collectives  63.7 us (61%)
  Pallas kernels  22.8 us (22%)
  starting transfers between devices  11.8 us (11%)
  other arithmetic  1.67 us (2%)
  waiting for transfers between devices  1.66 us (2%)
  local copies, waits for them, and re-layouts  1.14 us (1%)
    all_to_all x3, blocking collectives, exchange(): return lax.all_to_all(x, ('row', 'col'), 0, 0, axis_index_groups=groups)  63.7 us
    pallas_call x5, Pallas kernels, call(): pl.pallas_call(kernel, out_shape=out, in_specs=[VMEM] * len(args), out_sp...  17.9 us
    ppermute x7, starting transfers between devices, swap(): return lax.ppermute(x, ('row', 'col'), flip(mask))  11.6 us
    pallas_call x2, Pallas kernels, product(): pl.pallas_call(functools.partial(product_kernel, masks), out_shape=vmem(L...  4.93 us
  transfers between devices with their start and end apart: 9, of which 2 were waited for; matrix products, arithmetic and copies ran while one was open for 1% of the time, Pallas kernels for 17%

profile of v13, /device:TPU:0, one launch (start us, length us, event | category | flops | bytes accessed | tf_op | source)
XLA Modules:
  0.0 103.7 jit_solution(1175637738134815043)
XLA Ops:
  0.0 1.0 slice.17
  1.0 0.1 collective-permute-start
  1.7 1.4 %broadcast_select_fusion.x_ref = f32[128,2048]{1,0:T(8,128)S(1)} fusion(pred[128]{0:T(512)(128)(4,1)S(1)} %iota_compare_fusion, f32[1,128,2048]{2,1,0:T(8,128)} %param.2), kind=kLoop, calls=%fused_computation | loop fusion | flops 262144 | bytes 2097280 | tf_op jit(solution)/shard_map/jit(_where)/select_n | solution.py:301
  3.1 0.0 collective-permute-done
  3.1 0.1 slice_select_fusion.lead_ref
  3.2 0.2 pack.1
  3.4 33.2 %all_to_all.15 = f32[8,128,768]{2,1,0:T(8,128)S(1)} all-to-all(f32[8,128,768]{2,1,0:T(8,128)S(1)} %pack.1), channel_id=1, replica_groups={{0,6,8,14,96,102,104,110},{2,4,10,12,98,100,106,108},{24,30,16,22,120,1..., dimensions={0} | all-to-all | bytes 6291456 | tf_op jit(solution)/shard_map/all_to_all | solution.py:282
  36.7 2.4 %gram.1 = f32[8,128,256]{2,1,0:T(8,128)S(1)} custom-call(f32[1024,768]{1,0:T(8,128)S(1)} %bitcast.8), custom_call_target="tpu_custom_call" | custom-call | flops 1073741824 | bytes 4194304 | tf_op jit(solution)/shard_map/gram/pallas_call | solution.py:124
  39.0 15.7 %all_to_all.16 = f32[8,128,256]{2,1,0:T(8,128)S(1)} all-to-all(f32[8,128,256]{2,1,0:T(8,128)S(1)} %gram.1), channel_id=1, replica_groups={{0,2,24,26,32,34,56,58},{6,4,30,28,38,36,62,60},{8,10,16,18,40,42,48,50..., dimensions={0} | all-to-all | bytes 2097152 | tf_op jit(solution)/shard_map/all_to_all | solution.py:282
  54.7 0.1 reduce_sum.9
  54.8 0.1 broadcast_in_dim.35
  54.9 14.8 %all_to_all.17 = f32[8,128,256]{2,1,0:T(8,128)S(1)} all-to-all(f32[8,128,256]{2,1,0:T(8,128)S(1)} %broadcast_in_dim.35), channel_id=1, replica_groups={{0,2,24,26,32,34,56,58},{6,4,30,28,38,36,62,60},{8,10,16,18,40,42,48,50..., dimensions={0} | all-to-all | bytes 2097152 | tf_op jit(solution)/shard_map/all_to_all | solution.py:282
  69.7 0.1 fusion
  69.8 0.1 collective-permute-start.1
  69.9 0.6 collective-permute-start.6
  70.5 0.6 collective-permute-start.4
  71.1 0.0 collective-permute-start.2
  71.1 0.7 collective-permute-done.1.other.after_ref
  71.8 5.6 %collective-permute-start.8 = (f32[512,256]{1,0:T(8,128)S(1)}, f32[512,256]{1,0:T(8,128)S(1)}, u32[]{:S(2)}, u32[]{:S(2)}) collective-permute-start(f32[512,256]{1,0:T(8,128)S(1)} %later.1), channel_id=1, source_target_pairs={{0,110},{6,104},{8,102},{14,96},{96,14},{102,8},{104,6},{110,0},{2... | collective-permute-start | bytes 1572872 | tf_op jit(solution)/shard_map/ppermute | solution.py:296
  77.4 8.1 %first.1 = (f32[512,512]{1,0:T(8,128)S(1)}, f32[256,256]{1,0:T(8,128)S(1)}, f32[1,256]{1,0:T(1,128)S(1)}) custom-call(f32[512,256]{1,0:T(8,128)S(1)} %bitcast.15, f32[512,256]{1,0:T(8,128)S(1)} %collective-permute-done.1.other.after_ref), custom_call_target="tpu_custom_call" | custom-call | flops 10000000000 | bytes 2097152 | tf_op jit(solution)/shard_map/first/pallas_call | solution.py:124
  85.6 0.0 collective-permute-done.6.refs_1_
  85.6 1.0 collective-permute-done.4.refs_3_
  86.5 0.0 collective-permute-done.2.refs_2_
  86.5 0.1 broadcast_add_fusion
  86.7 2.1 %collective-permute-start.7 = (f32[512,256]{1,0:T(8,128)S(1)}, f32[512,256]{1,0:T(8,128)S(1)}, u32[]{:S(2)}, u32[]{:S(2)}) collective-permute-start(f32[512,256]{1,0:T(8,128)S(1)} %get-tuple-element.17), channel_id=1, source_target_pairs={{0,96},{6,102},{8,104},{14,110},{96,0},{102,6},{104,8},{110,14},{2... | collective-permute-start | bytes 1572872 | tf_op jit(solution)/shard_map/ppermute | solution.py:296
  88.8 0.0 collective-permute-start.5
  88.8 2.7 %collective-permute-start.3 = (f32[512,256]{1,0:T(8,128)S(1)}, f32[512,256]{1,0:T(8,128)S(1)}, u32[]{:S(2)}, u32[]{:S(2)}) collective-permute-start(f32[512,256]{1,0:T(8,128)S(1)} %get-tuple-element.19), channel_id=1, source_target_pairs={{0,6},{6,0},{8,14},{14,8},{96,102},{102,96},{104,110},{110,104},{2... | collective-permute-start | bytes 1572872 | tf_op jit(solution)/shard_map/ppermute | solution.py:296
  91.5 7.1 %second.1 = (bf16[1024,256]{1,0:T(8,128)(2,1)S(1)}, bf16[512,256]{1,0:T(8,128)(2,1)S(1)}) custom-call(f32[512,512]{1,0:T(8,128)S(1)} %get-tuple-element.10.half_ref, f32[256,256]{1,0:T(8,128)S(1)} %get-tuple-element.11.left_ref), custom_call_target="tpu_custom_call" | custom-call | flops 10000000000 | bytes 2097152 | tf_op jit(solution)/shard_map/second/pallas_call | solution.py:124
  98.6 0.0 collective-permute-done.8.refs_4_
  98.6 2.8 %product.2.refs_3_ = f32[512,2048]{1,0:T(8,128)} custom-call(bf16[1024,256]{1,0:T(8,128)(2,1)S(1)} %get-tuple-element.12.head_ref, bf16[512,256]{1,0:T(8,128)(2,1)S(1)} %get-tuple-element.13.tail_ref, f32[512,256]{1,0:T(8,128)S(1)} %bitcast.13, f32[512,256]{1,0:T(8,128)S(1)} %collective-permute-done.6.refs_1_, ...), custom_call_target="tpu_custom_call" | custom-call | flops 2000000000 | bytes 5242880 | tf_op jit(solution)/shard_map/product/pallas_call | solution.py:247
  101.4 0.0 collective-permute-done.7.refs_2_
  101.5 0.0 collective-permute-done.5.refs_1_
  101.5 0.0 collective-permute-done.3.refs_0_
  101.5 2.1 %product.3 = f32[512,2048]{1,0:T(8,128)} custom-call(bf16[1024,256]{1,0:T(8,128)(2,1)S(1)} %get-tuple-element.12.head_ref, bf16[512,256]{1,0:T(8,128)(2,1)S(1)} %get-tuple-element.13.tail_ref, f32[512,256]{1,0:T(8,128)S(1)} %collective-permute-done.3.refs_0_, f32[512,256]{1,0:T(8,128)S(1)} %collective-permute-done.5.refs_1_, ...), custom_call_target="tpu_custom_call", output_to_operand_aliasing={{}: (5, {})} | custom-call | flops 1200000000 | bytes 3145728 | tf_op jit(solution)/shard_map/product/pallas_call | solution.py:247
  (2 shorter events, 0.0 us)
Async XLA Ops:
  1.0 2.1 %collective-permute-start = (f32[128,512]{1,0:T(8,128)S(1)}, f32[128,512]{1,0:T(8,128)S(1)}, u32[]{:S(2)}, u32[]{:S(2)}) collective-permute-start(f32[128,512]{1,0:T(8,128)S(1)} %slice.17), channel_id=1, source_target_pairs={{0,1},{1,0},{2,3},{3,2},{4,5},{5,4},{6,7},{7,6},{8,9},{9,8},{10,11... | collective-permute-start | bytes 786440 | tf_op jit(solution)/shard_map/ppermute | solution.py:290
  69.8 2.0 %collective-permute-start.1 = (f32[512,256]{1,0:T(8,128)S(1)}, f32[512,256]{1,0:T(8,128)S(1)}, u32[]{:S(2)}, u32[]{:S(2)}) collective-permute-start(f32[512,256]{1,0:T(8,128)S(1)} %bitcast.14), channel_id=1, source_target_pairs={{0,1},{1,0},{2,3},{3,2},{4,5},{5,4},{6,7},{7,6},{8,9},{9,8},{10,11... | collective-permute-start | bytes 1572872 | tf_op jit(solution)/shard_map/ppermute | solution.py:290
  69.9 15.7 %collective-permute-start.6 = (f32[512,256]{1,0:T(8,128)S(1)}, f32[512,256]{1,0:T(8,128)S(1)}, u32[]{:S(2)}, u32[]{:S(2)}) collective-permute-start(f32[512,256]{1,0:T(8,128)S(1)} %bitcast.9), channel_id=1, source_target_pairs={{0,6},{6,0},{8,14},{14,8},{96,102},{102,96},{104,110},{110,104},{2... | collective-permute-start | bytes 1572872 | tf_op jit(solution)/shard_map/ppermute | solution.py:296
  70.5 16.0 %collective-permute-start.4 = (f32[512,256]{1,0:T(8,128)S(1)}, f32[512,256]{1,0:T(8,128)S(1)}, u32[]{:S(2)}, u32[]{:S(2)}) collective-permute-start(f32[512,256]{1,0:T(8,128)S(1)} %bitcast.10), channel_id=1, source_target_pairs={{0,96},{6,102},{8,104},{14,110},{96,0},{102,6},{104,8},{110,14},{2... | collective-permute-start | bytes 1572872 | tf_op jit(solution)/shard_map/ppermute | solution.py:296
  71.1 15.4 %collective-permute-start.2 = (f32[512,256]{1,0:T(8,128)S(1)}, f32[512,256]{1,0:T(8,128)S(1)}, u32[]{:S(2)}, u32[]{:S(2)}) collective-permute-start(f32[512,256]{1,0:T(8,128)S(1)} %bitcast.11), channel_id=1, source_target_pairs={{0,8},{6,14},{8,0},{14,6},{96,104},{102,110},{104,96},{110,102},{2... | collective-permute-start | bytes 1572872 | tf_op jit(solution)/shard_map/ppermute | solution.py:296
  71.8 26.8 %collective-permute-start.8 = (f32[512,256]{1,0:T(8,128)S(1)}, f32[512,256]{1,0:T(8,128)S(1)}, u32[]{:S(2)}, u32[]{:S(2)}) collective-permute-start(f32[512,256]{1,0:T(8,128)S(1)} %later.1), channel_id=1, source_target_pairs={{0,110},{6,104},{8,102},{14,96},{96,14},{102,8},{104,6},{110,0},{2... | collective-permute-start | bytes 1572872 | tf_op jit(solution)/shard_map/ppermute | solution.py:296
  86.7 14.8 %collective-permute-start.7 = (f32[512,256]{1,0:T(8,128)S(1)}, f32[512,256]{1,0:T(8,128)S(1)}, u32[]{:S(2)}, u32[]{:S(2)}) collective-permute-start(f32[512,256]{1,0:T(8,128)S(1)} %get-tuple-element.17), channel_id=1, source_target_pairs={{0,96},{6,102},{8,104},{14,110},{96,0},{102,6},{104,8},{110,14},{2... | collective-permute-start | bytes 1572872 | tf_op jit(solution)/shard_map/ppermute | solution.py:296
  88.8 12.7 %collective-permute-start.5 = (f32[512,256]{1,0:T(8,128)S(1)}, f32[512,256]{1,0:T(8,128)S(1)}, u32[]{:S(2)}, u32[]{:S(2)}) collective-permute-start(f32[512,256]{1,0:T(8,128)S(1)} %get-tuple-element.18), channel_id=1, source_target_pairs={{0,8},{6,14},{8,0},{14,6},{96,104},{102,110},{104,96},{110,102},{2... | collective-permute-start | bytes 1572872 | tf_op jit(solution)/shard_map/ppermute | solution.py:296
  88.8 12.7 %collective-permute-start.3 = (f32[512,256]{1,0:T(8,128)S(1)}, f32[512,256]{1,0:T(8,128)S(1)}, u32[]{:S(2)}, u32[]{:S(2)}) collective-permute-start(f32[512,256]{1,0:T(8,128)S(1)} %get-tuple-element.19), channel_id=1, source_target_pairs={{0,6},{6,0},{8,14},{14,8},{96,102},{102,96},{104,110},{110,104},{2... | collective-permute-start | bytes 1572872 | tf_op jit(solution)/shard_map/ppermute | solution.py:296

commit v14 on v12

--- a/solution.py
+++ b/solution.py
@@ -186,14 +186,15 @@
                     o_ref[ghi:, :ghi] = o_ref[ghi:, :ghi] - mtm(up, o_ref[glo:ghi, :ghi])
 
 
-def first_kernel(own, other, o_ref, left_ref, token, a, d, rows):
+def first_kernel(own, other, o_ref, left_ref, t0, t1, t2, a, d, rows):
     core = lax.axis_index("col")
     a[:, aligned(core, 256)] = own[...]
     a[:, aligned(1 - core, 256)] = other[...]
     o_ref[...] = jnp.zeros_like(o_ref)
     panels(0, d, a, o_ref, rows)
     left_ref[...] = a[256:, 256:]
-    token[...] = jnp.zeros_like(token)
+    for token in (t0, t1, t2):
+        token[...] = jnp.zeros_like(token)
 
 
 def second_kernel(half_ref, left_ref, head_ref, tail_ref, o, a, d, rows):
@@ -305,13 +306,13 @@
 
     near = [swap(rest, mask) for mask in (1, 2, 4)]
     far = swap(rest, 7)
-    out = (vmem(LEAD, LEAD), vmem(256, 256), vmem(1, 256))
+    out = (vmem(LEAD, LEAD), vmem(256, 256), *[vmem(1, 256)] * 3)
     scratch = (pltpu.VMEM((LEAD, LEAD), F32), pltpu.VMEM((128, 128), F32), pltpu.VMEM((336, 128), F32))
-    half, left, zero = call(first_kernel, out, (square, across(square)), 10**10, 2 << 20, scratch, name="first")
+    half, left, *zeros = call(first_kernel, out, (square, across(square)), 10**10, 2 << 20, scratch, name="first")
     scratch = (pltpu.VMEM((LEAD, LEAD), F32), pltpu.VMEM((256, 256), F32), pltpu.VMEM((128, 128), F32), pltpu.VMEM((336, 128), F32))
     out = (jax.ShapeDtypeStruct((2 * LEAD, 256), jnp.bfloat16), jax.ShapeDtypeStruct((LEAD, 256), jnp.bfloat16))
     inverse = call(second_kernel, out, (half, left), 10**10, 2 << 20, scratch, name="second")
-    x, y, z = (block + zero for block in near)
+    x, y, z = (block + zero for block, zero in zip(near, zeros))
     xy, yz, zx = swap(y, 1), swap(z, 2), swap(x, 4)
     done = product((0, 1, 2, 4, 7), inverse, (rest, *near, far))
     return product((3, 6, 5), inverse, (xy, yz, zx), done)

time: 104 us -> 104 us (level)
  starting transfers between devices: 11.5 us -> 12.6 us
where the time goes in v14:
time: 104 us
  blocking collectives  63.7 us (61%)
  Pallas kernels  22.8 us (22%)
  starting transfers between devices  12.6 us (12%)
  other arithmetic  1.64 us (2%)
  local copies, waits for them, and re-layouts  1.14 us (1%)
    all_to_all x3, blocking collectives, exchange(): return lax.all_to_all(x, ('row', 'col'), 0, 0, axis_index_groups=groups)  63.7 us
    pallas_call x4, Pallas kernels, call(): pl.pallas_call(kernel, out_shape=out, in_specs=[VMEM] * len(args), out_sp...  17.8 us
    ppermute x7, starting transfers between devices, swap(): return lax.ppermute(x, ('row', 'col'), flip(mask))  12.4 us
    pallas_call x2, Pallas kernels, product(): pl.pallas_call(functools.partial(product_kernel, masks), out_shape=vmem(L...  4.93 us
  transfers between devices with their start and end apart: 9, of which 1 were waited for; matrix products, arithmetic and copies ran while one was open for 1% of the time, Pallas kernels for 17%

profile of v14, /device:TPU:0, one launch (start us, length us, event | category | flops | bytes accessed | tf_op | source)
XLA Modules:
  0.0 103.6 jit_solution(3050381717551956999)
XLA Ops:
  0.0 1.0 slice.17
  1.0 0.1 collective-permute-start
  1.7 1.4 %broadcast_select_fusion.x_ref = f32[128,2048]{1,0:T(8,128)S(1)} fusion(pred[128]{0:T(512)(128)(4,1)S(1)} %iota_compare_fusion, f32[1,128,2048]{2,1,0:T(8,128)} %param.2), kind=kLoop, calls=%fused_computation | loop fusion | flops 262144 | bytes 2097280 | tf_op jit(solution)/shard_map/jit(_where)/select_n | solution.py:298
  3.1 0.0 collective-permute-done
  3.1 0.1 slice_select_fusion.lead_ref
  3.2 0.2 pack.1
  3.4 33.2 %all_to_all.15 = f32[8,128,768]{2,1,0:T(8,128)S(1)} all-to-all(f32[8,128,768]{2,1,0:T(8,128)S(1)} %pack.1), channel_id=1, replica_groups={{0,6,8,14,96,102,104,110},{2,4,10,12,98,100,106,108},{24,30,16,22,120,1..., dimensions={0} | all-to-all | bytes 6291456 | tf_op jit(solution)/shard_map/all_to_all | solution.py:279
  36.7 2.4 %gram.1 = f32[8,128,256]{2,1,0:T(8,128)S(1)} custom-call(f32[1024,768]{1,0:T(8,128)S(1)} %bitcast.10), custom_call_target="tpu_custom_call" | custom-call | flops 1073741824 | bytes 4194304 | tf_op jit(solution)/shard_map/gram/pallas_call | solution.py:124
  39.0 15.7 %all_to_all.16 = f32[8,128,256]{2,1,0:T(8,128)S(1)} all-to-all(f32[8,128,256]{2,1,0:T(8,128)S(1)} %gram.1), channel_id=1, replica_groups={{0,2,24,26,32,34,56,58},{6,4,30,28,38,36,62,60},{8,10,16,18,40,42,48,50..., dimensions={0} | all-to-all | bytes 2097152 | tf_op jit(solution)/shard_map/all_to_all | solution.py:279
  54.7 0.1 reduce_sum.9
  54.8 0.1 broadcast_in_dim.35
  54.9 14.8 %all_to_all.17 = f32[8,128,256]{2,1,0:T(8,128)S(1)} all-to-all(f32[8,128,256]{2,1,0:T(8,128)S(1)} %broadcast_in_dim.35), channel_id=1, replica_groups={{0,2,24,26,32,34,56,58},{6,4,30,28,38,36,62,60},{8,10,16,18,40,42,48,50..., dimensions={0} | all-to-all | bytes 2097152 | tf_op jit(solution)/shard_map/all_to_all | solution.py:279
  69.7 0.1 fusion
  69.8 0.1 collective-permute-start.1
  69.9 0.1 collective-permute-start.8
  70.0 0.9 collective-permute-start.6
  70.9 2.3 %collective-permute-start.4 = (f32[512,256]{1,0:T(8,128)S(1)}, f32[512,256]{1,0:T(8,128)S(1)}, u32[]{:S(2)}, u32[]{:S(2)}) collective-permute-start(f32[512,256]{1,0:T(8,128)S(1)} %bitcast.13), channel_id=1, source_target_pairs={{0,96},{6,102},{8,104},{14,110},{96,0},{102,6},{104,8},{110,14},{2... | collective-permute-start | bytes 1572872 | tf_op jit(solution)/shard_map/ppermute | solution.py:293
  73.2 4.1 %collective-permute-start.2 = (f32[512,256]{1,0:T(8,128)S(1)}, f32[512,256]{1,0:T(8,128)S(1)}, u32[]{:S(2)}, u32[]{:S(2)}) collective-permute-start(f32[512,256]{1,0:T(8,128)S(1)} %bitcast.14), channel_id=1, source_target_pairs={{0,8},{6,14},{8,0},{14,6},{96,104},{102,110},{104,96},{110,102},{2... | collective-permute-start | bytes 1572872 | tf_op jit(solution)/shard_map/ppermute | solution.py:293
  77.3 0.0 collective-permute-done.1.other
  77.3 8.1 %first.1 = (f32[512,512]{1,0:T(8,128)S(1)}, f32[256,256]{1,0:T(8,128)S(1)}, f32[1,256]{1,0:T(1,128)S(1)}, f32[1,256]{1,0:T(1,128)S(1)}, f32[1,256]{1,0:T(1,128)S(1)}) custom-call(f32[512,256]{1,0:T(8,128)S(1)} %bitcast.17, f32[512,256]{1,0:T(8,128)S(1)} %collective-permute-done.1.other), custom_call_target="tpu_custom_call" | custom-call | flops 10000000000 | bytes 2097152 | tf_op jit(solution)/shard_map/first/pallas_call | solution.py:124
  85.4 0.0 collective-permute-done.6.refs_1_
  85.5 0.6 collective-permute-start.7
  86.1 0.7 collective-permute-done.4.refs_3_
  86.9 3.5 %collective-permute-start.5 = (f32[512,256]{1,0:T(8,128)S(1)}, f32[512,256]{1,0:T(8,128)S(1)}, u32[]{:S(2)}, u32[]{:S(2)}) collective-permute-start(f32[512,256]{1,0:T(8,128)S(1)} %broadcast_add_fusion.1), channel_id=1, source_target_pairs={{0,8},{6,14},{8,0},{14,6},{96,104},{102,110},{104,96},{110,102},{2... | collective-permute-start | bytes 1572872 | tf_op jit(solution)/shard_map/ppermute | solution.py:293
  90.4 0.0 collective-permute-done.2.refs_2_
  90.5 0.8 collective-permute-start.3
  91.3 7.1 %second.1 = (bf16[1024,256]{1,0:T(8,128)(2,1)S(1)}, bf16[512,256]{1,0:T(8,128)(2,1)S(1)}) custom-call(f32[512,512]{1,0:T(8,128)S(1)} %get-tuple-element.12.half_ref, f32[256,256]{1,0:T(8,128)S(1)} %get-tuple-element.13.left_ref), custom_call_target="tpu_custom_call" | custom-call | flops 10000000000 | bytes 2097152 | tf_op jit(solution)/shard_map/second/pallas_call | solution.py:124
  98.4 0.0 collective-permute-done.8.refs_4_
  98.5 2.8 %product.2.refs_3_ = f32[512,2048]{1,0:T(8,128)} custom-call(bf16[1024,256]{1,0:T(8,128)(2,1)S(1)} %get-tuple-element.14.head_ref, bf16[512,256]{1,0:T(8,128)(2,1)S(1)} %get-tuple-element.15.tail_ref, f32[512,256]{1,0:T(8,128)S(1)} %bitcast.15, f32[512,256]{1,0:T(8,128)S(1)} %collective-permute-done.6.refs_1_, ...), custom_call_target="tpu_custom_call" | custom-call | flops 2000000000 | bytes 5242880 | tf_op jit(solution)/shard_map/product/pallas_call | solution.py:244
  101.3 0.0 collective-permute-done.7.refs_2_
  101.3 0.0 collective-permute-done.5.refs_1_
  101.3 0.0 collective-permute-done.3.refs_0_
  101.3 2.1 %product.3 = f32[512,2048]{1,0:T(8,128)} custom-call(bf16[1024,256]{1,0:T(8,128)(2,1)S(1)} %get-tuple-element.14.head_ref, bf16[512,256]{1,0:T(8,128)(2,1)S(1)} %get-tuple-element.15.tail_ref, f32[512,256]{1,0:T(8,128)S(1)} %collective-permute-done.3.refs_0_, f32[512,256]{1,0:T(8,128)S(1)} %collective-permute-done.5.refs_1_, ...), custom_call_target="tpu_custom_call", output_to_operand_aliasing={{}: (5, {})} | custom-call | flops 1200000000 | bytes 3145728 | tf_op jit(solution)/shard_map/product/pallas_call | solution.py:244
  (4 shorter events, 0.1 us)
Async XLA Ops:
  1.0 2.1 %collective-permute-start = (f32[128,512]{1,0:T(8,128)S(1)}, f32[128,512]{1,0:T(8,128)S(1)}, u32[]{:S(2)}, u32[]{:S(2)}) collective-permute-start(f32[128,512]{1,0:T(8,128)S(1)} %slice.17), channel_id=1, source_target_pairs={{0,1},{1,0},{2,3},{3,2},{4,5},{5,4},{6,7},{7,6},{8,9},{9,8},{10,11... | collective-permute-start | bytes 786440 | tf_op jit(solution)/shard_map/ppermute | solution.py:287
  69.8 7.5 %collective-permute-start.1 = (f32[512,256]{1,0:T(8,128)S(1)}, f32[512,256]{1,0:T(8,128)S(1)}, u32[]{:S(2)}, u32[]{:S(2)}) collective-permute-start(f32[512,256]{1,0:T(8,128)S(1)} %bitcast.16), channel_id=1, source_target_pairs={{0,1},{1,0},{2,3},{3,2},{4,5},{5,4},{6,7},{7,6},{8,9},{9,8},{10,11... | collective-permute-start | bytes 1572872 | tf_op jit(solution)/shard_map/ppermute | solution.py:287
  69.9 28.6 %collective-permute-start.8 = (f32[512,256]{1,0:T(8,128)S(1)}, f32[512,256]{1,0:T(8,128)S(1)}, u32[]{:S(2)}, u32[]{:S(2)}) collective-permute-start(f32[512,256]{1,0:T(8,128)S(1)} %bitcast.11), channel_id=1, source_target_pairs={{0,110},{6,104},{8,102},{14,96},{96,14},{102,8},{104,6},{110,0},{2... | collective-permute-start | bytes 1572872 | tf_op jit(solution)/shard_map/ppermute | solution.py:293
  70.0 15.5 %collective-permute-start.6 = (f32[512,256]{1,0:T(8,128)S(1)}, f32[512,256]{1,0:T(8,128)S(1)}, u32[]{:S(2)}, u32[]{:S(2)}) collective-permute-start(f32[512,256]{1,0:T(8,128)S(1)} %bitcast.12), channel_id=1, source_target_pairs={{0,6},{6,0},{8,14},{14,8},{96,102},{102,96},{104,110},{110,104},{2... | collective-permute-start | bytes 1572872 | tf_op jit(solution)/shard_map/ppermute | solution.py:293
  70.9 16.0 %collective-permute-start.4 = (f32[512,256]{1,0:T(8,128)S(1)}, f32[512,256]{1,0:T(8,128)S(1)}, u32[]{:S(2)}, u32[]{:S(2)}) collective-permute-start(f32[512,256]{1,0:T(8,128)S(1)} %bitcast.13), channel_id=1, source_target_pairs={{0,96},{6,102},{8,104},{14,110},{96,0},{102,6},{104,8},{110,14},{2... | collective-permute-start | bytes 1572872 | tf_op jit(solution)/shard_map/ppermute | solution.py:293
  73.2 17.2 %collective-permute-start.2 = (f32[512,256]{1,0:T(8,128)S(1)}, f32[512,256]{1,0:T(8,128)S(1)}, u32[]{:S(2)}, u32[]{:S(2)}) collective-permute-start(f32[512,256]{1,0:T(8,128)S(1)} %bitcast.14), channel_id=1, source_target_pairs={{0,8},{6,14},{8,0},{14,6},{96,104},{102,110},{104,96},{110,102},{2... | collective-permute-start | bytes 1572872 | tf_op jit(solution)/shard_map/ppermute | solution.py:293
  85.5 15.8 %collective-permute-start.7 = (f32[512,256]{1,0:T(8,128)S(1)}, f32[512,256]{1,0:T(8,128)S(1)}, u32[]{:S(2)}, u32[]{:S(2)}) collective-permute-start(f32[512,256]{1,0:T(8,128)S(1)} %broadcast_add_fusion), channel_id=1, source_target_pairs={{0,96},{6,102},{8,104},{14,110},{96,0},{102,6},{104,8},{110,14},{2... | collective-permute-start | bytes 1572872 | tf_op jit(solution)/shard_map/ppermute | solution.py:293
  86.9 14.4 %collective-permute-start.5 = (f32[512,256]{1,0:T(8,128)S(1)}, f32[512,256]{1,0:T(8,128)S(1)}, u32[]{:S(2)}, u32[]{:S(2)}) collective-permute-start(f32[512,256]{1,0:T(8,128)S(1)} %broadcast_add_fusion.1), channel_id=1, source_target_pairs={{0,8},{6,14},{8,0},{14,6},{96,104},{102,110},{104,96},{110,102},{2... | collective-permute-start | bytes 1572872 | tf_op jit(solution)/shard_map/ppermute | solution.py:293
  90.5 10.8 %collective-permute-start.3 = (f32[512,256]{1,0:T(8,128)S(1)}, f32[512,256]{1,0:T(8,128)S(1)}, u32[]{:S(2)}, u32[]{:S(2)}) collective-permute-start(f32[512,256]{1,0:T(8,128)S(1)} %broadcast_add_fusion.2), channel_id=1, source_target_pairs={{0,6},{6,0},{8,14},{14,8},{96,102},{102,96},{104,110},{110,104},{2... | collective-permute-start | bytes 1572872 | tf_op jit(solution)/shard_map/ppermute | solution.py:293

commit v15 on v11

--- a/solution.py
+++ b/solution.py
@@ -40,7 +40,8 @@
         X=V[k]
         u[8*k:8*k+8,:]=X
         R=[u[pl.ds(8*k+j,8,stride=0),:] for j in range(8)]
-        S=[[lb(R[i],8*k+j) if i>=j else None for j in range(8)] for i in range(8)]
+        for j in range(8): u[256+64*k+8*j:264+64*k+8*j,:]=lb(X,8*k+j)
+        S=[[u[pl.ds(256+64*k+8*j+i,8,stride=0),:] if i>=j else None for j in range(8)] for i in range(8)]
         u[128+8*k:136+8*k,:]=E[k]
         F=[u[pl.ds(128+8*k+j,8,stride=0),:] for j in range(8)]
         l=[[None]*8 for _ in range(8)]
@@ -73,9 +74,8 @@
                     S[i][m]=near[i,m] if (i,m) in near else S[i][m]-l[i][j]*p[m]-l[i][j+1]*r[m]
             for t in (j,j+1):
                 if k<15:
-                    cc=C[t]*inv[t]
-                    v1=v1-cc*R[t]
-                    e1=e1-cc*F[t]
+                    v1=v1-C[t]*(R[t]*inv[t])
+                    e1=e1-C[t]*(F[t]*inv[t])
                     for i in range(t+1,8):
                         C[i]=C[i]-l[i][t]*C[t]
                 for i in range(t+1,8):
@@ -305,9 +305,9 @@
     near = [swap(rest, mask) for mask in (1, 2, 4)]
     far = swap(rest, 7)
     out = (vmem(LEAD, LEAD), vmem(256, 256), vmem(1, 256))
-    scratch = (pltpu.VMEM((LEAD, LEAD), F32), pltpu.VMEM((128, 128), F32), pltpu.VMEM((272, 128), F32))
+    scratch = (pltpu.VMEM((LEAD, LEAD), F32), pltpu.VMEM((128, 128), F32), pltpu.VMEM((1288, 128), F32))
     half, left, zero = call(first_kernel, out, (square, across(square)), 10**10, 2 << 20, scratch, name="first")
-    scratch = (pltpu.VMEM((LEAD, LEAD), F32), pltpu.VMEM((256, 256), F32), pltpu.VMEM((128, 128), F32), pltpu.VMEM((272, 128), F32))
+    scratch = (pltpu.VMEM((LEAD, LEAD), F32), pltpu.VMEM((256, 256), F32), pltpu.VMEM((128, 128), F32), pltpu.VMEM((1288, 128), F32))
     out = (jax.ShapeDtypeStruct((2 * LEAD, 256), jnp.bfloat16), jax.ShapeDtypeStruct((LEAD, 256), jnp.bfloat16))
     inverse = call(second_kernel, out, (half, left), 10**10, 2 << 20, scratch, name="second")
     x, y, z = (block + zero for block in near)

time: 104 us -> 104 us (level)
  Pallas kernels: 24.5 us -> 22.7 us
    pallas_call x4, Pallas kernels: 19.5 us -> 17.8 us  [call(): pl.pallas_call(kernel, out_shape=out, in_specs=[VMEM] * len(args), out_sp...]
  transfers between devices with their start and end apart: 9 -> 9, of which waited for: 1 -> 1; matrix products, arithmetic and copies ran while one was open for 1% -> 1% of each run, Pallas kernels for 19% -> 17%
where the time goes in v15:
time: 104 us; the launch traced here: 103 us
  blocking collectives  63.7 us (61%)
  Pallas kernels  22.7 us (22%)
  starting transfers between devices  11.5 us (11%)
  other arithmetic  1.67 us (2%)
  waiting for transfers between devices  1.47 us (1%)
  local copies, waits for them, and re-layouts  1.14 us (1%)
    all_to_all x3, blocking collectives, exchange(): return lax.all_to_all(x, ('row', 'col'), 0, 0, axis_index_groups=groups)  63.7 us
    pallas_call x4, Pallas kernels, call(): pl.pallas_call(kernel, out_shape=out, in_specs=[VMEM] * len(args), out_sp...  17.8 us
    ppermute x7, starting transfers between devices, swap(): return lax.ppermute(x, ('row', 'col'), flip(mask))  11.4 us
    pallas_call x2, Pallas kernels, product(): pl.pallas_call(functools.partial(product_kernel, masks), out_shape=vmem(L...  4.93 us
  transfers between devices with their start and end apart: 9, of which 1 were waited for; matrix products, arithmetic and copies ran while one was open for 1% of the time, Pallas kernels for 17%

profile of v15, /device:TPU:0, one launch (start us, length us, event | category | flops | bytes accessed | tf_op | source)
XLA Modules:
  0.0 103.3 jit_solution(6438296545290835588)
XLA Ops:
  0.0 1.0 slice.17
  1.0 0.1 collective-permute-start
  1.7 1.4 %broadcast_select_fusion.x_ref = f32[128,2048]{1,0:T(8,128)S(1)} fusion(pred[128]{0:T(512)(128)(4,1)S(1)} %iota_compare_fusion, f32[1,128,2048]{2,1,0:T(8,128)} %param.2), kind=kLoop, calls=%fused_computation | loop fusion | flops 262144 | bytes 2097280 | tf_op jit(solution)/shard_map/jit(_where)/select_n | solution.py:296
  3.1 0.0 collective-permute-done
  3.1 0.1 slice_select_fusion.lead_ref
  3.2 0.2 pack.1
  3.4 33.2 %all_to_all.15 = f32[8,128,768]{2,1,0:T(8,128)S(1)} all-to-all(f32[8,128,768]{2,1,0:T(8,128)S(1)} %pack.1), channel_id=1, replica_groups={{0,6,8,14,96,102,104,110},{2,4,10,12,98,100,106,108},{24,30,16,22,120,1..., dimensions={0} | all-to-all | bytes 6291456 | tf_op jit(solution)/shard_map/all_to_all | solution.py:277
  36.7 2.4 %gram.1 = f32[8,128,256]{2,1,0:T(8,128)S(1)} custom-call(f32[1024,768]{1,0:T(8,128)S(1)} %bitcast.8), custom_call_target="tpu_custom_call" | custom-call | flops 1073741824 | bytes 4194304 | tf_op jit(solution)/shard_map/gram/pallas_call | solution.py:123
  39.0 15.7 %all_to_all.16 = f32[8,128,256]{2,1,0:T(8,128)S(1)} all-to-all(f32[8,128,256]{2,1,0:T(8,128)S(1)} %gram.1), channel_id=1, replica_groups={{0,2,24,26,32,34,56,58},{6,4,30,28,38,36,62,60},{8,10,16,18,40,42,48,50..., dimensions={0} | all-to-all | bytes 2097152 | tf_op jit(solution)/shard_map/all_to_all | solution.py:277
  54.7 0.1 reduce_sum.9
  54.8 0.1 broadcast_in_dim.35
  54.9 14.8 %all_to_all.17 = f32[8,128,256]{2,1,0:T(8,128)S(1)} all-to-all(f32[8,128,256]{2,1,0:T(8,128)S(1)} %broadcast_in_dim.35), channel_id=1, replica_groups={{0,2,24,26,32,34,56,58},{6,4,30,28,38,36,62,60},{8,10,16,18,40,42,48,50..., dimensions={0} | all-to-all | bytes 2097152 | tf_op jit(solution)/shard_map/all_to_all | solution.py:277
  69.7 0.1 fusion
  69.8 0.1 collective-permute-start.1
  69.9 0.1 collective-permute-start.8
  70.0 0.9 collective-permute-start.6
  70.9 2.3 %collective-permute-start.4 = (f32[512,256]{1,0:T(8,128)S(1)}, f32[512,256]{1,0:T(8,128)S(1)}, u32[]{:S(2)}, u32[]{:S(2)}) collective-permute-start(f32[512,256]{1,0:T(8,128)S(1)} %bitcast.11), channel_id=1, source_target_pairs={{0,96},{6,102},{8,104},{14,110},{96,0},{102,6},{104,8},{110,14},{2... | collective-permute-start | bytes 1572872 | tf_op jit(solution)/shard_map/ppermute | solution.py:291
  73.2 4.1 %collective-permute-start.2 = (f32[512,256]{1,0:T(8,128)S(1)}, f32[512,256]{1,0:T(8,128)S(1)}, u32[]{:S(2)}, u32[]{:S(2)}) collective-permute-start(f32[512,256]{1,0:T(8,128)S(1)} %bitcast.12), channel_id=1, source_target_pairs={{0,8},{6,14},{8,0},{14,6},{96,104},{102,110},{104,96},{110,102},{2... | collective-permute-start | bytes 1572872 | tf_op jit(solution)/shard_map/ppermute | solution.py:291
  77.3 0.0 collective-permute-done.1.other
  77.3 8.1 %first.1 = (f32[512,512]{1,0:T(8,128)S(1)}, f32[256,256]{1,0:T(8,128)S(1)}, f32[1,256]{1,0:T(1,128)S(1)}) custom-call(f32[512,256]{1,0:T(8,128)S(1)} %bitcast.15, f32[512,256]{1,0:T(8,128)S(1)} %collective-permute-done.1.other), custom_call_target="tpu_custom_call" | custom-call | flops 10000000000 | bytes 2097152 | tf_op jit(solution)/shard_map/first/pallas_call | solution.py:123
  85.4 0.0 collective-permute-done.6.refs_1_
  85.4 1.4 %collective-permute-done.4.refs_3_ = f32[512,256]{1,0:T(8,128)S(1)} collective-permute-done((f32[512,256]{1,0:T(8,128)S(1)}, f32[512,256]{1,0:T(8,128)S(1)}, u32[]{:S(2)}, u32[]{:S(2)}) %collective-permute-start.4) | collective-permute-done | bytes 524320 | tf_op jit(solution)/shard_map/ppermute | solution.py:291
  86.9 0.0 collective-permute-done.2.refs_2_
  86.9 0.1 broadcast_add_fusion
  87.0 2.8 %collective-permute-start.7 = (f32[512,256]{1,0:T(8,128)S(1)}, f32[512,256]{1,0:T(8,128)S(1)}, u32[]{:S(2)}, u32[]{:S(2)}) collective-permute-start(f32[512,256]{1,0:T(8,128)S(1)} %get-tuple-element.17), channel_id=1, source_target_pairs={{0,96},{6,102},{8,104},{14,110},{96,0},{102,6},{104,8},{110,14},{2... | collective-permute-start | bytes 1572872 | tf_op jit(solution)/shard_map/ppermute | solution.py:291
  89.8 0.6 collective-permute-start.5
  90.4 0.6 collective-permute-start.3
  91.0 7.1 %second.1 = (bf16[1024,256]{1,0:T(8,128)(2,1)S(1)}, bf16[512,256]{1,0:T(8,128)(2,1)S(1)}) custom-call(f32[512,512]{1,0:T(8,128)S(1)} %get-tuple-element.10.half_ref, f32[256,256]{1,0:T(8,128)S(1)} %get-tuple-element.11.left_ref), custom_call_target="tpu_custom_call" | custom-call | flops 10000000000 | bytes 2097152 | tf_op jit(solution)/shard_map/second/pallas_call | solution.py:123
  98.1 0.0 collective-permute-done.8.refs_4_
  98.1 2.8 %product.2.refs_3_ = f32[512,2048]{1,0:T(8,128)} custom-call(bf16[1024,256]{1,0:T(8,128)(2,1)S(1)} %get-tuple-element.12.head_ref, bf16[512,256]{1,0:T(8,128)(2,1)S(1)} %get-tuple-element.13.tail_ref, f32[512,256]{1,0:T(8,128)S(1)} %bitcast.13, f32[512,256]{1,0:T(8,128)S(1)} %collective-permute-done.6.refs_1_, ...), custom_call_target="tpu_custom_call" | custom-call | flops 2000000000 | bytes 5242880 | tf_op jit(solution)/shard_map/product/pallas_call | solution.py:242
  101.0 0.0 collective-permute-done.7.refs_2_
  101.0 0.0 collective-permute-done.5.refs_1_
  101.0 0.0 collective-permute-done.3.refs_0_
  101.0 2.1 %product.3 = f32[512,2048]{1,0:T(8,128)} custom-call(bf16[1024,256]{1,0:T(8,128)(2,1)S(1)} %get-tuple-element.12.head_ref, bf16[512,256]{1,0:T(8,128)(2,1)S(1)} %get-tuple-element.13.tail_ref, f32[512,256]{1,0:T(8,128)S(1)} %collective-permute-done.3.refs_0_, f32[512,256]{1,0:T(8,128)S(1)} %collective-permute-done.5.refs_1_, ...), custom_call_target="tpu_custom_call", output_to_operand_aliasing={{}: (5, {})} | custom-call | flops 1200000000 | bytes 3145728 | tf_op jit(solution)/shard_map/product/pallas_call | solution.py:242
  (1 shorter events, 0.0 us)
Async XLA Ops:
  1.0 2.1 %collective-permute-start = (f32[128,512]{1,0:T(8,128)S(1)}, f32[128,512]{1,0:T(8,128)S(1)}, u32[]{:S(2)}, u32[]{:S(2)}) collective-permute-start(f32[128,512]{1,0:T(8,128)S(1)} %slice.17), channel_id=1, source_target_pairs={{0,1},{1,0},{2,3},{3,2},{4,5},{5,4},{6,7},{7,6},{8,9},{9,8},{10,11... | collective-permute-start | bytes 786440 | tf_op jit(solution)/shard_map/ppermute | solution.py:285
  69.8 7.5 %collective-permute-start.1 = (f32[512,256]{1,0:T(8,128)S(1)}, f32[512,256]{1,0:T(8,128)S(1)}, u32[]{:S(2)}, u32[]{:S(2)}) collective-permute-start(f32[512,256]{1,0:T(8,128)S(1)} %bitcast.14), channel_id=1, source_target_pairs={{0,1},{1,0},{2,3},{3,2},{4,5},{5,4},{6,7},{7,6},{8,9},{9,8},{10,11... | collective-permute-start | bytes 1572872 | tf_op jit(solution)/shard_map/ppermute | solution.py:285
  69.9 28.3 %collective-permute-start.8 = (f32[512,256]{1,0:T(8,128)S(1)}, f32[512,256]{1,0:T(8,128)S(1)}, u32[]{:S(2)}, u32[]{:S(2)}) collective-permute-start(f32[512,256]{1,0:T(8,128)S(1)} %bitcast.9), channel_id=1, source_target_pairs={{0,110},{6,104},{8,102},{14,96},{96,14},{102,8},{104,6},{110,0},{2... | collective-permute-start | bytes 1572872 | tf_op jit(solution)/shard_map/ppermute | solution.py:291
  70.0 15.5 %collective-permute-start.6 = (f32[512,256]{1,0:T(8,128)S(1)}, f32[512,256]{1,0:T(8,128)S(1)}, u32[]{:S(2)}, u32[]{:S(2)}) collective-permute-start(f32[512,256]{1,0:T(8,128)S(1)} %bitcast.10), channel_id=1, source_target_pairs={{0,6},{6,0},{8,14},{14,8},{96,102},{102,96},{104,110},{110,104},{2... | collective-permute-start | bytes 1572872 | tf_op jit(solution)/shard_map/ppermute | solution.py:291
  70.9 16.0 %collective-permute-start.4 = (f32[512,256]{1,0:T(8,128)S(1)}, f32[512,256]{1,0:T(8,128)S(1)}, u32[]{:S(2)}, u32[]{:S(2)}) collective-permute-start(f32[512,256]{1,0:T(8,128)S(1)} %bitcast.11), channel_id=1, source_target_pairs={{0,96},{6,102},{8,104},{14,110},{96,0},{102,6},{104,8},{110,14},{2... | collective-permute-start | bytes 1572872 | tf_op jit(solution)/shard_map/ppermute | solution.py:291
  73.2 13.7 %collective-permute-start.2 = (f32[512,256]{1,0:T(8,128)S(1)}, f32[512,256]{1,0:T(8,128)S(1)}, u32[]{:S(2)}, u32[]{:S(2)}) collective-permute-start(f32[512,256]{1,0:T(8,128)S(1)} %bitcast.12), channel_id=1, source_target_pairs={{0,8},{6,14},{8,0},{14,6},{96,104},{102,110},{104,96},{110,102},{2... | collective-permute-start | bytes 1572872 | tf_op jit(solution)/shard_map/ppermute | solution.py:291
  87.0 13.9 %collective-permute-start.7 = (f32[512,256]{1,0:T(8,128)S(1)}, f32[512,256]{1,0:T(8,128)S(1)}, u32[]{:S(2)}, u32[]{:S(2)}) collective-permute-start(f32[512,256]{1,0:T(8,128)S(1)} %get-tuple-element.17), channel_id=1, source_target_pairs={{0,96},{6,102},{8,104},{14,110},{96,0},{102,6},{104,8},{110,14},{2... | collective-permute-start | bytes 1572872 | tf_op jit(solution)/shard_map/ppermute | solution.py:291
  89.8 11.2 %collective-permute-start.5 = (f32[512,256]{1,0:T(8,128)S(1)}, f32[512,256]{1,0:T(8,128)S(1)}, u32[]{:S(2)}, u32[]{:S(2)}) collective-permute-start(f32[512,256]{1,0:T(8,128)S(1)} %get-tuple-element.18), channel_id=1, source_target_pairs={{0,8},{6,14},{8,0},{14,6},{96,104},{102,110},{104,96},{110,102},{2... | collective-permute-start | bytes 1572872 | tf_op jit(solution)/shard_map/ppermute | solution.py:291
  90.4 10.6 %collective-permute-start.3 = (f32[512,256]{1,0:T(8,128)S(1)}, f32[512,256]{1,0:T(8,128)S(1)}, u32[]{:S(2)}, u32[]{:S(2)}) collective-permute-start(f32[512,256]{1,0:T(8,128)S(1)} %get-tuple-element.19), channel_id=1, source_target_pairs={{0,6},{6,0},{8,14},{14,8},{96,102},{102,96},{104,110},{110,104},{2... | collective-permute-start | bytes 1572872 | tf_op jit(solution)/shard_map/ppermute | solution.py:291
